TPU v7x, 512 devices: a whole 4x8x8 slice. The times are simulated.
512 devices in a mesh: img: 16 (over z_lo, x, core), txt: 32 (over y, z_hi).
Axes of the slice: x: 4, y: 8, z: 8 (z_hi: 4, z_lo: 2; z = z_hi * 2 + z_lo), core: 2. Of those that a mesh axis runs over, the one named last changes fastest.
Arguments:
- image_emb: bfloat16 [16384, 1152], P(('txt', 'img')), may hold values from -6 to 6
- text_emb: bfloat16 [16384, 1152], P(('img', 'txt')), may hold values from -6 to 6
- logit_scale: float32 [1], replicated, may hold values from 10 to 40
- logit_bias: float32 [1], replicated, may hold values from -6 to -3
Outputs:
- grad_image: float32 [16384, 1152], P(('txt', 'img'))
- grad_text: float32 [16384, 1152], P(('img', 'txt'))
All inputs are finite; a program needn't handle non-finite values.
Results may differ from a plain program's by a relative error of at most 0.007.
Values may be sent and summed in bfloat16 or wider, within the bound.
No kernel may reach another device: no remote copies, remote signals or barrier semaphores. Data moves between devices by JAX's collectives and lax.ppermute only.
A program may use at most 64 MiB of HBM per device.

v0:
```python
import jax
import jax.numpy as jnp
from jax import lax
from jax.sharding import PartitionSpec as P

EPS = 1e-06


def from_behind(block, axis, distance):
    devices = range(lax.axis_size(axis))
    route = [((i - distance) % len(devices), i) for i in devices]
    return lax.ppermute(block, axis, route)


def unit_rows(embedded):
    values = embedded.astype(jnp.float32)
    inverse = lax.rsqrt(jnp.sum(values * values, axis=1, keepdims=True) + EPS)
    return (values * inverse, inverse)


def project_back(grad, unit, inverse):
    inner = jnp.sum(unit * grad, axis=1, keepdims=True)
    return (grad - unit * inner) * inverse


def score_block(stretch, text_ids, gathered, image_ids, scale, bias):
    scores = (
        scale
        * lax.dot_general(
            stretch, gathered, (((1,), (1,)), ((), ())), preferred_element_type=jnp.float32
        )
        + bias
    )
    match = (text_ids[:, None] == image_ids[None, :]).astype(jnp.float32)
    weights = (jax.nn.sigmoid(scores) - match).astype(jnp.bfloat16)
    partial_grad = scale * jnp.dot(weights, gathered, preferred_element_type=jnp.float32)
    return (weights, partial_grad)


def contract_rows(weight_store, text_store):
    return lax.dot_general(
        weight_store, text_store, (((0,), (0,)), ((), ())), preferred_element_type=jnp.float32
    )


def per_device(image_emb, text_emb, logit_scale, logit_bias):
    scale = logit_scale[0]
    bias = logit_bias[0]
    n_img = lax.axis_size("img")
    n_txt = lax.axis_size("txt")
    rows = image_emb.shape[0]
    width = image_emb.shape[1]
    img_unit, img_inv = unit_rows(image_emb)
    txt_unit, txt_inv = unit_rows(text_emb)
    txt_half = txt_unit.astype(jnp.bfloat16)
    gathered = lax.all_gather(img_unit.astype(jnp.bfloat16), "img", axis=0, tiled=True)
    group_rows = n_img * rows
    image_ids = lax.axis_index("txt") * group_rows + lax.iota(jnp.int32, group_rows)
    text_base = lax.axis_index("img") * (n_txt * rows)
    position = lax.axis_index("txt")

    def advance(step, carry):
        stretch, riding, weight_store, text_store = carry
        anchor = (position - step) % n_txt
        text_ids = text_base + anchor * rows + lax.iota(jnp.int32, rows)
        weights, partial_grad = score_block(stretch, text_ids, gathered, image_ids, scale, bias)
        riding = riding + partial_grad
        weight_store = lax.dynamic_update_slice_in_dim(weight_store, weights, step * rows, 0)
        text_store = lax.dynamic_update_slice_in_dim(text_store, stretch, step * rows, 0)
        stretch = from_behind(stretch, "txt", 1)
        riding = from_behind(riding, "txt", 1)
        return (stretch, riding, weight_store, text_store)

    start = (
        txt_half,
        jnp.zeros((rows, width), jnp.float32),
        jnp.zeros((n_txt * rows, group_rows), jnp.bfloat16),
        jnp.zeros((n_txt * rows, width), jnp.bfloat16),
    )
    stretch, txt_grad, weight_store, text_store = lax.fori_loop(0, n_txt, advance, start)
    img_part = scale * contract_rows(weight_store, text_store)
    img_grad = lax.psum_scatter(img_part, "img", scatter_dimension=0, tiled=True)
    return (project_back(img_grad, img_unit, img_inv), project_back(txt_grad, txt_unit, txt_inv))


def solution(mesh):
    placed = (P(("txt", "img"), None), P(("img", "txt"), None), P(), P())
    return jax.shard_map(
        per_device,
        mesh=mesh,
        in_specs=placed,
        out_specs=(P(("txt", "img"), None), P(("img", "txt"), None)),
        check_vma=False,
    )
```

profile of v0, /device:TPU:1, one launch (start us, length us, event | category | flops | bytes accessed | tf_op | source)
XLA Modules:
  0.0 698.1 jit_solution(13189665950754041088)
XLA Ops:
  12.6 42.2 %all-gather.2.cloned.1.call-done = bf16[512,1152]{1,0:T(8,128)(2,1)} async-done(((bf16[32,1152]{1,0:T(8,128)(2,1)}), bf16[512,1152]{1,0:T(8,128)(2,1)}) %all-gather.2.cloned.1.call-update) | async-done | bytes 1179664 | tf_op jit(solution)/shard_map/all_gather | solution.py:56
  56.4 531.8 %while.22 = (s32[]{:T(128)}, bf16[32,1152]{1,0:T(8,128)(2,1)S(1)}, f32[32,1152]{1,0:T(8,128)S(1)}, bf16[1024,512]{1,0:T(8,128)(2,1)S(1)}, bf16[1024,1152]{1,0:T(...) while((s32[]{:T(128)}, bf16[32,1152]{1,0:T(8,128)(2,1)S(1)}, ...), condition=%wide.region_3.4_spmd.clone, body=%wide.region_2.3_spmd.clone.sunk | while | flops 75719216 | bytes 4011072 | solution.py:80
  56.4 4.4 collective-permute-start
  63.6 5.1 collective-permute-start.1
  69.4 7.4 %collective-permute-done.1 = f32[32,1152]{1,0:T(8,128)S(1)} collective-permute-done((f32[32,1152]{1,0:T(8,128)S(1)}, f32[32,1152]{1,0:T(8,128)S(1)}, u32[]{:S(2)}, u32[]{:S(2)}) %collective-permute-start.1) | collective-permute-done | bytes 147488 | tf_op jit(solution)/shard_map/while/body/eval_jaxpr/ppermute | solution.py:12
  81.5 2.1 collective-permute-start.1
  86.1 7.0 collective-permute-done.1
  100.4 2.7 collective-permute-done
  103.1 7.4 %collective-permute-done.1 = f32[32,1152]{1,0:T(8,128)S(1)} collective-permute-done((f32[32,1152]{1,0:T(8,128)S(1)}, f32[32,1152]{1,0:T(8,128)S(1)}, u32[]{:S(2)}, u32[]{:S(2)}) %collective-permute-start.1) | collective-permute-done | bytes 147488 | tf_op jit(solution)/shard_map/while/body/eval_jaxpr/ppermute | solution.py:12
  119.8 7.8 %collective-permute-done.1 = f32[32,1152]{1,0:T(8,128)S(1)} collective-permute-done((f32[32,1152]{1,0:T(8,128)S(1)}, f32[32,1152]{1,0:T(8,128)S(1)}, u32[]{:S(2)}, u32[]{:S(2)}) %collective-permute-start.1) | collective-permute-done | bytes 147488 | tf_op jit(solution)/shard_map/while/body/eval_jaxpr/ppermute | solution.py:12
  136.9 7.7 %collective-permute-done.1 = f32[32,1152]{1,0:T(8,128)S(1)} collective-permute-done((f32[32,1152]{1,0:T(8,128)S(1)}, f32[32,1152]{1,0:T(8,128)S(1)}, u32[]{:S(2)}, u32[]{:S(2)}) %collective-permute-start.1) | collective-permute-done | bytes 147488 | tf_op jit(solution)/shard_map/while/body/eval_jaxpr/ppermute | solution.py:12
  151.9 2.0 collective-permute-done
  153.9 7.5 %collective-permute-done.1 = f32[32,1152]{1,0:T(8,128)S(1)} collective-permute-done((f32[32,1152]{1,0:T(8,128)S(1)}, f32[32,1152]{1,0:T(8,128)S(1)}, u32[]{:S(2)}, u32[]{:S(2)}) %collective-permute-start.1) | collective-permute-done | bytes 147488 | tf_op jit(solution)/shard_map/while/body/eval_jaxpr/ppermute | solution.py:12
  168.7 2.8 collective-permute-done
  171.5 6.3 collective-permute-done.1
  185.1 2.0 collective-permute-done
  187.1 7.1 %collective-permute-done.1 = f32[32,1152]{1,0:T(8,128)S(1)} collective-permute-done((f32[32,1152]{1,0:T(8,128)S(1)}, f32[32,1152]{1,0:T(8,128)S(1)}, u32[]{:S(2)}, u32[]{:S(2)}) %collective-permute-start.1) | collective-permute-done | bytes 147488 | tf_op jit(solution)/shard_map/while/body/eval_jaxpr/ppermute | solution.py:12
  201.5 2.7 collective-permute-done
  204.2 6.4 collective-permute-done.1
  219.8 6.6 collective-permute-done.1
  233.7 2.3 collective-permute-done
  236.1 5.6 collective-permute-done.1
  249.0 2.6 collective-permute-done
  251.6 5.0 collective-permute-done.1
  263.9 5.0 collective-permute-done
  268.9 3.0 collective-permute-done.1
  272.0 2.6 collective-permute-start
  281.4 6.8 collective-permute-done.1
  295.5 2.0 collective-permute-done
  297.5 7.8 %collective-permute-done.1 = f32[32,1152]{1,0:T(8,128)S(1)} collective-permute-done((f32[32,1152]{1,0:T(8,128)S(1)}, f32[32,1152]{1,0:T(8,128)S(1)}, u32[]{:S(2)}, u32[]{:S(2)}) %collective-permute-start.1) | collective-permute-done | bytes 147488 | tf_op jit(solution)/shard_map/while/body/eval_jaxpr/ppermute | solution.py:12
  314.5 5.7 collective-permute-done.1
  329.6 7.9 %collective-permute-done.1 = f32[32,1152]{1,0:T(8,128)S(1)} collective-permute-done((f32[32,1152]{1,0:T(8,128)S(1)}, f32[32,1152]{1,0:T(8,128)S(1)}, u32[]{:S(2)}, u32[]{:S(2)}) %collective-permute-start.1) | collective-permute-done | bytes 147488 | tf_op jit(solution)/shard_map/while/body/eval_jaxpr/ppermute | solution.py:12
  346.8 6.0 collective-permute-done.1
  362.2 5.5 collective-permute-done.1
  375.0 3.5 collective-permute-done
  378.5 4.1 collective-permute-done.1
  387.3 4.9 collective-permute-start.1
  392.8 5.6 collective-permute-done.1
  398.4 3.0 collective-permute-start
  404.2 4.1 collective-permute-start.1
  409.0 6.7 collective-permute-done.1
  420.4 2.3 collective-permute-start.1
  423.3 2.6 collective-permute-done
  425.9 7.9 %collective-permute-done.1 = f32[32,1152]{1,0:T(8,128)S(1)} collective-permute-done((f32[32,1152]{1,0:T(8,128)S(1)}, f32[32,1152]{1,0:T(8,128)S(1)}, u32[]{:S(2)}, u32[]{:S(2)}) %collective-permute-start.1) | collective-permute-done | bytes 147488 | tf_op jit(solution)/shard_map/while/body/eval_jaxpr/ppermute | solution.py:12
  441.1 2.8 collective-permute-done
  443.9 6.8 collective-permute-done.1
  458.0 2.5 collective-permute-done
  460.6 6.5 collective-permute-done.1
  474.3 2.7 collective-permute-done
  477.0 6.8 collective-permute-done.1
  491.1 2.6 collective-permute-done
  493.7 6.9 collective-permute-done.1
  507.8 2.2 collective-permute-done
  510.1 7.3 %collective-permute-done.1 = f32[32,1152]{1,0:T(8,128)S(1)} collective-permute-done((f32[32,1152]{1,0:T(8,128)S(1)}, f32[32,1152]{1,0:T(8,128)S(1)}, u32[]{:S(2)}, u32[]{:S(2)}) %collective-permute-start.1) | collective-permute-done | bytes 147488 | tf_op jit(solution)/shard_map/while/body/eval_jaxpr/ppermute | solution.py:12
  524.7 2.2 collective-permute-done
  526.8 7.3 %collective-permute-done.1 = f32[32,1152]{1,0:T(8,128)S(1)} collective-permute-done((f32[32,1152]{1,0:T(8,128)S(1)}, f32[32,1152]{1,0:T(8,128)S(1)}, u32[]{:S(2)}, u32[]{:S(2)}) %collective-permute-start.1) | collective-permute-done | bytes 147488 | tf_op jit(solution)/shard_map/while/body/eval_jaxpr/ppermute | solution.py:12
  541.5 2.2 collective-permute-done
  543.7 8.9 %collective-permute-done.1 = f32[32,1152]{1,0:T(8,128)S(1)} collective-permute-done((f32[32,1152]{1,0:T(8,128)S(1)}, f32[32,1152]{1,0:T(8,128)S(1)}, u32[]{:S(2)}, u32[]{:S(2)}) %collective-permute-start.1) | collective-permute-done | bytes 147488 | tf_op jit(solution)/shard_map/while/body/eval_jaxpr/ppermute | solution.py:12
  559.9 3.3 collective-permute-done
  563.2 7.8 %collective-permute-done.1 = f32[32,1152]{1,0:T(8,128)S(1)} collective-permute-done((f32[32,1152]{1,0:T(8,128)S(1)}, f32[32,1152]{1,0:T(8,128)S(1)}, u32[]{:S(2)}, u32[]{:S(2)}) %collective-permute-start.1) | collective-permute-done | bytes 147488 | tf_op jit(solution)/shard_map/while/body/eval_jaxpr/ppermute | solution.py:12
  578.3 2.6 collective-permute-done
  580.9 7.3 %collective-permute-done.1 = f32[32,1152]{1,0:T(8,128)S(1)} collective-permute-done((f32[32,1152]{1,0:T(8,128)S(1)}, f32[32,1152]{1,0:T(8,128)S(1)}, u32[]{:S(2)}, u32[]{:S(2)}) %collective-permute-start.1) | collective-permute-done | bytes 147488 | tf_op jit(solution)/shard_map/while/body/eval_jaxpr/ppermute | solution.py:12
  588.2 4.6 convolution_multiply_fusion.2
  594.7 93.8 %reduce-scatter.2.cloned.1.call-done = f32[32,1152]{1,0:T(8,128)} async-done(((f32[512,1152]{1,0:T(8,128)}), f32[32,1152]{1,0:T(8,128)}) %reduce-scatter.2.cloned.1.call-update) | async-done | bytes 147472 | tf_op jit(solution)/shard_map/reduce_scatter | solution.py:82
  (283 shorter events, 244.0 us)
Async XLA Ops:
  7.2 47.6 %all-gather.2.cloned.1.call-start = ((), (), s32[]{:S(2)}) async-start(), calls=%async_computation.1 | async-start | bytes 1253376 | tf_op jit(solution)/shard_map/all_gather | solution.py:56
  9.9 678.6 %reduce-scatter.2.cloned.1.call-start = ((), (), s32[]{:S(2)}) async-start(), calls=%async_computation.2 | async-start | bytes 2506752 | tf_op jit(solution)/shard_map/reduce_scatter | solution.py:82
  56.4 12.9 %collective-permute-start = (bf16[32,1152]{1,0:T(8,128)(2,1)S(1)}, bf16[32,1152]{1,0:T(8,128)(2,1)S(1)}, u32[]{:S(2)}, u32[]{:S(2)}) collective-permute-start(bf16[32,1152]{1,0:T(8,128)(2,1)S(1)} %copy.14), channel_id=1, source_target_pairs={{31,0},{0,1},{1,2},{2,3},{3,4},{4,5},{5,6},{6,7},{7,8},{8,9},{9,10... | collective-permute-start | bytes 221192 | tf_op jit(solution)/shard_map/while/body/eval_jaxpr/ppermute | solution.py:12
  63.6 13.2 %collective-permute-start.1 = (f32[32,1152]{1,0:T(8,128)S(1)}, f32[32,1152]{1,0:T(8,128)S(1)}, u32[]{:S(2)}, u32[]{:S(2)}) collective-permute-start(f32[32,1152]{1,0:T(8,128)S(1)} %fusion.39), channel_id=1, source_target_pairs={{31,0},{0,1},{1,2},{2,3},{3,4},{4,5},{5,6},{6,7},{7,8},{8,9},{9,10... | collective-permute-start | bytes 442376 | tf_op jit(solution)/shard_map/while/body/eval_jaxpr/ppermute | solution.py:12
  76.8 9.3 %collective-permute-start = (bf16[32,1152]{1,0:T(8,128)(2,1)S(1)}, bf16[32,1152]{1,0:T(8,128)(2,1)S(1)}, u32[]{:S(2)}, u32[]{:S(2)}) collective-permute-start(bf16[32,1152]{1,0:T(8,128)(2,1)S(1)} %copy.14), channel_id=1, source_target_pairs={{31,0},{0,1},{1,2},{2,3},{3,4},{4,5},{5,6},{6,7},{7,8},{8,9},{9,10... | collective-permute-start | bytes 221192 | tf_op jit(solution)/shard_map/while/body/eval_jaxpr/ppermute | solution.py:12
  81.5 11.6 %collective-permute-start.1 = (f32[32,1152]{1,0:T(8,128)S(1)}, f32[32,1152]{1,0:T(8,128)S(1)}, u32[]{:S(2)}, u32[]{:S(2)}) collective-permute-start(f32[32,1152]{1,0:T(8,128)S(1)} %fusion.39), channel_id=1, source_target_pairs={{31,0},{0,1},{1,2},{2,3},{3,4},{4,5},{5,6},{6,7},{7,8},{8,9},{9,10... | collective-permute-start | bytes 442376 | tf_op jit(solution)/shard_map/while/body/eval_jaxpr/ppermute | solution.py:12
  93.1 10.0 %collective-permute-start = (bf16[32,1152]{1,0:T(8,128)(2,1)S(1)}, bf16[32,1152]{1,0:T(8,128)(2,1)S(1)}, u32[]{:S(2)}, u32[]{:S(2)}) collective-permute-start(bf16[32,1152]{1,0:T(8,128)(2,1)S(1)} %copy.14), channel_id=1, source_target_pairs={{31,0},{0,1},{1,2},{2,3},{3,4},{4,5},{5,6},{6,7},{7,8},{8,9},{9,10... | collective-permute-start | bytes 221192 | tf_op jit(solution)/shard_map/while/body/eval_jaxpr/ppermute | solution.py:12
  97.8 12.6 %collective-permute-start.1 = (f32[32,1152]{1,0:T(8,128)S(1)}, f32[32,1152]{1,0:T(8,128)S(1)}, u32[]{:S(2)}, u32[]{:S(2)}) collective-permute-start(f32[32,1152]{1,0:T(8,128)S(1)} %fusion.39), channel_id=1, source_target_pairs={{31,0},{0,1},{1,2},{2,3},{3,4},{4,5},{5,6},{6,7},{7,8},{8,9},{9,10... | collective-permute-start | bytes 442376 | tf_op jit(solution)/shard_map/while/body/eval_jaxpr/ppermute | solution.py:12
  110.5 9.3 %collective-permute-start = (bf16[32,1152]{1,0:T(8,128)(2,1)S(1)}, bf16[32,1152]{1,0:T(8,128)(2,1)S(1)}, u32[]{:S(2)}, u32[]{:S(2)}) collective-permute-start(bf16[32,1152]{1,0:T(8,128)(2,1)S(1)} %copy.14), channel_id=1, source_target_pairs={{31,0},{0,1},{1,2},{2,3},{3,4},{4,5},{5,6},{6,7},{7,8},{8,9},{9,10... | collective-permute-start | bytes 221192 | tf_op jit(solution)/shard_map/while/body/eval_jaxpr/ppermute | solution.py:12
  115.2 12.4 %collective-permute-start.1 = (f32[32,1152]{1,0:T(8,128)S(1)}, f32[32,1152]{1,0:T(8,128)S(1)}, u32[]{:S(2)}, u32[]{:S(2)}) collective-permute-start(f32[32,1152]{1,0:T(8,128)S(1)} %fusion.39), channel_id=1, source_target_pairs={{31,0},{0,1},{1,2},{2,3},{3,4},{4,5},{5,6},{6,7},{7,8},{8,9},{9,10... | collective-permute-start | bytes 442376 | tf_op jit(solution)/shard_map/while/body/eval_jaxpr/ppermute | solution.py:12
  127.6 9.3 %collective-permute-start = (bf16[32,1152]{1,0:T(8,128)(2,1)S(1)}, bf16[32,1152]{1,0:T(8,128)(2,1)S(1)}, u32[]{:S(2)}, u32[]{:S(2)}) collective-permute-start(bf16[32,1152]{1,0:T(8,128)(2,1)S(1)} %copy.14), channel_id=1, source_target_pairs={{31,0},{0,1},{1,2},{2,3},{3,4},{4,5},{5,6},{6,7},{7,8},{8,9},{9,10... | collective-permute-start | bytes 221192 | tf_op jit(solution)/shard_map/while/body/eval_jaxpr/ppermute | solution.py:12
  132.3 12.3 %collective-permute-start.1 = (f32[32,1152]{1,0:T(8,128)S(1)}, f32[32,1152]{1,0:T(8,128)S(1)}, u32[]{:S(2)}, u32[]{:S(2)}) collective-permute-start(f32[32,1152]{1,0:T(8,128)S(1)} %fusion.39), channel_id=1, source_target_pairs={{31,0},{0,1},{1,2},{2,3},{3,4},{4,5},{5,6},{6,7},{7,8},{8,9},{9,10... | collective-permute-start | bytes 442376 | tf_op jit(solution)/shard_map/while/body/eval_jaxpr/ppermute | solution.py:12
  144.6 9.3 %collective-permute-start = (bf16[32,1152]{1,0:T(8,128)(2,1)S(1)}, bf16[32,1152]{1,0:T(8,128)(2,1)S(1)}, u32[]{:S(2)}, u32[]{:S(2)}) collective-permute-start(bf16[32,1152]{1,0:T(8,128)(2,1)S(1)} %copy.14), channel_id=1, source_target_pairs={{31,0},{0,1},{1,2},{2,3},{3,4},{4,5},{5,6},{6,7},{7,8},{8,9},{9,10... | collective-permute-start | bytes 221192 | tf_op jit(solution)/shard_map/while/body/eval_jaxpr/ppermute | solution.py:12
  149.3 12.1 %collective-permute-start.1 = (f32[32,1152]{1,0:T(8,128)S(1)}, f32[32,1152]{1,0:T(8,128)S(1)}, u32[]{:S(2)}, u32[]{:S(2)}) collective-permute-start(f32[32,1152]{1,0:T(8,128)S(1)} %fusion.39), channel_id=1, source_target_pairs={{31,0},{0,1},{1,2},{2,3},{3,4},{4,5},{5,6},{6,7},{7,8},{8,9},{9,10... | collective-permute-start | bytes 442376 | tf_op jit(solution)/shard_map/while/body/eval_jaxpr/ppermute | solution.py:12
  161.4 10.1 %collective-permute-start = (bf16[32,1152]{1,0:T(8,128)(2,1)S(1)}, bf16[32,1152]{1,0:T(8,128)(2,1)S(1)}, u32[]{:S(2)}, u32[]{:S(2)}) collective-permute-start(bf16[32,1152]{1,0:T(8,128)(2,1)S(1)} %copy.14), channel_id=1, source_target_pairs={{31,0},{0,1},{1,2},{2,3},{3,4},{4,5},{5,6},{6,7},{7,8},{8,9},{9,10... | collective-permute-start | bytes 221192 | tf_op jit(solution)/shard_map/while/body/eval_jaxpr/ppermute | solution.py:12
  166.2 11.7 %collective-permute-start.1 = (f32[32,1152]{1,0:T(8,128)S(1)}, f32[32,1152]{1,0:T(8,128)S(1)}, u32[]{:S(2)}, u32[]{:S(2)}) collective-permute-start(f32[32,1152]{1,0:T(8,128)S(1)} %fusion.39), channel_id=1, source_target_pairs={{31,0},{0,1},{1,2},{2,3},{3,4},{4,5},{5,6},{6,7},{7,8},{8,9},{9,10... | collective-permute-start | bytes 442376 | tf_op jit(solution)/shard_map/while/body/eval_jaxpr/ppermute | solution.py:12
  182.5 11.7 %collective-permute-start.1 = (f32[32,1152]{1,0:T(8,128)S(1)}, f32[32,1152]{1,0:T(8,128)S(1)}, u32[]{:S(2)}, u32[]{:S(2)}) collective-permute-start(f32[32,1152]{1,0:T(8,128)S(1)} %fusion.39), channel_id=1, source_target_pairs={{31,0},{0,1},{1,2},{2,3},{3,4},{4,5},{5,6},{6,7},{7,8},{8,9},{9,10... | collective-permute-start | bytes 442376 | tf_op jit(solution)/shard_map/while/body/eval_jaxpr/ppermute | solution.py:12
  194.2 9.9 %collective-permute-start = (bf16[32,1152]{1,0:T(8,128)(2,1)S(1)}, bf16[32,1152]{1,0:T(8,128)(2,1)S(1)}, u32[]{:S(2)}, u32[]{:S(2)}) collective-permute-start(bf16[32,1152]{1,0:T(8,128)(2,1)S(1)} %copy.14), channel_id=1, source_target_pairs={{31,0},{0,1},{1,2},{2,3},{3,4},{4,5},{5,6},{6,7},{7,8},{8,9},{9,10... | collective-permute-start | bytes 221192 | tf_op jit(solution)/shard_map/while/body/eval_jaxpr/ppermute | solution.py:12
  199.0 11.6 %collective-permute-start.1 = (f32[32,1152]{1,0:T(8,128)S(1)}, f32[32,1152]{1,0:T(8,128)S(1)}, u32[]{:S(2)}, u32[]{:S(2)}) collective-permute-start(f32[32,1152]{1,0:T(8,128)S(1)} %fusion.39), channel_id=1, source_target_pairs={{31,0},{0,1},{1,2},{2,3},{3,4},{4,5},{5,6},{6,7},{7,8},{8,9},{9,10... | collective-permute-start | bytes 442376 | tf_op jit(solution)/shard_map/while/body/eval_jaxpr/ppermute | solution.py:12
  210.5 9.3 %collective-permute-start = (bf16[32,1152]{1,0:T(8,128)(2,1)S(1)}, bf16[32,1152]{1,0:T(8,128)(2,1)S(1)}, u32[]{:S(2)}, u32[]{:S(2)}) collective-permute-start(bf16[32,1152]{1,0:T(8,128)(2,1)S(1)} %copy.14), channel_id=1, source_target_pairs={{31,0},{0,1},{1,2},{2,3},{3,4},{4,5},{5,6},{6,7},{7,8},{8,9},{9,10... | collective-permute-start | bytes 221192 | tf_op jit(solution)/shard_map/while/body/eval_jaxpr/ppermute | solution.py:12
  215.3 11.2 %collective-permute-start.1 = (f32[32,1152]{1,0:T(8,128)S(1)}, f32[32,1152]{1,0:T(8,128)S(1)}, u32[]{:S(2)}, u32[]{:S(2)}) collective-permute-start(f32[32,1152]{1,0:T(8,128)S(1)} %fusion.39), channel_id=1, source_target_pairs={{31,0},{0,1},{1,2},{2,3},{3,4},{4,5},{5,6},{6,7},{7,8},{8,9},{9,10... | collective-permute-start | bytes 442376 | tf_op jit(solution)/shard_map/while/body/eval_jaxpr/ppermute | solution.py:12
  226.5 9.6 %collective-permute-start = (bf16[32,1152]{1,0:T(8,128)(2,1)S(1)}, bf16[32,1152]{1,0:T(8,128)(2,1)S(1)}, u32[]{:S(2)}, u32[]{:S(2)}) collective-permute-start(bf16[32,1152]{1,0:T(8,128)(2,1)S(1)} %copy.14), channel_id=1, source_target_pairs={{31,0},{0,1},{1,2},{2,3},{3,4},{4,5},{5,6},{6,7},{7,8},{8,9},{9,10... | collective-permute-start | bytes 221192 | tf_op jit(solution)/shard_map/while/body/eval_jaxpr/ppermute | solution.py:12
  231.2 10.5 %collective-permute-start.1 = (f32[32,1152]{1,0:T(8,128)S(1)}, f32[32,1152]{1,0:T(8,128)S(1)}, u32[]{:S(2)}, u32[]{:S(2)}) collective-permute-start(f32[32,1152]{1,0:T(8,128)S(1)} %fusion.39), channel_id=1, source_target_pairs={{31,0},{0,1},{1,2},{2,3},{3,4},{4,5},{5,6},{6,7},{7,8},{8,9},{9,10... | collective-permute-start | bytes 442376 | tf_op jit(solution)/shard_map/while/body/eval_jaxpr/ppermute | solution.py:12
  241.7 9.9 %collective-permute-start = (bf16[32,1152]{1,0:T(8,128)(2,1)S(1)}, bf16[32,1152]{1,0:T(8,128)(2,1)S(1)}, u32[]{:S(2)}, u32[]{:S(2)}) collective-permute-start(bf16[32,1152]{1,0:T(8,128)(2,1)S(1)} %copy.14), channel_id=1, source_target_pairs={{31,0},{0,1},{1,2},{2,3},{3,4},{4,5},{5,6},{6,7},{7,8},{8,9},{9,10... | collective-permute-start | bytes 221192 | tf_op jit(solution)/shard_map/while/body/eval_jaxpr/ppermute | solution.py:12
  246.4 10.2 %collective-permute-start.1 = (f32[32,1152]{1,0:T(8,128)S(1)}, f32[32,1152]{1,0:T(8,128)S(1)}, u32[]{:S(2)}, u32[]{:S(2)}) collective-permute-start(f32[32,1152]{1,0:T(8,128)S(1)} %fusion.39), channel_id=1, source_target_pairs={{31,0},{0,1},{1,2},{2,3},{3,4},{4,5},{5,6},{6,7},{7,8},{8,9},{9,10... | collective-permute-start | bytes 442376 | tf_op jit(solution)/shard_map/while/body/eval_jaxpr/ppermute | solution.py:12
  256.6 12.3 %collective-permute-start = (bf16[32,1152]{1,0:T(8,128)(2,1)S(1)}, bf16[32,1152]{1,0:T(8,128)(2,1)S(1)}, u32[]{:S(2)}, u32[]{:S(2)}) collective-permute-start(bf16[32,1152]{1,0:T(8,128)(2,1)S(1)} %copy.14), channel_id=1, source_target_pairs={{31,0},{0,1},{1,2},{2,3},{3,4},{4,5},{5,6},{6,7},{7,8},{8,9},{9,10... | collective-permute-start | bytes 221192 | tf_op jit(solution)/shard_map/while/body/eval_jaxpr/ppermute | solution.py:12
  261.3 10.6 %collective-permute-start.1 = (f32[32,1152]{1,0:T(8,128)S(1)}, f32[32,1152]{1,0:T(8,128)S(1)}, u32[]{:S(2)}, u32[]{:S(2)}) collective-permute-start(f32[32,1152]{1,0:T(8,128)S(1)} %fusion.39), channel_id=1, source_target_pairs={{31,0},{0,1},{1,2},{2,3},{3,4},{4,5},{5,6},{6,7},{7,8},{8,9},{9,10... | collective-permute-start | bytes 442376 | tf_op jit(solution)/shard_map/while/body/eval_jaxpr/ppermute | solution.py:12
  272.0 9.4 %collective-permute-start = (bf16[32,1152]{1,0:T(8,128)(2,1)S(1)}, bf16[32,1152]{1,0:T(8,128)(2,1)S(1)}, u32[]{:S(2)}, u32[]{:S(2)}) collective-permute-start(bf16[32,1152]{1,0:T(8,128)(2,1)S(1)} %copy.14), channel_id=1, source_target_pairs={{31,0},{0,1},{1,2},{2,3},{3,4},{4,5},{5,6},{6,7},{7,8},{8,9},{9,10... | collective-permute-start | bytes 221192 | tf_op jit(solution)/shard_map/while/body/eval_jaxpr/ppermute | solution.py:12
  277.3 10.8 %collective-permute-start.1 = (f32[32,1152]{1,0:T(8,128)S(1)}, f32[32,1152]{1,0:T(8,128)S(1)}, u32[]{:S(2)}, u32[]{:S(2)}) collective-permute-start(f32[32,1152]{1,0:T(8,128)S(1)} %fusion.39), channel_id=1, source_target_pairs={{31,0},{0,1},{1,2},{2,3},{3,4},{4,5},{5,6},{6,7},{7,8},{8,9},{9,10... | collective-permute-start | bytes 442376 | tf_op jit(solution)/shard_map/while/body/eval_jaxpr/ppermute | solution.py:12
  288.2 9.3 %collective-permute-start = (bf16[32,1152]{1,0:T(8,128)(2,1)S(1)}, bf16[32,1152]{1,0:T(8,128)(2,1)S(1)}, u32[]{:S(2)}, u32[]{:S(2)}) collective-permute-start(bf16[32,1152]{1,0:T(8,128)(2,1)S(1)} %copy.14), channel_id=1, source_target_pairs={{31,0},{0,1},{1,2},{2,3},{3,4},{4,5},{5,6},{6,7},{7,8},{8,9},{9,10... | collective-permute-start | bytes 221192 | tf_op jit(solution)/shard_map/while/body/eval_jaxpr/ppermute | solution.py:12
  292.9 12.3 %collective-permute-start.1 = (f32[32,1152]{1,0:T(8,128)S(1)}, f32[32,1152]{1,0:T(8,128)S(1)}, u32[]{:S(2)}, u32[]{:S(2)}) collective-permute-start(f32[32,1152]{1,0:T(8,128)S(1)} %fusion.39), channel_id=1, source_target_pairs={{31,0},{0,1},{1,2},{2,3},{3,4},{4,5},{5,6},{6,7},{7,8},{8,9},{9,10... | collective-permute-start | bytes 442376 | tf_op jit(solution)/shard_map/while/body/eval_jaxpr/ppermute | solution.py:12
  310.0 10.3 %collective-permute-start.1 = (f32[32,1152]{1,0:T(8,128)S(1)}, f32[32,1152]{1,0:T(8,128)S(1)}, u32[]{:S(2)}, u32[]{:S(2)}) collective-permute-start(f32[32,1152]{1,0:T(8,128)S(1)} %fusion.39), channel_id=1, source_target_pairs={{31,0},{0,1},{1,2},{2,3},{3,4},{4,5},{5,6},{6,7},{7,8},{8,9},{9,10... | collective-permute-start | bytes 442376 | tf_op jit(solution)/shard_map/while/body/eval_jaxpr/ppermute | solution.py:12
  320.3 9.3 %collective-permute-start = (bf16[32,1152]{1,0:T(8,128)(2,1)S(1)}, bf16[32,1152]{1,0:T(8,128)(2,1)S(1)}, u32[]{:S(2)}, u32[]{:S(2)}) collective-permute-start(bf16[32,1152]{1,0:T(8,128)(2,1)S(1)} %copy.14), channel_id=1, source_target_pairs={{31,0},{0,1},{1,2},{2,3},{3,4},{4,5},{5,6},{6,7},{7,8},{8,9},{9,10... | collective-permute-start | bytes 221192 | tf_op jit(solution)/shard_map/while/body/eval_jaxpr/ppermute | solution.py:12
  325.0 12.5 %collective-permute-start.1 = (f32[32,1152]{1,0:T(8,128)S(1)}, f32[32,1152]{1,0:T(8,128)S(1)}, u32[]{:S(2)}, u32[]{:S(2)}) collective-permute-start(f32[32,1152]{1,0:T(8,128)S(1)} %fusion.39), channel_id=1, source_target_pairs={{31,0},{0,1},{1,2},{2,3},{3,4},{4,5},{5,6},{6,7},{7,8},{8,9},{9,10... | collective-permute-start | bytes 442376 | tf_op jit(solution)/shard_map/while/body/eval_jaxpr/ppermute | solution.py:12
  337.5 9.3 %collective-permute-start = (bf16[32,1152]{1,0:T(8,128)(2,1)S(1)}, bf16[32,1152]{1,0:T(8,128)(2,1)S(1)}, u32[]{:S(2)}, u32[]{:S(2)}) collective-permute-start(bf16[32,1152]{1,0:T(8,128)(2,1)S(1)} %copy.14), channel_id=1, source_target_pairs={{31,0},{0,1},{1,2},{2,3},{3,4},{4,5},{5,6},{6,7},{7,8},{8,9},{9,10... | collective-permute-start | bytes 221192 | tf_op jit(solution)/shard_map/while/body/eval_jaxpr/ppermute | solution.py:12
  342.2 10.6 %collective-permute-start.1 = (f32[32,1152]{1,0:T(8,128)S(1)}, f32[32,1152]{1,0:T(8,128)S(1)}, u32[]{:S(2)}, u32[]{:S(2)}) collective-permute-start(f32[32,1152]{1,0:T(8,128)S(1)} %fusion.39), channel_id=1, source_target_pairs={{31,0},{0,1},{1,2},{2,3},{3,4},{4,5},{5,6},{6,7},{7,8},{8,9},{9,10... | collective-permute-start | bytes 442376 | tf_op jit(solution)/shard_map/while/body/eval_jaxpr/ppermute | solution.py:12
  352.9 9.3 %collective-permute-start = (bf16[32,1152]{1,0:T(8,128)(2,1)S(1)}, bf16[32,1152]{1,0:T(8,128)(2,1)S(1)}, u32[]{:S(2)}, u32[]{:S(2)}) collective-permute-start(bf16[32,1152]{1,0:T(8,128)(2,1)S(1)} %copy.14), channel_id=1, source_target_pairs={{31,0},{0,1},{1,2},{2,3},{3,4},{4,5},{5,6},{6,7},{7,8},{8,9},{9,10... | collective-permute-start | bytes 221192 | tf_op jit(solution)/shard_map/while/body/eval_jaxpr/ppermute | solution.py:12
  357.6 10.1 %collective-permute-start.1 = (f32[32,1152]{1,0:T(8,128)S(1)}, f32[32,1152]{1,0:T(8,128)S(1)}, u32[]{:S(2)}, u32[]{:S(2)}) collective-permute-start(f32[32,1152]{1,0:T(8,128)S(1)} %fusion.39), channel_id=1, source_target_pairs={{31,0},{0,1},{1,2},{2,3},{3,4},{4,5},{5,6},{6,7},{7,8},{8,9},{9,10... | collective-permute-start | bytes 442376 | tf_op jit(solution)/shard_map/while/body/eval_jaxpr/ppermute | solution.py:12
  367.7 10.8 %collective-permute-start = (bf16[32,1152]{1,0:T(8,128)(2,1)S(1)}, bf16[32,1152]{1,0:T(8,128)(2,1)S(1)}, u32[]{:S(2)}, u32[]{:S(2)}) collective-permute-start(bf16[32,1152]{1,0:T(8,128)(2,1)S(1)} %copy.14), channel_id=1, source_target_pairs={{31,0},{0,1},{1,2},{2,3},{3,4},{4,5},{5,6},{6,7},{7,8},{8,9},{9,10... | collective-permute-start | bytes 221192 | tf_op jit(solution)/shard_map/while/body/eval_jaxpr/ppermute | solution.py:12
  372.4 10.1 %collective-permute-start.1 = (f32[32,1152]{1,0:T(8,128)S(1)}, f32[32,1152]{1,0:T(8,128)S(1)}, u32[]{:S(2)}, u32[]{:S(2)}) collective-permute-start(f32[32,1152]{1,0:T(8,128)S(1)} %fusion.39), channel_id=1, source_target_pairs={{31,0},{0,1},{1,2},{2,3},{3,4},{4,5},{5,6},{6,7},{7,8},{8,9},{9,10... | collective-permute-start | bytes 442376 | tf_op jit(solution)/shard_map/while/body/eval_jaxpr/ppermute | solution.py:12
  382.5 10.2 %collective-permute-start = (bf16[32,1152]{1,0:T(8,128)(2,1)S(1)}, bf16[32,1152]{1,0:T(8,128)(2,1)S(1)}, u32[]{:S(2)}, u32[]{:S(2)}) collective-permute-start(bf16[32,1152]{1,0:T(8,128)(2,1)S(1)} %copy.14), channel_id=1, source_target_pairs={{31,0},{0,1},{1,2},{2,3},{3,4},{4,5},{5,6},{6,7},{7,8},{8,9},{9,10... | collective-permute-start | bytes 221192 | tf_op jit(solution)/shard_map/while/body/eval_jaxpr/ppermute | solution.py:12
  387.3 11.1 %collective-permute-start.1 = (f32[32,1152]{1,0:T(8,128)S(1)}, f32[32,1152]{1,0:T(8,128)S(1)}, u32[]{:S(2)}, u32[]{:S(2)}) collective-permute-start(f32[32,1152]{1,0:T(8,128)S(1)} %fusion.39), channel_id=1, source_target_pairs={{31,0},{0,1},{1,2},{2,3},{3,4},{4,5},{5,6},{6,7},{7,8},{8,9},{9,10... | collective-permute-start | bytes 442376 | tf_op jit(solution)/shard_map/while/body/eval_jaxpr/ppermute | solution.py:12
  398.4 10.6 %collective-permute-start = (bf16[32,1152]{1,0:T(8,128)(2,1)S(1)}, bf16[32,1152]{1,0:T(8,128)(2,1)S(1)}, u32[]{:S(2)}, u32[]{:S(2)}) collective-permute-start(bf16[32,1152]{1,0:T(8,128)(2,1)S(1)} %copy.14), channel_id=1, source_target_pairs={{31,0},{0,1},{1,2},{2,3},{3,4},{4,5},{5,6},{6,7},{7,8},{8,9},{9,10... | collective-permute-start | bytes 221192 | tf_op jit(solution)/shard_map/while/body/eval_jaxpr/ppermute | solution.py:12
  404.2 11.4 %collective-permute-start.1 = (f32[32,1152]{1,0:T(8,128)S(1)}, f32[32,1152]{1,0:T(8,128)S(1)}, u32[]{:S(2)}, u32[]{:S(2)}) collective-permute-start(f32[32,1152]{1,0:T(8,128)S(1)} %fusion.39), channel_id=1, source_target_pairs={{31,0},{0,1},{1,2},{2,3},{3,4},{4,5},{5,6},{6,7},{7,8},{8,9},{9,10... | collective-permute-start | bytes 442376 | tf_op jit(solution)/shard_map/while/body/eval_jaxpr/ppermute | solution.py:12
  415.7 10.2 %collective-permute-start = (bf16[32,1152]{1,0:T(8,128)(2,1)S(1)}, bf16[32,1152]{1,0:T(8,128)(2,1)S(1)}, u32[]{:S(2)}, u32[]{:S(2)}) collective-permute-start(bf16[32,1152]{1,0:T(8,128)(2,1)S(1)} %copy.14), channel_id=1, source_target_pairs={{31,0},{0,1},{1,2},{2,3},{3,4},{4,5},{5,6},{6,7},{7,8},{8,9},{9,10... | collective-permute-start | bytes 221192 | tf_op jit(solution)/shard_map/while/body/eval_jaxpr/ppermute | solution.py:12
  420.4 13.4 %collective-permute-start.1 = (f32[32,1152]{1,0:T(8,128)S(1)}, f32[32,1152]{1,0:T(8,128)S(1)}, u32[]{:S(2)}, u32[]{:S(2)}) collective-permute-start(f32[32,1152]{1,0:T(8,128)S(1)} %fusion.39), channel_id=1, source_target_pairs={{31,0},{0,1},{1,2},{2,3},{3,4},{4,5},{5,6},{6,7},{7,8},{8,9},{9,10... | collective-permute-start | bytes 442376 | tf_op jit(solution)/shard_map/while/body/eval_jaxpr/ppermute | solution.py:12
  433.8 10.1 %collective-permute-start = (bf16[32,1152]{1,0:T(8,128)(2,1)S(1)}, bf16[32,1152]{1,0:T(8,128)(2,1)S(1)}, u32[]{:S(2)}, u32[]{:S(2)}) collective-permute-start(bf16[32,1152]{1,0:T(8,128)(2,1)S(1)} %copy.14), channel_id=1, source_target_pairs={{31,0},{0,1},{1,2},{2,3},{3,4},{4,5},{5,6},{6,7},{7,8},{8,9},{9,10... | collective-permute-start | bytes 221192 | tf_op jit(solution)/shard_map/while/body/eval_jaxpr/ppermute | solution.py:12
  438.5 12.2 %collective-permute-start.1 = (f32[32,1152]{1,0:T(8,128)S(1)}, f32[32,1152]{1,0:T(8,128)S(1)}, u32[]{:S(2)}, u32[]{:S(2)}) collective-permute-start(f32[32,1152]{1,0:T(8,128)S(1)} %fusion.39), channel_id=1, source_target_pairs={{31,0},{0,1},{1,2},{2,3},{3,4},{4,5},{5,6},{6,7},{7,8},{8,9},{9,10... | collective-permute-start | bytes 442376 | tf_op jit(solution)/shard_map/while/body/eval_jaxpr/ppermute | solution.py:12
  450.7 9.8 %collective-permute-start = (bf16[32,1152]{1,0:T(8,128)(2,1)S(1)}, bf16[32,1152]{1,0:T(8,128)(2,1)S(1)}, u32[]{:S(2)}, u32[]{:S(2)}) collective-permute-start(bf16[32,1152]{1,0:T(8,128)(2,1)S(1)} %copy.14), channel_id=1, source_target_pairs={{31,0},{0,1},{1,2},{2,3},{3,4},{4,5},{5,6},{6,7},{7,8},{8,9},{9,10... | collective-permute-start | bytes 221192 | tf_op jit(solution)/shard_map/while/body/eval_jaxpr/ppermute | solution.py:12
  455.5 11.5 %collective-permute-start.1 = (f32[32,1152]{1,0:T(8,128)S(1)}, f32[32,1152]{1,0:T(8,128)S(1)}, u32[]{:S(2)}, u32[]{:S(2)}) collective-permute-start(f32[32,1152]{1,0:T(8,128)S(1)} %fusion.39), channel_id=1, source_target_pairs={{31,0},{0,1},{1,2},{2,3},{3,4},{4,5},{5,6},{6,7},{7,8},{8,9},{9,10... | collective-permute-start | bytes 442376 | tf_op jit(solution)/shard_map/while/body/eval_jaxpr/ppermute | solution.py:12
  467.0 10.0 %collective-permute-start = (bf16[32,1152]{1,0:T(8,128)(2,1)S(1)}, bf16[32,1152]{1,0:T(8,128)(2,1)S(1)}, u32[]{:S(2)}, u32[]{:S(2)}) collective-permute-start(bf16[32,1152]{1,0:T(8,128)(2,1)S(1)} %copy.14), channel_id=1, source_target_pairs={{31,0},{0,1},{1,2},{2,3},{3,4},{4,5},{5,6},{6,7},{7,8},{8,9},{9,10... | collective-permute-start | bytes 221192 | tf_op jit(solution)/shard_map/while/body/eval_jaxpr/ppermute | solution.py:12
  471.7 12.0 %collective-permute-start.1 = (f32[32,1152]{1,0:T(8,128)S(1)}, f32[32,1152]{1,0:T(8,128)S(1)}, u32[]{:S(2)}, u32[]{:S(2)}) collective-permute-start(f32[32,1152]{1,0:T(8,128)S(1)} %fusion.39), channel_id=1, source_target_pairs={{31,0},{0,1},{1,2},{2,3},{3,4},{4,5},{5,6},{6,7},{7,8},{8,9},{9,10... | collective-permute-start | bytes 442376 | tf_op jit(solution)/shard_map/while/body/eval_jaxpr/ppermute | solution.py:12
  483.8 9.9 %collective-permute-start = (bf16[32,1152]{1,0:T(8,128)(2,1)S(1)}, bf16[32,1152]{1,0:T(8,128)(2,1)S(1)}, u32[]{:S(2)}, u32[]{:S(2)}) collective-permute-start(bf16[32,1152]{1,0:T(8,128)(2,1)S(1)} %copy.14), channel_id=1, source_target_pairs={{31,0},{0,1},{1,2},{2,3},{3,4},{4,5},{5,6},{6,7},{7,8},{8,9},{9,10... | collective-permute-start | bytes 221192 | tf_op jit(solution)/shard_map/while/body/eval_jaxpr/ppermute | solution.py:12
  488.5 12.0 %collective-permute-start.1 = (f32[32,1152]{1,0:T(8,128)S(1)}, f32[32,1152]{1,0:T(8,128)S(1)}, u32[]{:S(2)}, u32[]{:S(2)}) collective-permute-start(f32[32,1152]{1,0:T(8,128)S(1)} %fusion.39), channel_id=1, source_target_pairs={{31,0},{0,1},{1,2},{2,3},{3,4},{4,5},{5,6},{6,7},{7,8},{8,9},{9,10... | collective-permute-start | bytes 442376 | tf_op jit(solution)/shard_map/while/body/eval_jaxpr/ppermute | solution.py:12
  500.6 9.5 %collective-permute-start = (bf16[32,1152]{1,0:T(8,128)(2,1)S(1)}, bf16[32,1152]{1,0:T(8,128)(2,1)S(1)}, u32[]{:S(2)}, u32[]{:S(2)}) collective-permute-start(bf16[32,1152]{1,0:T(8,128)(2,1)S(1)} %copy.14), channel_id=1, source_target_pairs={{31,0},{0,1},{1,2},{2,3},{3,4},{4,5},{5,6},{6,7},{7,8},{8,9},{9,10... | collective-permute-start | bytes 221192 | tf_op jit(solution)/shard_map/while/body/eval_jaxpr/ppermute | solution.py:12
  505.3 12.1 %collective-permute-start.1 = (f32[32,1152]{1,0:T(8,128)S(1)}, f32[32,1152]{1,0:T(8,128)S(1)}, u32[]{:S(2)}, u32[]{:S(2)}) collective-permute-start(f32[32,1152]{1,0:T(8,128)S(1)} %fusion.39), channel_id=1, source_target_pairs={{31,0},{0,1},{1,2},{2,3},{3,4},{4,5},{5,6},{6,7},{7,8},{8,9},{9,10... | collective-permute-start | bytes 442376 | tf_op jit(solution)/shard_map/while/body/eval_jaxpr/ppermute | solution.py:12
  517.4 9.5 %collective-permute-start = (bf16[32,1152]{1,0:T(8,128)(2,1)S(1)}, bf16[32,1152]{1,0:T(8,128)(2,1)S(1)}, u32[]{:S(2)}, u32[]{:S(2)}) collective-permute-start(bf16[32,1152]{1,0:T(8,128)(2,1)S(1)} %copy.14), channel_id=1, source_target_pairs={{31,0},{0,1},{1,2},{2,3},{3,4},{4,5},{5,6},{6,7},{7,8},{8,9},{9,10... | collective-permute-start | bytes 221192 | tf_op jit(solution)/shard_map/while/body/eval_jaxpr/ppermute | solution.py:12
  522.1 12.1 %collective-permute-start.1 = (f32[32,1152]{1,0:T(8,128)S(1)}, f32[32,1152]{1,0:T(8,128)S(1)}, u32[]{:S(2)}, u32[]{:S(2)}) collective-permute-start(f32[32,1152]{1,0:T(8,128)S(1)} %fusion.39), channel_id=1, source_target_pairs={{31,0},{0,1},{1,2},{2,3},{3,4},{4,5},{5,6},{6,7},{7,8},{8,9},{9,10... | collective-permute-start | bytes 442376 | tf_op jit(solution)/shard_map/while/body/eval_jaxpr/ppermute | solution.py:12
  534.2 9.5 %collective-permute-start = (bf16[32,1152]{1,0:T(8,128)(2,1)S(1)}, bf16[32,1152]{1,0:T(8,128)(2,1)S(1)}, u32[]{:S(2)}, u32[]{:S(2)}) collective-permute-start(bf16[32,1152]{1,0:T(8,128)(2,1)S(1)} %copy.14), channel_id=1, source_target_pairs={{31,0},{0,1},{1,2},{2,3},{3,4},{4,5},{5,6},{6,7},{7,8},{8,9},{9,10... | collective-permute-start | bytes 221192 | tf_op jit(solution)/shard_map/while/body/eval_jaxpr/ppermute | solution.py:12
  538.9 13.7 %collective-permute-start.1 = (f32[32,1152]{1,0:T(8,128)S(1)}, f32[32,1152]{1,0:T(8,128)S(1)}, u32[]{:S(2)}, u32[]{:S(2)}) collective-permute-start(f32[32,1152]{1,0:T(8,128)S(1)} %fusion.39), channel_id=1, source_target_pairs={{31,0},{0,1},{1,2},{2,3},{3,4},{4,5},{5,6},{6,7},{7,8},{8,9},{9,10... | collective-permute-start | bytes 442376 | tf_op jit(solution)/shard_map/while/body/eval_jaxpr/ppermute | solution.py:12
  552.6 10.6 %collective-permute-start = (bf16[32,1152]{1,0:T(8,128)(2,1)S(1)}, bf16[32,1152]{1,0:T(8,128)(2,1)S(1)}, u32[]{:S(2)}, u32[]{:S(2)}) collective-permute-start(bf16[32,1152]{1,0:T(8,128)(2,1)S(1)} %copy.14), channel_id=1, source_target_pairs={{31,0},{0,1},{1,2},{2,3},{3,4},{4,5},{5,6},{6,7},{7,8},{8,9},{9,10... | collective-permute-start | bytes 221192 | tf_op jit(solution)/shard_map/while/body/eval_jaxpr/ppermute | solution.py:12
  557.3 13.6 %collective-permute-start.1 = (f32[32,1152]{1,0:T(8,128)S(1)}, f32[32,1152]{1,0:T(8,128)S(1)}, u32[]{:S(2)}, u32[]{:S(2)}) collective-permute-start(f32[32,1152]{1,0:T(8,128)S(1)} %fusion.39), channel_id=1, source_target_pairs={{31,0},{0,1},{1,2},{2,3},{3,4},{4,5},{5,6},{6,7},{7,8},{8,9},{9,10... | collective-permute-start | bytes 442376 | tf_op jit(solution)/shard_map/while/body/eval_jaxpr/ppermute | solution.py:12
  571.0 9.9 %collective-permute-start = (bf16[32,1152]{1,0:T(8,128)(2,1)S(1)}, bf16[32,1152]{1,0:T(8,128)(2,1)S(1)}, u32[]{:S(2)}, u32[]{:S(2)}) collective-permute-start(bf16[32,1152]{1,0:T(8,128)(2,1)S(1)} %copy.14), channel_id=1, source_target_pairs={{31,0},{0,1},{1,2},{2,3},{3,4},{4,5},{5,6},{6,7},{7,8},{8,9},{9,10... | collective-permute-start | bytes 221192 | tf_op jit(solution)/shard_map/while/body/eval_jaxpr/ppermute | solution.py:12
  575.7 12.5 %collective-permute-start.1 = (f32[32,1152]{1,0:T(8,128)S(1)}, f32[32,1152]{1,0:T(8,128)S(1)}, u32[]{:S(2)}, u32[]{:S(2)}) collective-permute-start(f32[32,1152]{1,0:T(8,128)S(1)} %fusion.39), channel_id=1, source_target_pairs={{31,0},{0,1},{1,2},{2,3},{3,4},{4,5},{5,6},{6,7},{7,8},{8,9},{9,10... | collective-permute-start | bytes 442376 | tf_op jit(solution)/shard_map/while/body/eval_jaxpr/ppermute | solution.py:12
  (5 other events, 116.8 us)
Sparse Core Ops, SparseCore 0:
  10.7 43.9 all-gather.1
  593.0 95.4 reduce-scatter.1
where the time goes:
time: 703 us; the launch traced here: 698 us
  waiting for transfers between devices  421 us (60%)
  starting transfers between devices  136 us (19%)
  matrix products  92.2 us (13%)
  local copies, waits for them, and re-layouts  23.1 us (3%)
  between operations  14.7 us (2%)
  other arithmetic  8.66 us (1%)
    ppermute x64, waiting for transfers between devices, from_behind(): return lax.ppermute(block, axis, route)  285 us
    ppermute x64, starting transfers between devices, from_behind(): return lax.ppermute(block, axis, route)  136 us
    reduce_scatter x1, waiting for transfers between devices, per_device(): lax.psum_scatter(img_part, 'img', scatter_dimension=0, tiled=True)  93.8 us
    dot_general x32, matrix products, score_block(): lax.dot_general(stretch, gathered, (((1,), (1,)), ((), ())), preferred_el...  56.7 us
    all_gather x1, waiting for transfers between devices, per_device(): lax.all_gather(img_unit.astype(jnp.bfloat16), 'img', axis=0, tiled=True)  42.2 us
    dot_general x32, matrix products, score_block(): jnp.dot(weights, gathered, preferred_element_type=jnp.float32)  30.8 us
    dynamic_update_slice x32, local copies, waits for them, and re-layouts, advance(): lax.dynamic_update_slice_in_dim(text_store, stretch, step * rows, 0)  20.4 us
  transfers between devices with their start and end apart: 66, of which 63 were waited for; matrix products, arithmetic and copies ran while one was open for 16% of the time, Pallas kernels for 0%

commit v1 on v0

v1 whole, which is shorter than its diff:
```python
import jax
import jax.numpy as jnp
from jax import lax
from jax.sharding import Mesh, PartitionSpec as P

EPS = 1e-06
SIZES = (("zl", 2), ("x", 4), ("c", 2), ("y", 8), ("zh", 4))
IMG_ORDER = ("y", "zh", "zl", "x", "c")
TXT_ORDER = ("zl", "x", "c", "y", "zh")
IMG_GROUP = ("zh", "x")
TXT_GROUP = ("zl", "y")


def unit_rows(embedded):
    values = embedded.astype(jnp.float32)
    inverse = lax.rsqrt(jnp.sum(values * values, axis=1, keepdims=True) + EPS)
    return (values * inverse, inverse)


def project_back(grad, unit, inverse):
    inner = jnp.sum(unit * grad, axis=1, keepdims=True)
    return (grad - unit * inner) * inverse


def exchange(blocks, axes):
    return lax.all_to_all(blocks, axes, 0, 0, tiled=False)


def spread(rows, axes):
    count = lax.axis_size(axes)
    copies = lax.optimization_barrier(jnp.broadcast_to(rows[None], (count,) + rows.shape))
    return exchange(copies, axes)


def swap_cores(block):
    return lax.ppermute(block, "c", [(0, 1), (1, 0)])


def row_ids(order, group, rows, fixed):
    size = dict(SIZES)
    count = 1
    for name in group:
        count *= size[name]
    index = lax.iota(jnp.int32, count * rows)
    peer, row = index // rows, index % rows
    place = {}
    for name in reversed(group):
        place[name] = peer % size[name]
        peer = peer // size[name]
    block = jnp.zeros_like(index)
    for name in order:
        block = block * size[name] + place.get(name, fixed[name])
    return block * rows + row


def weigh(text, image, text_ids, image_ids, scale, bias):
    scores = lax.dot_general(text, image, (((1,), (1,)), ((), ())), preferred_element_type=jnp.float32)
    match = (text_ids[:, None] == image_ids[None, :]).astype(jnp.float32)
    return (jax.nn.sigmoid(scale * scores + bias) - match).astype(jnp.bfloat16)


def down(weights, text):
    return lax.dot_general(weights, text, (((0,), (0,)), ((), ())), preferred_element_type=jnp.float32)


def per_device(image_emb, text_emb, logit_scale, logit_bias):
    scale = logit_scale[0]
    bias = logit_bias[0]
    rows, width = image_emb.shape
    img_unit, img_inv = unit_rows(image_emb)
    txt_unit, txt_inv = unit_rows(text_emb)

    own = spread(img_unit.astype(jnp.bfloat16), IMG_GROUP)
    own = own.reshape(-1, width)
    other = swap_cores(own)
    text = spread(txt_unit.astype(jnp.bfloat16), TXT_GROUP).reshape(-1, width)

    here = {name: lax.axis_index(name) for name, _ in SIZES}
    there = dict(here, c=1 - here["c"])
    text_ids = row_ids(TXT_ORDER, TXT_GROUP, rows, here)
    own_ids = row_ids(IMG_ORDER, IMG_GROUP, rows, here)
    other_ids = row_ids(IMG_ORDER, IMG_GROUP, rows, there)

    other_weights = weigh(text, other, text_ids, other_ids, scale, bias)
    foreign = swap_cores(down(other_weights, text).astype(jnp.bfloat16))
    own_weights = weigh(text, own, text_ids, own_ids, scale, bias)
    txt_part = jnp.dot(own_weights, own, preferred_element_type=jnp.float32)
    txt_part = txt_part + jnp.dot(other_weights, other, preferred_element_type=jnp.float32)
    txt_parts = exchange(txt_part.astype(jnp.bfloat16).reshape(-1, rows, width), TXT_GROUP)
    img_part = down(own_weights, text) + foreign.astype(jnp.float32)
    img_parts = exchange(img_part.astype(jnp.bfloat16).reshape(-1, rows, width), IMG_GROUP)

    txt_grad = scale * jnp.sum(txt_parts.astype(jnp.float32), axis=0)
    img_grad = scale * jnp.sum(img_parts.astype(jnp.float32), axis=0)
    return (project_back(img_grad, img_unit, img_inv), project_back(txt_grad, txt_unit, txt_inv))


def solution(mesh):
    names = tuple(name for name, _ in SIZES)
    fine = Mesh(mesh.devices.reshape(tuple(size for _, size in SIZES)), names)
    placed = (P(IMG_ORDER, None), P(TXT_ORDER, None), P(), P())
    return jax.shard_map(
        per_device,
        mesh=fine,
        in_specs=placed,
        out_specs=(P(IMG_ORDER, None), P(TXT_ORDER, None)),
        check_vma=False,
    )
```

time: 703 us -> 164 us (0.23)
  waiting for transfers between devices: 421 us -> 96.5 us
  starting transfers between devices: 136 us -> 47 us
  matrix products: 92.2 us -> 8.35 us
  local copies, waits for them, and re-layouts: 23.1 us -> 2.95 us
  between operations: 14.7 us -> 2.12 us
    ppermute x64 -> x2, waiting for transfers between devices: 285 us -> 2.45 us  [swap_cores(): return lax.ppermute(block, 'c', [(0, 1), (1, 0)])]
    ppermute x64 -> x2, starting transfers between devices: 136 us -> 5.66 us  [swap_cores(): return lax.ppermute(block, 'c', [(0, 1), (1, 0)])]
    all_to_all x0 -> x4, waiting for transfers between devices: none -> 94 us  [exchange(): return lax.all_to_all(blocks, axes, 0, 0, tiled=False)]
    reduce_scatter x1 -> x0, waiting for transfers between devices: 93.8 us -> none  [per_device(): lax.psum_scatter(img_part, 'img', scatter_dimension=0, tiled=True)]
    dot_general x65 -> x6, matrix products: 92.2 us -> 8.35 us  [the longest x2 2.82 us: down(): lax.dot_general(weights, text, (((0,), (0,)), ((), ())), preferred_elemen...]
    all_gather x1 -> x0, waiting for transfers between devices: 42.2 us -> none  [per_device(): lax.all_gather(img_unit.astype(jnp.bfloat16), 'img', axis=0, tiled=True)]
    all_to_all x0 -> x4, starting transfers between devices: none -> 41.4 us  [exchange(): return lax.all_to_all(blocks, axes, 0, 0, tiled=False)]
    dynamic_update_slice x32 -> x0, local copies, waits for them, and re-layouts: 20.4 us -> none  [advance(): lax.dynamic_update_slice_in_dim(text_store, stretch, step * rows, 0)]
  transfers between devices with their start and end apart: 66 -> 6, of which waited for: 63 -> 5; matrix products, arithmetic and copies ran while one was open for 16% -> 5% of each run, Pallas kernels for 0% -> 0%
where the time goes in v1:
time: 164 us; the launch traced here: 162 us
  waiting for transfers between devices  96.5 us (59%)
  starting transfers between devices  47 us (29%)
  matrix products  8.35 us (5%)
  other arithmetic  5.07 us (3%)
  local copies, waits for them, and re-layouts  2.95 us (2%)
  between operations  2.12 us (1%)
    all_to_all x4, waiting for transfers between devices, exchange(): return lax.all_to_all(blocks, axes, 0, 0, tiled=False)  94 us
    all_to_all x4, starting transfers between devices, exchange(): return lax.all_to_all(blocks, axes, 0, 0, tiled=False)  41.4 us
    ppermute x2, starting transfers between devices, swap_cores(): return lax.ppermute(block, 'c', [(0, 1), (1, 0)])  5.66 us
  transfers between devices with their start and end apart: 6, of which 5 were waited for; matrix products, arithmetic and copies ran while one was open for 5% of the time, Pallas kernels for 0%

profile of v1, /device:TPU:1, one launch (start us, length us, event | category | flops | bytes accessed | tf_op | source)
XLA Modules:
  0.0 162.0 jit_solution(3768824636927678329)
XLA Ops:
  0.6 1.0 fusion.28
  1.6 1.0 fusion.17
  2.6 1.1 broadcast_in_dim.5
  3.8 0.0 copy-start
  3.8 13.6 %all-to-all-start.1 = ((bf16[16,32,1152]{2,1,0:T(8,128)(2,1)}), bf16[16,32,1152]{2,1,0:T(8,128)(2,1)S(1)}, u32[]{:S(2)}, u32[]{:S(2)}) async-start(bf16[16,32,1152]{2,1,0:T(8,128)(2,1)} %broadcast_in_dim.5), calls=%async_computation.1 | async-start | bytes 2359296 | tf_op jit(solution)/shard_map/all_to_all | solution.py:26
  17.3 0.0 copy-done
  17.3 0.1 fusion.24
  17.5 0.1 fusion.20
  17.5 1.1 broadcast_in_dim.4
  18.6 22.7 %all-to-all-done.1 = bf16[16,32,1152]{2,1,0:T(8,128)(2,1)S(1)} async-done(((bf16[16,32,1152]{2,1,0:T(8,128)(2,1)}), bf16[16,32,1152]{2,1,0:T(8,128)(2,1)S(1)}, u32[]{:S(2)}, u32[]{:S(2)}) %all-to-all-start.1) | async-done | bytes 1179680 | tf_op jit(solution)/shard_map/all_to_all | solution.py:26
  41.3 17.7 %all-to-all-start = ((bf16[16,32,1152]{2,1,0:T(8,128)(2,1)}), bf16[16,32,1152]{2,1,0:T(8,128)(2,1)S(1)}, u32[]{:S(2)}, u32[]{:S(2)}) async-start(bf16[16,32,1152]{2,1,0:T(8,128)(2,1)} %broadcast_in_dim.4), calls=%async_computation | async-start | bytes 2359296 | tf_op jit(solution)/shard_map/all_to_all | solution.py:26
  59.0 3.0 %collective-permute-start = (bf16[512,1152]{1,0:T(8,128)(2,1)S(1)}, bf16[512,1152]{1,0:T(8,128)(2,1)S(1)}, u32[]{:S(2)}, u32[]{:S(2)}) collective-permute-start(bf16[512,1152]{1,0:T(8,128)(2,1)S(1)} %bitcast.26), channel_id=1, source_target_pairs={{0,32},{32,0},{1,33},{33,1},{2,34},{34,2},{3,35},{35,3},{4,36},{36... | collective-permute-start | bytes 3538952 | tf_op jit(solution)/shard_map/ppermute | solution.py:36
  63.3 0.6 multiply_add_fusion.1
  64.0 23.3 %all-to-all-done = bf16[16,32,1152]{2,1,0:T(8,128)(2,1)S(1)} async-done(((bf16[16,32,1152]{2,1,0:T(8,128)(2,1)}), bf16[16,32,1152]{2,1,0:T(8,128)(2,1)S(1)}, u32[]{:S(2)}, u32[]{:S(2)}) %all-to-all-start) | async-done | bytes 1179680 | tf_op jit(solution)/shard_map/all_to_all | solution.py:26
  87.3 1.7 %fusion.13 = bf16[512,512]{1,0:T(8,128)(2,1)S(1)} fusion(bf16[512,1152]{1,0:T(8,128)(2,1)S(1)} %bitcast.29, bf16[512,1152]{1,0:T(8,128)(2,1)S(1)} %bitcast.27, s32[512]{0:T(512)} %multiply_add_fusion.1, f32[]{:T(128)} %bitcast.24, f32[]{:T(128)} %bitcast.19, s32[512]{0:T(512)S(1)} %get-tuple-element.3), kind=kOutput, calls=%fused_computation.20 | convolution fusion | flops 606339072 | bytes 2887688 | tf_op jit(solution)/shard_map/dot_general | solution.py:57
  89.0 0.0 copy-start.3
  89.0 0.9 fusion.54
  89.9 0.0 copy-done.3
  89.9 0.0 collective-permute-done
  89.9 1.1 fusion.14
  91.0 0.0 copy-start.5
  91.0 1.9 %fusion = bf16[512,1152]{1,0:T(8,128)(2,1)} fusion(f32[512,1152]{1,0:T(8,128)S(1)} %fusion.54, bf16[512,512]{1,0:T(8,128)(2,1)S(1)} %fusion.14, bf16[512,1152]{1,0:T(8,128)(2,1)S(1)} %collective-permute-done), kind=kOutput, calls=%fused_computation.1 | convolution fusion | flops 605159424 | bytes 5242880 | tf_op jit(solution)/shard_map/dot_general | solution.py:88
  92.9 0.0 copy-done.5
  92.9 0.0 copy-start.6
  92.9 6.3 %all-to-all-start.3 = ((bf16[16,32,1152]{2,1,0:T(8,128)(2,1)}), bf16[16,32,1152]{2,1,0:T(8,128)(2,1)S(1)}, u32[]{:S(2)}, u32[]{:S(2)}) async-start(bf16[16,32,1152]{2,1,0:T(8,128)(2,1)} %bitcast.5), calls=%async_computation.3 | async-start | bytes 2359296 | tf_op jit(solution)/shard_map/all_to_all | solution.py:26
  99.2 0.0 copy-done.6
  99.3 0.0 copy-start.4
  99.3 0.9 convolution_convert_fusion
  100.1 2.7 %collective-permute-start.1 = (bf16[512,1152]{1,0:T(8,128)(2,1)S(1)}, bf16[512,1152]{1,0:T(8,128)(2,1)S(1)}, u32[]{:S(2)}, u32[]{:S(2)}) collective-permute-start(bf16[512,1152]{1,0:T(8,128)(2,1)S(1)} %convolution_convert_fusion), channel_id=1, source_target_pairs={{0,32},{32,0},{1,33},{33,1},{2,34},{34,2},{3,35},{35,3},{4,36},{36... | collective-permute-start | bytes 3538952 | tf_op jit(solution)/shard_map/ppermute | solution.py:36
  102.8 2.5 %collective-permute-done.1 = bf16[512,1152]{1,0:T(8,128)(2,1)S(1)} collective-permute-done((bf16[512,1152]{1,0:T(8,128)(2,1)S(1)}, bf16[512,1152]{1,0:T(8,128)(2,1)S(1)}, u32[]{:S(2)}, u32[]{:S(2)}) %collective-permute-start.1) | collective-permute-done | bytes 1179680 | tf_op jit(solution)/shard_map/ppermute | solution.py:36
  105.3 0.0 copy-done.4
  105.3 1.9 %add_convert_fusion = bf16[512,1152]{1,0:T(8,128)(2,1)} fusion(bf16[512,1152]{1,0:T(8,128)(2,1)S(1)} %collective-permute-done.1, bf16[512,512]{1,0:T(8,128)(2,1)S(1)} %copy-done.4, bf16[512,1152]{1,0:T(8,128)(2,1)S(1)} %bitcast.32), kind=kOutput, calls=%fused_computation.5 | convolution fusion | flops 605749248 | bytes 4063232 | tf_op jit(solution)/shard_map/dot_general | solution.py:63
  107.2 20.1 %all-to-all-done.3 = bf16[16,32,1152]{2,1,0:T(8,128)(2,1)S(1)} async-done(((bf16[16,32,1152]{2,1,0:T(8,128)(2,1)}), bf16[16,32,1152]{2,1,0:T(8,128)(2,1)S(1)}, u32[]{:S(2)}, u32[]{:S(2)}) %all-to-all-start.3) | async-done | bytes 1179680 | tf_op jit(solution)/shard_map/all_to_all | solution.py:26
  127.3 3.8 %all-to-all-start.2 = ((bf16[16,32,1152]{2,1,0:T(8,128)(2,1)}), bf16[16,32,1152]{2,1,0:T(8,128)(2,1)S(1)}, u32[]{:S(2)}, u32[]{:S(2)}) async-start(bf16[16,32,1152]{2,1,0:T(8,128)(2,1)} %bitcast.4), calls=%async_computation.2 | async-start | bytes 2359296 | tf_op jit(solution)/shard_map/all_to_all | solution.py:26
  131.1 0.0 copy-start.1
  131.1 0.2 convert_reduce_fusion
  131.3 0.0 copy-start.2
  131.3 0.7 copy-done.1
  132.0 0.2 fusion.21
  132.2 0.8 fusion.23
  132.9 28.0 %all-to-all-done.2 = bf16[16,32,1152]{2,1,0:T(8,128)(2,1)S(1)} async-done(((bf16[16,32,1152]{2,1,0:T(8,128)(2,1)}), bf16[16,32,1152]{2,1,0:T(8,128)(2,1)S(1)}, u32[]{:S(2)}, u32[]{:S(2)}) %all-to-all-start.2) | async-done | bytes 1179680 | tf_op jit(solution)/shard_map/all_to_all | solution.py:26
  160.9 0.2 convert_reduce_fusion.1
  161.1 0.0 copy-done.2
  161.1 0.2 fusion.25
  161.3 0.8 fusion.27
  (3 shorter events, 0.0 us)
Async XLA Ops:
  3.8 13.6 %copy-start = (bf16[32,1152]{1,0:T(8,128)(2,1)S(1)}, bf16[32,1152]{1,0:T(8,128)(2,1)}, u32[]{:S(2)}) copy-start(bf16[32,1152]{1,0:T(8,128)(2,1)} %param.5) | copy-start | bytes 221188
  3.8 37.6 %all-to-all-start.1 = ((bf16[16,32,1152]{2,1,0:T(8,128)(2,1)}), bf16[16,32,1152]{2,1,0:T(8,128)(2,1)S(1)}, u32[]{:S(2)}, u32[]{:S(2)}) async-start(bf16[16,32,1152]{2,1,0:T(8,128)(2,1)} %broadcast_in_dim.5), calls=%async_computation.1 | async-start | bytes 2359296 | tf_op jit(solution)/shard_map/all_to_all | solution.py:26
  41.3 46.0 %all-to-all-start = ((bf16[16,32,1152]{2,1,0:T(8,128)(2,1)}), bf16[16,32,1152]{2,1,0:T(8,128)(2,1)S(1)}, u32[]{:S(2)}, u32[]{:S(2)}) async-start(bf16[16,32,1152]{2,1,0:T(8,128)(2,1)} %broadcast_in_dim.4), calls=%async_computation | async-start | bytes 2359296 | tf_op jit(solution)/shard_map/all_to_all | solution.py:26
  59.0 30.9 %collective-permute-start = (bf16[512,1152]{1,0:T(8,128)(2,1)S(1)}, bf16[512,1152]{1,0:T(8,128)(2,1)S(1)}, u32[]{:S(2)}, u32[]{:S(2)}) collective-permute-start(bf16[512,1152]{1,0:T(8,128)(2,1)S(1)} %bitcast.26), channel_id=1, source_target_pairs={{0,32},{32,0},{1,33},{33,1},{2,34},{34,2},{3,35},{35,3},{4,36},{36... | collective-permute-start | bytes 3538952 | tf_op jit(solution)/shard_map/ppermute | solution.py:36
  89.0 0.9 copy-start.3
  91.0 1.9 %copy-start.5 = (bf16[512,512]{1,0:T(8,128)(2,1)}, bf16[512,512]{1,0:T(8,128)(2,1)S(1)}, u32[]{:S(2)}) copy-start(bf16[512,512]{1,0:T(8,128)(2,1)S(1)} %fusion.14) | copy-start | bytes 1572868
  92.9 6.4 %copy-start.6 = (bf16[512,512]{1,0:T(8,128)(2,1)S(1)}, bf16[512,512]{1,0:T(8,128)(2,1)}, u32[]{:S(2)}) copy-start(bf16[512,512]{1,0:T(8,128)(2,1)} %copy-done.5) | copy-start | bytes 1572868
  92.9 34.4 %all-to-all-start.3 = ((bf16[16,32,1152]{2,1,0:T(8,128)(2,1)}), bf16[16,32,1152]{2,1,0:T(8,128)(2,1)S(1)}, u32[]{:S(2)}, u32[]{:S(2)}) async-start(bf16[16,32,1152]{2,1,0:T(8,128)(2,1)} %bitcast.5), calls=%async_computation.3 | async-start | bytes 2359296 | tf_op jit(solution)/shard_map/all_to_all | solution.py:26
  99.3 6.0 %copy-start.4 = (bf16[512,512]{1,0:T(8,128)(2,1)S(1)}, bf16[512,512]{1,0:T(8,128)(2,1)}, u32[]{:S(2)}) copy-start(bf16[512,512]{1,0:T(8,128)(2,1)} %copy-done.3) | copy-start | bytes 1572868
  100.1 5.1 %collective-permute-start.1 = (bf16[512,1152]{1,0:T(8,128)(2,1)S(1)}, bf16[512,1152]{1,0:T(8,128)(2,1)S(1)}, u32[]{:S(2)}, u32[]{:S(2)}) collective-permute-start(bf16[512,1152]{1,0:T(8,128)(2,1)S(1)} %convolution_convert_fusion), channel_id=1, source_target_pairs={{0,32},{32,0},{1,33},{33,1},{2,34},{34,2},{3,35},{35,3},{4,36},{36... | collective-permute-start | bytes 3538952 | tf_op jit(solution)/shard_map/ppermute | solution.py:36
  127.3 33.6 %all-to-all-start.2 = ((bf16[16,32,1152]{2,1,0:T(8,128)(2,1)}), bf16[16,32,1152]{2,1,0:T(8,128)(2,1)S(1)}, u32[]{:S(2)}, u32[]{:S(2)}) async-start(bf16[16,32,1152]{2,1,0:T(8,128)(2,1)} %bitcast.4), calls=%async_computation.2 | async-start | bytes 2359296 | tf_op jit(solution)/shard_map/all_to_all | solution.py:26
  131.1 0.9 copy-start.1
  131.3 29.8 %copy-start.2 = (bf16[32,1152]{1,0:T(8,128)(2,1)S(1)}, bf16[32,1152]{1,0:T(8,128)(2,1)}, u32[]{:S(2)}) copy-start(bf16[32,1152]{1,0:T(8,128)(2,1)} %param.4) | copy-start | bytes 221188

commit v2 on v1

v2 whole, which is shorter than its diff:
```python
import jax
import jax.numpy as jnp
from jax import lax
from jax.experimental import pallas as pl
from jax.experimental.pallas import tpu as pltpu
from jax.sharding import Mesh, PartitionSpec as P

EPS = 1e-06
NAMES = ("zl", "xh", "xl", "c", "y", "zh")
SHAPE = (2, 2, 2, 2, 8, 4)
IMG_ORDER = ("y", "zh", "zl", "xh", "xl", "c")
TXT_ORDER = ("zl", "xh", "xl", "c", "y", "zh")
PEERS = 16
HALF = 2
MIB = 1 << 20


def device_index(x, y, z, c):
    return ((((z % 2) * 4 + x) * 2 + c) * 8 + y) * 4 + z // 2


def exchange_groups():
    text = [
        [device_index(x, y, z, 0) for x in (first, first + 1) for y in range(8)]
        for first in (0, 2)
        for z in range(8)
    ]
    image = [
        [device_index(x, y, z, 1) for x in (first, 3 - first) for z in range(8)]
        for first in (0, 1)
        for y in range(8)
    ]
    return text + image


def exchange(blocks):
    return lax.all_to_all(blocks, NAMES, 0, 0, axis_index_groups=exchange_groups(), tiled=False)


def swap_cores(block):
    return lax.ppermute(block, "c", [(0, 1), (1, 0)])


def unit_rows(embedded):
    values = embedded.astype(jnp.float32)
    inverse = lax.rsqrt(jnp.sum(values * values, axis=1, keepdims=True) + EPS)
    return (values * inverse, inverse)


def project_back(grad, unit, inverse):
    inner = jnp.sum(unit * grad, axis=1, keepdims=True)
    return (grad - unit * inner) * inverse


def normalize_kernel(place, image, text, mine, given):
    img_unit = unit_rows(image[...])[0]
    txt_unit = unit_rows(text[...])[0]
    speaks_text = place[0] == 0
    mine[...] = jnp.where(speaks_text, txt_unit, img_unit).astype(jnp.bfloat16)
    given[...] = jnp.where(speaks_text, img_unit, txt_unit).astype(jnp.bfloat16)


def global_rows(index, is_text, place, rows):
    x, y, zl, zh = place[1], place[2], place[3], place[4]
    row = index % rows
    slot = (index // rows) % 2
    peer = index // (2 * rows)
    side, ring = peer // 8, peer % 8
    text = (((zl * 4 + (x // 2) * 2 + side) * 2 + slot) * 8 + ring) * 4 + zh
    low = jnp.minimum(x, 3 - x)
    across = low + side * (3 - 2 * low)
    image = ((y * 8 + ring) * 4 + across) * 2 + 1 - slot
    return jnp.where(is_text, text, image) * rows + row


def tile_kernel(rows, place, scalars, mine, theirs, grad_mine, grad_theirs):
    core = place[0]
    speaks_text = core == 0
    scale, bias = scalars[0], scalars[1]
    part = mine.shape[0] // HALF
    for half in range(HALF):
        start = pl.multiple_of(((half + core) % HALF) * part, part)
        here = mine[half * part : (half + 1) * part, :]
        there = theirs[pl.ds(start, part), :]
        scores = lax.dot_general(here, there, (((1,), (1,)), ((), ())), preferred_element_type=jnp.float32)
        here_ids = global_rows(
            half * part + lax.broadcasted_iota(jnp.int32, (part, 1), 0), speaks_text, place, rows
        )
        there_ids = global_rows(
            start + lax.broadcasted_iota(jnp.int32, (1, part), 1), jnp.logical_not(speaks_text), place, rows
        )
        match = jnp.where(here_ids == there_ids, 1.0, 0.0)
        weights = (jax.nn.sigmoid(scale * scores + bias) - match).astype(jnp.bfloat16)
        grad_mine[half * part : (half + 1) * part, :] = jnp.dot(
            weights, there, preferred_element_type=jnp.float32
        )
        grad_theirs[pl.ds(start, part), :] = lax.dot_general(
            weights, here, (((0,), (0,)), ((), ())), preferred_element_type=jnp.float32
        ).astype(jnp.bfloat16)


def finish_kernel(place, scalars, summed, received, image, text, grad_image, grad_text):
    speaks_text = place[0] == 0
    scale = scalars[0]
    own, other = scale * summed[...], scale * received[...]
    img_unit, img_inv = unit_rows(image[...])
    txt_unit, txt_inv = unit_rows(text[...])
    grad_image[...] = project_back(jnp.where(speaks_text, other, own), img_unit, img_inv)
    grad_text[...] = project_back(jnp.where(speaks_text, own, other), txt_unit, txt_inv)


SMEM = pl.BlockSpec(memory_space=pltpu.SMEM)
VMEM = pl.BlockSpec(memory_space=pltpu.VMEM)


def per_device(image_emb, text_emb, logit_scale, logit_bias):
    rows, width = image_emb.shape
    x = lax.axis_index("xh") * 2 + lax.axis_index("xl")
    place = jnp.stack(
        [lax.axis_index("c"), x, lax.axis_index("y"), lax.axis_index("zl"), lax.axis_index("zh")]
    ).astype(jnp.int32)
    scalars = jnp.concatenate([logit_scale, logit_bias])

    small = jax.ShapeDtypeStruct((rows, width), jnp.bfloat16)
    mine, given = pl.pallas_call(
        normalize_kernel,
        out_shape=(small, small),
        in_specs=[SMEM, VMEM, VMEM],
        out_specs=(VMEM, VMEM),
        name="normalize",
    )(place, image_emb, text_emb)
    block = jnp.concatenate([mine, swap_cores(given)], axis=0)
    copies = lax.optimization_barrier(jnp.broadcast_to(block[None], (PEERS, 2 * rows, width)))
    mine = exchange(copies).reshape(PEERS * 2 * rows, width)
    theirs = swap_cores(mine)

    total = PEERS * 2 * rows
    grad_mine, grad_theirs = pl.pallas_call(
        lambda *refs: tile_kernel(rows, *refs),
        out_shape=(
            jax.ShapeDtypeStruct((total, width), jnp.float32),
            jax.ShapeDtypeStruct((total, width), jnp.bfloat16),
        ),
        in_specs=[SMEM, SMEM, VMEM, VMEM],
        out_specs=(VMEM, VMEM),
        compiler_params=pltpu.CompilerParams(vmem_limit_bytes=40 * MIB),
        cost_estimate=pl.CostEstimate(
            flops=3 * total * total * width, bytes_accessed=10 * total * width, transcendentals=total * total // 2
        ),
        name="tile",
    )(place, scalars, mine, theirs)

    partial = grad_mine + swap_cores(grad_theirs).astype(jnp.float32)
    parts = exchange(partial.astype(jnp.bfloat16).reshape(PEERS, 2 * rows, width))
    summed = jnp.sum(parts.astype(jnp.float32), axis=0)
    received = swap_cores(summed[rows:])
    out = jax.ShapeDtypeStruct((rows, width), jnp.float32)
    return pl.pallas_call(
        finish_kernel,
        out_shape=(out, out),
        in_specs=[SMEM, SMEM, VMEM, VMEM, VMEM, VMEM],
        out_specs=(VMEM, VMEM),
        name="finish",
    )(place, scalars, summed[:rows], received, image_emb, text_emb)


def solution(mesh):
    fine = Mesh(mesh.devices.reshape(SHAPE), NAMES)
    return jax.shard_map(
        per_device,
        mesh=fine,
        in_specs=(P(IMG_ORDER, None), P(TXT_ORDER, None), P(), P()),
        out_specs=(P(IMG_ORDER, None), P(TXT_ORDER, None)),
        check_vma=False,
    )
```

time: 164 us -> 117 us (0.71); the launches traced: 162 us -> 117 us
  waiting for transfers between devices: 96.5 us -> 9.94 us
  blocking collectives: 0 us -> 76.7 us
  starting transfers between devices: 47 us -> 14.6 us
  Pallas kernels: 0 us -> 9.29 us
  matrix products: 8.35 us -> 0 us
  other arithmetic: 5.07 us -> 1.8 us
    all_to_all x4 -> x0, waiting for transfers between devices: 94 us -> none  [exchange(): return lax.all_to_all(blocks, axes, 0, 0, tiled=False)]
    all_to_all x0 -> x2, blocking collectives: none -> 76.7 us  [exchange(): lax.all_to_all(blocks, NAMES, 0, 0, axis_index_groups=exchange_groups(),...]
    all_to_all x4 -> x0, starting transfers between devices: 41.4 us -> none  [exchange(): return lax.all_to_all(blocks, axes, 0, 0, tiled=False)]
    pallas_call x0 -> x3, Pallas kernels: none -> 9.29 us  [the longest x1 5.6 us: per_device(): pl.pallas_call(lambda *refs: tile_kernel(rows, *refs), out_shape=(jax.Sha...]
    ppermute x2 -> x4, starting transfers between devices: 5.66 us -> 14.6 us  [swap_cores(): return lax.ppermute(block, 'c', [(0, 1), (1, 0)])]
    dot_general x6 -> x0, matrix products: 8.35 us -> none  [the longest x2 2.82 us: down(): lax.dot_general(weights, text, (((0,), (0,)), ((), ())), preferred_elemen...]
    ppermute x2 -> x4, waiting for transfers between devices: 2.45 us -> 9.94 us  [swap_cores(): return lax.ppermute(block, 'c', [(0, 1), (1, 0)])]
    broadcast_in_dim x2 -> x1, local copies, waits for them, and re-layouts: 2.23 us -> 0.31 us  [per_device(): jnp.broadcast_to(block[None], (PEERS, 2 * rows, width))]
  transfers between devices with their start and end apart: 6 -> 4, of which waited for: 5 -> 4; matrix products, arithmetic and copies ran while one was open for 5% -> 0% of each run, Pallas kernels for 0% -> 0%
where the time goes in v2:
time: 117 us
  blocking collectives  76.7 us (66%)
  starting transfers between devices  14.6 us (12%)
  waiting for transfers between devices  9.94 us (8%)
  Pallas kernels  9.29 us (8%)
  local copies, waits for them, and re-layouts  2.33 us (2%)
  between operations  2.01 us (2%)
  other arithmetic  1.8 us (2%)
    all_to_all x2, blocking collectives, exchange(): lax.all_to_all(blocks, NAMES, 0, 0, axis_index_groups=exchange_groups(),...  76.7 us
    ppermute x4, starting transfers between devices, swap_cores(): return lax.ppermute(block, 'c', [(0, 1), (1, 0)])  14.6 us
    ppermute x4, waiting for transfers between devices, swap_cores(): return lax.ppermute(block, 'c', [(0, 1), (1, 0)])  9.94 us
    pallas_call x1, Pallas kernels, per_device(): pl.pallas_call(lambda *refs: tile_kernel(rows, *refs), out_shape=(jax.Sha...  5.6 us
  transfers between devices with their start and end apart: 4, of which 4 were waited for; matrix products, arithmetic and copies ran while one was open for 0% of the time, Pallas kernels for 0%

profile of v2, /device:TPU:1, one launch (start us, length us, event | category | flops | bytes accessed | tf_op | source)
XLA Modules:
  0.0 116.7 jit_solution(4521657629390139097)
XLA Ops:
  0.6 0.7 stack.23.place.refs_0_
  1.3 1.7 %normalize.1 = (bf16[32,1152]{1,0:T(8,128)(2,1)}, bf16[32,1152]{1,0:T(8,128)(2,1)}) custom-call(s32[5]{0:T(128)} %stack.23.place.refs_0_, bf16[32,1152]{1,0:T(8,128)(2,1)} %image.3, bf16[32,1152]{1,0:T(8,128)(2,1)} %text.3), custom_call_target="tpu_custom_call" | custom-call | tf_op jit(solution)/shard_map/normalize/pallas_call | solution.py:125
  3.0 8.8 %collective-permute-start = (bf16[32,1152]{1,0:T(8,128)(2,1)}, bf16[32,1152]{1,0:T(8,128)(2,1)S(1)}, u32[]{:S(2)}, u32[]{:S(2)}) collective-permute-start(bf16[32,1152]{1,0:T(8,128)(2,1)} %get-tuple-element.7), channel_id=1, source_target_pairs={{0,32},{32,0},{1,33},{33,1},{2,34},{34,2},{3,35},{35,3},{4,36},{36... | collective-permute-start | bytes 221192 | tf_op jit(solution)/shard_map/ppermute | solution.py:41
  11.8 1.1 collective-permute-done
  12.9 0.9 pad_maximum_fusion
  13.8 0.3 broadcast_in_dim.2
  14.1 0.0 copy-start
  14.1 37.9 %all_to_all.10 = bf16[16,64,1152]{2,1,0:T(8,128)(2,1)S(1)} all-to-all(bf16[16,64,1152]{2,1,0:T(8,128)(2,1)S(1)} %broadcast_in_dim.2), channel_id=1, replica_groups={{0,4,8,12,16,20,24,28,64,68,72,76,80,84,88,92},{256,260,264,268,272,276..., dimensions={0} | all-to-all | bytes 4718592 | tf_op jit(solution)/shard_map/all_to_all | solution.py:37
  52.1 1.9 %collective-permute-start.1 = (bf16[1024,1152]{1,0:T(8,128)(2,1)S(1)}, bf16[1024,1152]{1,0:T(8,128)(2,1)S(1)}, u32[]{:S(2)}, u32[]{:S(2)}) collective-permute-start(bf16[1024,1152]{1,0:T(8,128)(2,1)S(1)} %bitcast.7), channel_id=1, source_target_pairs={{0,32},{32,0},{1,33},{33,1},{2,34},{34,2},{3,35},{35,3},{4,36},{36... | collective-permute-start | bytes 7077896 | tf_op jit(solution)/shard_map/ppermute | solution.py:41
  55.3 0.1 pad_maximum_fusion.1.refs_1_.scalars
  55.3 0.0 copy-start.1
  55.4 3.1 %collective-permute-done.1.refs_3_ = bf16[1024,1152]{1,0:T(8,128)(2,1)S(1)} collective-permute-done((bf16[1024,1152]{1,0:T(8,128)(2,1)S(1)}, bf16[1024,1152]{1,0:T(8,128)(2,1)S(1)}, u32[]{:S(2)}, u32[]{:S(2)}) %collective-permute-start.1) | collective-permute-done | bytes 2359328 | tf_op jit(solution)/shard_map/ppermute | solution.py:41
  58.5 0.0 copy-done
  58.5 5.6 %tile.1 = (f32[1024,1152]{1,0:T(8,128)S(1)}, bf16[1024,1152]{1,0:T(8,128)(2,1)S(1)}) custom-call(s32[5]{0:T(128)S(1)} %copy-done, f32[2]{0:T(128)S(1)} %pad_maximum_fusion.1.refs_1_.scalars, bf16[1024,1152]{1,0:T(8,128)(2,1)S(1)} %bitcast.8, bf16[1024,1152]{1,0:T(8,128)(2,1)S(1)} %collective-permute-done.1.refs_3_), custom_call_target="tpu_custom_call" | custom-call | flops 3623878656 | bytes 11796480 | tf_op jit(solution)/shard_map/tile/pallas_call | solution.py:138
  64.1 0.0 copy-done.1
  64.1 2.0 %collective-permute-start.2 = (bf16[1024,1152]{1,0:T(8,128)(2,1)S(1)}, bf16[1024,1152]{1,0:T(8,128)(2,1)S(1)}, u32[]{:S(2)}, u32[]{:S(2)}) collective-permute-start(bf16[1024,1152]{1,0:T(8,128)(2,1)S(1)} %get-tuple-element.9), channel_id=1, source_target_pairs={{0,32},{32,0},{1,33},{33,1},{2,34},{34,2},{3,35},{35,3},{4,36},{36... | collective-permute-start | bytes 7077896 | tf_op jit(solution)/shard_map/ppermute | solution.py:41
  66.1 4.4 %collective-permute-done.2 = bf16[1024,1152]{1,0:T(8,128)(2,1)S(1)} collective-permute-done((bf16[1024,1152]{1,0:T(8,128)(2,1)S(1)}, bf16[1024,1152]{1,0:T(8,128)(2,1)S(1)}, u32[]{:S(2)}, u32[]{:S(2)}) %collective-permute-start.2) | collective-permute-done | bytes 2359328 | tf_op jit(solution)/shard_map/ppermute | solution.py:41
  70.5 0.5 add_convert_fusion
  71.0 38.8 %all_to_all.11 = bf16[16,64,1152]{2,1,0:T(8,128)(2,1)S(1)} all-to-all(bf16[16,64,1152]{2,1,0:T(8,128)(2,1)S(1)} %bitcast.9), channel_id=1, replica_groups={{0,4,8,12,16,20,24,28,64,68,72,76,80,84,88,92},{256,260,264,268,272,276..., dimensions={0} | all-to-all | bytes 4718592 | tf_op jit(solution)/shard_map/all_to_all | solution.py:37
  109.9 0.3 convert_reduce_fusion
  110.2 0.7 fusion
  110.9 1.9 %collective-permute-start.3 = (f32[32,1152]{1,0:T(8,128)S(1)}, f32[32,1152]{1,0:T(8,128)S(1)}, u32[]{:S(2)}, u32[]{:S(2)}) collective-permute-start(f32[32,1152]{1,0:T(8,128)S(1)} %get-tuple-element.10), channel_id=1, source_target_pairs={{0,32},{32,0},{1,33},{33,1},{2,34},{34,2},{3,35},{35,3},{4,36},{36... | collective-permute-start | bytes 442376 | tf_op jit(solution)/shard_map/ppermute | solution.py:41
  112.8 1.3 %collective-permute-done.3.received = f32[32,1152]{1,0:T(8,128)S(1)} collective-permute-done((f32[32,1152]{1,0:T(8,128)S(1)}, f32[32,1152]{1,0:T(8,128)S(1)}, u32[]{:S(2)}, u32[]{:S(2)}) %collective-permute-start.3) | collective-permute-done | bytes 147488 | tf_op jit(solution)/shard_map/ppermute | solution.py:41
  114.1 0.0 copy-start.2
  114.1 0.7 copy-done.2
  114.8 2.0 %finish.1 = (f32[32,1152]{1,0:T(8,128)}, f32[32,1152]{1,0:T(8,128)}) custom-call(s32[5]{0:T(128)} %stack.23.place.refs_0_, f32[2]{0:T(128)} %copy-done.1, f32[32,1152]{1,0:T(8,128)} %get-tuple-element.11.summed, f32[32,1152]{1,0:T(8,128)} %copy-done.2, bf16[32,1152]{1,0:T(8,128)(2,1)} %image.3, bf16[32,1152]{1,0:T(8,128)(2,1)} %text.3), custom_call_target="tpu_custom_call" | custom-call | tf_op jit(solution)/shard_map/finish/pallas_call | solution.py:158
Async XLA Ops:
  3.0 9.9 %collective-permute-start = (bf16[32,1152]{1,0:T(8,128)(2,1)}, bf16[32,1152]{1,0:T(8,128)(2,1)S(1)}, u32[]{:S(2)}, u32[]{:S(2)}) collective-permute-start(bf16[32,1152]{1,0:T(8,128)(2,1)} %get-tuple-element.7), channel_id=1, source_target_pairs={{0,32},{32,0},{1,33},{33,1},{2,34},{34,2},{3,35},{35,3},{4,36},{36... | collective-permute-start | bytes 221192 | tf_op jit(solution)/shard_map/ppermute | solution.py:41
  14.1 44.4 %copy-start = (s32[5]{0:T(128)S(1)}, s32[5]{0:T(128)}, u32[]{:S(2)}) copy-start(s32[5]{0:T(128)} %stack.23.place.refs_0_) | copy-start | bytes 64
  52.1 6.4 %collective-permute-start.1 = (bf16[1024,1152]{1,0:T(8,128)(2,1)S(1)}, bf16[1024,1152]{1,0:T(8,128)(2,1)S(1)}, u32[]{:S(2)}, u32[]{:S(2)}) collective-permute-start(bf16[1024,1152]{1,0:T(8,128)(2,1)S(1)} %bitcast.7), channel_id=1, source_target_pairs={{0,32},{32,0},{1,33},{33,1},{2,34},{34,2},{3,35},{35,3},{4,36},{36... | collective-permute-start | bytes 7077896 | tf_op jit(solution)/shard_map/ppermute | solution.py:41
  55.3 8.7 %copy-start.1 = (f32[2]{0:T(128)}, f32[2]{0:T(128)S(1)}, u32[]{:S(2)}) copy-start(f32[2]{0:T(128)S(1)} %pad_maximum_fusion.1.refs_1_.scalars) | copy-start | bytes 28
  64.1 6.4 %collective-permute-start.2 = (bf16[1024,1152]{1,0:T(8,128)(2,1)S(1)}, bf16[1024,1152]{1,0:T(8,128)(2,1)S(1)}, u32[]{:S(2)}, u32[]{:S(2)}) collective-permute-start(bf16[1024,1152]{1,0:T(8,128)(2,1)S(1)} %get-tuple-element.9), channel_id=1, source_target_pairs={{0,32},{32,0},{1,33},{33,1},{2,34},{34,2},{3,35},{35,3},{4,36},{36... | collective-permute-start | bytes 7077896 | tf_op jit(solution)/shard_map/ppermute | solution.py:41
  110.9 3.3 %collective-permute-start.3 = (f32[32,1152]{1,0:T(8,128)S(1)}, f32[32,1152]{1,0:T(8,128)S(1)}, u32[]{:S(2)}, u32[]{:S(2)}) collective-permute-start(f32[32,1152]{1,0:T(8,128)S(1)} %get-tuple-element.10), channel_id=1, source_target_pairs={{0,32},{32,0},{1,33},{33,1},{2,34},{34,2},{3,35},{35,3},{4,36},{36... | collective-permute-start | bytes 442376 | tf_op jit(solution)/shard_map/ppermute | solution.py:41
  114.1 0.7 copy-start.2

commit v3 on v2

v3 whole, which is shorter than its diff:
```python
import jax
import jax.numpy as jnp
from jax import lax
from jax.experimental import pallas as pl
from jax.experimental.pallas import tpu as pltpu
from jax.sharding import Mesh, PartitionSpec as P

EPS = 1e-06
NAMES = ("zl", "xh", "xl", "c", "y", "zh")
SHAPE = (2, 2, 2, 2, 8, 4)
IMG_ORDER = ("y", "zh", "zl", "xh", "xl", "c")
TXT_ORDER = ("zl", "xh", "xl", "c", "y", "zh")
PEERS = 16
CHUNKS = 4
MIB = 1 << 20


def device_index(x, y, z, c):
    return ((((z % 2) * 4 + x) * 2 + c) * 8 + y) * 4 + z // 2


def exchange_groups():
    text = [
        [device_index(x, y, z, 0) for x in (first, first + 1) for y in range(8)]
        for first in (0, 2)
        for z in range(8)
    ]
    image = [
        [device_index(x, y, z, 1) for x in (first, 3 - first) for z in range(8)]
        for first in (0, 1)
        for y in range(8)
    ]
    return text + image


def exchange(blocks):
    return lax.all_to_all(blocks, NAMES, 0, 0, axis_index_groups=exchange_groups(), tiled=False)


def swap_cores(block):
    return lax.ppermute(block, "c", [(0, 1), (1, 0)])


def unit_rows(embedded):
    values = embedded.astype(jnp.float32)
    inverse = lax.rsqrt(jnp.sum(values * values, axis=1, keepdims=True) + EPS)
    return (values * inverse, inverse)


def project_back(grad, unit, inverse):
    inner = jnp.sum(unit * grad, axis=1, keepdims=True)
    return (grad - unit * inner) * inverse


def spread_kernel(image, text, received, copies):
    speaks_text = lax.axis_index("c") == 0
    own = jnp.where(speaks_text, text[...].astype(jnp.float32), image[...].astype(jnp.float32))
    rows = own.shape[0]
    own = unit_rows(own)[0].astype(jnp.bfloat16)
    other = unit_rows(received[...])[0].astype(jnp.bfloat16)
    for peer in range(PEERS):
        copies[peer, :rows, :] = own
        copies[peer, rows:, :] = other


def global_rows(index, is_text, rows):
    x = lax.axis_index("xh") * 2 + lax.axis_index("xl")
    row = index % rows
    slot = (index // rows) % 2
    peer = index // (2 * rows)
    side, ring = peer // 8, peer % 8
    text = (
        ((lax.axis_index("zl") * 4 + lax.axis_index("xh") * 2 + side) * 2 + slot) * 8 + ring
    ) * 4 + lax.axis_index("zh")
    low = jnp.minimum(x, 3 - x)
    across = low + side * (3 - 2 * low)
    image = ((lax.axis_index("y") * 8 + ring) * 4 + across) * 2 + 1 - slot
    return jnp.where(is_text, text, image) * rows + row


def tile_kernel(rows, scalars, mine, theirs, grad):
    speaks_text = lax.axis_index("c") == 0
    scale, bias = scalars[0], scalars[1]
    total = mine.shape[0]
    part = total // CHUNKS
    there = theirs[...]
    there_ids = global_rows(
        lax.broadcasted_iota(jnp.int32, (1, total), 1), jnp.logical_not(speaks_text), rows
    )
    for start in range(0, total, part):
        here = mine[start : start + part, :]
        scores = lax.dot_general(here, there, (((1,), (1,)), ((), ())), preferred_element_type=jnp.float32)
        here_ids = global_rows(start + lax.broadcasted_iota(jnp.int32, (part, 1), 0), speaks_text, rows)
        match = jnp.where(here_ids == there_ids, 1.0, 0.0)
        weights = (jax.nn.sigmoid(scale * scores + bias) - match).astype(jnp.bfloat16)
        grad[start : start + part, :] = jnp.dot(
            weights, there, preferred_element_type=jnp.float32
        ).astype(jnp.bfloat16)


def sum_kernel(parts, own, other):
    rows = own.shape[0]
    own[...] = jnp.sum(parts[:, :rows, :].astype(jnp.float32), axis=0)
    other[...] = jnp.sum(parts[:, rows:, :].astype(jnp.float32), axis=0)


def finish_kernel(scalars, summed, received, image, text, grad_image, grad_text):
    speaks_text = lax.axis_index("c") == 0
    scale = scalars[0]
    own, other = scale * summed[...], scale * received[...]
    img_unit, img_inv = unit_rows(image[...])
    txt_unit, txt_inv = unit_rows(text[...])
    grad_image[...] = project_back(jnp.where(speaks_text, other, own), img_unit, img_inv)
    grad_text[...] = project_back(jnp.where(speaks_text, own, other), txt_unit, txt_inv)


SMEM = pl.BlockSpec(memory_space=pltpu.SMEM)
VMEM = pl.BlockSpec(memory_space=pltpu.VMEM)


def per_device(image_emb, text_emb, logit_scale, logit_bias):
    rows, width = image_emb.shape
    total = PEERS * 2 * rows
    scalars = jnp.concatenate([logit_scale, logit_bias])

    received = swap_cores(jnp.where(lax.axis_index("c") == 0, image_emb, text_emb))
    copies = pl.pallas_call(
        spread_kernel,
        out_shape=jax.ShapeDtypeStruct((PEERS, 2 * rows, width), jnp.bfloat16),
        in_specs=[VMEM, VMEM, VMEM],
        out_specs=VMEM,
        name="spread",
    )(image_emb, text_emb, received)
    mine = exchange(copies).reshape(total, width)
    theirs = swap_cores(mine)

    grad = pl.pallas_call(
        lambda *refs: tile_kernel(rows, *refs),
        out_shape=jax.ShapeDtypeStruct((total, width), jnp.bfloat16),
        in_specs=[SMEM, VMEM, VMEM],
        out_specs=VMEM,
        compiler_params=pltpu.CompilerParams(vmem_limit_bytes=40 * MIB),
        cost_estimate=pl.CostEstimate(
            flops=4 * total * total * width, bytes_accessed=6 * total * width, transcendentals=total * total
        ),
        name="tile",
    )(scalars, mine, theirs)

    parts = exchange(grad.reshape(PEERS, 2 * rows, width))
    out = jax.ShapeDtypeStruct((rows, width), jnp.float32)
    own, other = pl.pallas_call(
        sum_kernel,
        out_shape=(out, out),
        in_specs=[VMEM],
        out_specs=(VMEM, VMEM),
        name="sum",
    )(parts)
    return pl.pallas_call(
        finish_kernel,
        out_shape=(out, out),
        in_specs=[SMEM, VMEM, VMEM, VMEM, VMEM],
        out_specs=(VMEM, VMEM),
        name="finish",
    )(scalars, own, swap_cores(other), image_emb, text_emb)


def solution(mesh):
    fine = Mesh(mesh.devices.reshape(SHAPE), NAMES)
    return jax.shard_map(
        per_device,
        mesh=fine,
        in_specs=(P(IMG_ORDER, None), P(TXT_ORDER, None), P(), P()),
        out_specs=(P(IMG_ORDER, None), P(TXT_ORDER, None)),
        check_vma=False,
    )
```

time: 117 us -> 113 us (0.966)
  waiting for transfers between devices: 9.94 us -> 5.57 us
  Pallas kernels: 9.29 us -> 13.6 us
  starting transfers between devices: 14.6 us -> 12.6 us
    ppermute x4 -> x3, waiting for transfers between devices: 9.94 us -> 5.57 us  [swap_cores(): return lax.ppermute(block, 'c', [(0, 1), (1, 0)])]
    pallas_call x3 -> x4, Pallas kernels: 9.29 us -> 13.6 us  [the longest x1 6.33 us: per_device(): pl.pallas_call(lambda *refs: tile_kernel(rows, *refs), out_shape=jax.Shap...]
    ppermute x4 -> x3, starting transfers between devices: 14.6 us -> 12.6 us  [swap_cores(): return lax.ppermute(block, 'c', [(0, 1), (1, 0)])]
  transfers between devices with their start and end apart: 4 -> 3, of which waited for: 4 -> 3; matrix products, arithmetic and copies ran while one was open for 0% -> 0% of each run, Pallas kernels for 0% -> 0%
where the time goes in v3:
time: 113 us
  blocking collectives  77 us (68%)
  Pallas kernels  13.6 us (12%)
  starting transfers between devices  12.6 us (11%)
  waiting for transfers between devices  5.57 us (5%)
  between operations  1.97 us (2%)
  local copies, waits for them, and re-layouts  1.29 us (1%)
    all_to_all x2, blocking collectives, exchange(): lax.all_to_all(blocks, NAMES, 0, 0, axis_index_groups=exchange_groups(),...  77 us
    ppermute x3, starting transfers between devices, swap_cores(): return lax.ppermute(block, 'c', [(0, 1), (1, 0)])  12.6 us
    pallas_call x1, Pallas kernels, per_device(): pl.pallas_call(lambda *refs: tile_kernel(rows, *refs), out_shape=jax.Shap...  6.33 us
    ppermute x3, waiting for transfers between devices, swap_cores(): return lax.ppermute(block, 'c', [(0, 1), (1, 0)])  5.57 us
    pallas_call x1, Pallas kernels, per_device(): pl.pallas_call(spread_kernel, out_shape=jax.ShapeDtypeStruct((PEERS, 2 *...  2.65 us
    pallas_call x1, Pallas kernels, per_device(): pl.pallas_call(sum_kernel, out_shape=(out, out), in_specs=[VMEM], out_spe...  2.63 us
  transfers between devices with their start and end apart: 3, of which 3 were waited for; matrix products, arithmetic and copies ran while one was open for 0% of the time, Pallas kernels for 0%

profile of v3, /device:TPU:1, one launch (start us, length us, event | category | flops | bytes accessed | tf_op | source)
XLA Modules:
  0.0 113.0 jit_solution(17436441373003883339)
XLA Ops:
  0.6 0.9 broadcast_select_fusion
  1.5 8.8 %collective-permute-start = (bf16[32,1152]{1,0:T(8,128)(2,1)S(1)}, bf16[32,1152]{1,0:T(8,128)(2,1)S(1)}, u32[]{:S(2)}, u32[]{:S(2)}) collective-permute-start(bf16[32,1152]{1,0:T(8,128)(2,1)S(1)} %broadcast_select_fusion), channel_id=1, source_target_pairs={{0,32},{32,0},{1,33},{33,1},{2,34},{34,2},{3,35},{35,3},{4,36},{36... | collective-permute-start | bytes 221192 | tf_op jit(solution)/shard_map/ppermute | solution.py:41
  10.3 0.9 collective-permute-done.received
  11.2 0.0 copy-start.2
  11.2 0.6 copy-done.2
  11.9 2.6 %spread.1 = bf16[16,64,1152]{2,1,0:T(8,128)(2,1)} custom-call(bf16[32,1152]{1,0:T(8,128)(2,1)} %image.3, bf16[32,1152]{1,0:T(8,128)(2,1)} %text.3, bf16[32,1152]{1,0:T(8,128)(2,1)} %copy-done.2), custom_call_target="tpu_custom_call" | custom-call | tf_op jit(solution)/shard_map/spread/pallas_call | solution.py:127
  14.5 38.1 %all_to_all.10 = bf16[16,64,1152]{2,1,0:T(8,128)(2,1)S(1)} all-to-all(bf16[16,64,1152]{2,1,0:T(8,128)(2,1)} %spread.1), channel_id=1, replica_groups={{0,4,8,12,16,20,24,28,64,68,72,76,80,84,88,92},{256,260,264,268,272,276..., dimensions={0} | all-to-all | bytes 4718592 | tf_op jit(solution)/shard_map/all_to_all | solution.py:37
  52.6 1.9 %collective-permute-start.1 = (bf16[1024,1152]{1,0:T(8,128)(2,1)S(1)}, bf16[1024,1152]{1,0:T(8,128)(2,1)S(1)}, u32[]{:S(2)}, u32[]{:S(2)}) collective-permute-start(bf16[1024,1152]{1,0:T(8,128)(2,1)S(1)} %bitcast.2), channel_id=1, source_target_pairs={{0,32},{32,0},{1,33},{33,1},{2,34},{34,2},{3,35},{35,3},{4,36},{36... | collective-permute-start | bytes 7077896 | tf_op jit(solution)/shard_map/ppermute | solution.py:41
  55.8 0.1 pad_maximum_fusion.refs_0_.scalars
  55.9 0.0 copy-start
  55.9 3.1 %collective-permute-done.1.refs_2_ = bf16[1024,1152]{1,0:T(8,128)(2,1)S(1)} collective-permute-done((bf16[1024,1152]{1,0:T(8,128)(2,1)S(1)}, bf16[1024,1152]{1,0:T(8,128)(2,1)S(1)}, u32[]{:S(2)}, u32[]{:S(2)}) %collective-permute-start.1) | collective-permute-done | bytes 2359328 | tf_op jit(solution)/shard_map/ppermute | solution.py:41
  59.1 6.3 %tile.1 = bf16[1024,1152]{1,0:T(8,128)(2,1)S(1)} custom-call(f32[2]{0:T(128)S(1)} %pad_maximum_fusion.refs_0_.scalars, bf16[1024,1152]{1,0:T(8,128)(2,1)S(1)} %bitcast.3, bf16[1024,1152]{1,0:T(8,128)(2,1)S(1)} %collective-permute-done.1.refs_2_), custom_call_target="tpu_custom_call" | custom-call | flops 4831838208 | bytes 7077888 | tf_op jit(solution)/shard_map/tile/pallas_call | solution.py:137
  65.4 0.0 copy-done
  65.4 38.9 %all_to_all.11.parts = bf16[16,64,1152]{2,1,0:T(8,128)(2,1)} all-to-all(bf16[16,64,1152]{2,1,0:T(8,128)(2,1)S(1)} %bitcast.4), channel_id=1, replica_groups={{0,4,8,12,16,20,24,28,64,68,72,76,80,84,88,92},{256,260,264,268,272,276..., dimensions={0} | all-to-all | bytes 4718592 | tf_op jit(solution)/shard_map/all_to_all | solution.py:37
  104.3 2.6 %sum.1 = (f32[32,1152]{1,0:T(8,128)}, f32[32,1152]{1,0:T(8,128)}) custom-call(bf16[16,64,1152]{2,1,0:T(8,128)(2,1)} %all_to_all.11.parts), custom_call_target="tpu_custom_call" | custom-call | tf_op jit(solution)/shard_map/sum/pallas_call | solution.py:151
  106.9 1.9 %collective-permute-start.2 = (f32[32,1152]{1,0:T(8,128)}, f32[32,1152]{1,0:T(8,128)S(1)}, u32[]{:S(2)}, u32[]{:S(2)}) collective-permute-start(f32[32,1152]{1,0:T(8,128)} %get-tuple-element.5), channel_id=1, source_target_pairs={{0,32},{32,0},{1,33},{33,1},{2,34},{34,2},{3,35},{35,3},{4,36},{36... | collective-permute-start | bytes 442376 | tf_op jit(solution)/shard_map/ppermute | solution.py:41
  108.9 1.5 %collective-permute-done.2.received = f32[32,1152]{1,0:T(8,128)S(1)} collective-permute-done((f32[32,1152]{1,0:T(8,128)}, f32[32,1152]{1,0:T(8,128)S(1)}, u32[]{:S(2)}, u32[]{:S(2)}) %collective-permute-start.2) | collective-permute-done | bytes 147488 | tf_op jit(solution)/shard_map/ppermute | solution.py:41
  110.4 0.0 copy-start.1
  110.4 0.7 copy-done.1
  111.1 2.0 %finish.1 = (f32[32,1152]{1,0:T(8,128)}, f32[32,1152]{1,0:T(8,128)}) custom-call(f32[2]{0:T(128)} %copy-done, f32[32,1152]{1,0:T(8,128)} %get-tuple-element.4.summed, f32[32,1152]{1,0:T(8,128)} %copy-done.1, bf16[32,1152]{1,0:T(8,128)(2,1)} %image.3, bf16[32,1152]{1,0:T(8,128)(2,1)} %text.3), custom_call_target="tpu_custom_call" | custom-call | tf_op jit(solution)/shard_map/finish/pallas_call | solution.py:158
Async XLA Ops:
  1.5 9.7 %collective-permute-start = (bf16[32,1152]{1,0:T(8,128)(2,1)S(1)}, bf16[32,1152]{1,0:T(8,128)(2,1)S(1)}, u32[]{:S(2)}, u32[]{:S(2)}) collective-permute-start(bf16[32,1152]{1,0:T(8,128)(2,1)S(1)} %broadcast_select_fusion), channel_id=1, source_target_pairs={{0,32},{32,0},{1,33},{33,1},{2,34},{34,2},{3,35},{35,3},{4,36},{36... | collective-permute-start | bytes 221192 | tf_op jit(solution)/shard_map/ppermute | solution.py:41
  11.2 0.6 copy-start.2
  52.6 6.4 %collective-permute-start.1 = (bf16[1024,1152]{1,0:T(8,128)(2,1)S(1)}, bf16[1024,1152]{1,0:T(8,128)(2,1)S(1)}, u32[]{:S(2)}, u32[]{:S(2)}) collective-permute-start(bf16[1024,1152]{1,0:T(8,128)(2,1)S(1)} %bitcast.2), channel_id=1, source_target_pairs={{0,32},{32,0},{1,33},{33,1},{2,34},{34,2},{3,35},{35,3},{4,36},{36... | collective-permute-start | bytes 7077896 | tf_op jit(solution)/shard_map/ppermute | solution.py:41
  55.9 9.5 %copy-start = (f32[2]{0:T(128)}, f32[2]{0:T(128)S(1)}, u32[]{:S(2)}) copy-start(f32[2]{0:T(128)S(1)} %pad_maximum_fusion.refs_0_.scalars) | copy-start | bytes 28
  106.9 3.5 %collective-permute-start.2 = (f32[32,1152]{1,0:T(8,128)}, f32[32,1152]{1,0:T(8,128)S(1)}, u32[]{:S(2)}, u32[]{:S(2)}) collective-permute-start(f32[32,1152]{1,0:T(8,128)} %get-tuple-element.5), channel_id=1, source_target_pairs={{0,32},{32,0},{1,33},{33,1},{2,34},{34,2},{3,35},{35,3},{4,36},{36... | collective-permute-start | bytes 442376 | tf_op jit(solution)/shard_map/ppermute | solution.py:41
  110.4 0.7 copy-start.1

commit v4 on v3

--- a/solution.py
+++ b/solution.py
@@ -116,6 +116,7 @@
 
 SMEM = pl.BlockSpec(memory_space=pltpu.SMEM)
 VMEM = pl.BlockSpec(memory_space=pltpu.VMEM)
+SMALL = pltpu.CompilerParams(vmem_limit_bytes=8 * MIB)
 
 
 def per_device(image_emb, text_emb, logit_scale, logit_bias):
@@ -129,6 +130,7 @@
         out_shape=jax.ShapeDtypeStruct((PEERS, 2 * rows, width), jnp.bfloat16),
         in_specs=[VMEM, VMEM, VMEM],
         out_specs=VMEM,
+        compiler_params=SMALL,
         name="spread",
     )(image_emb, text_emb, received)
     mine = exchange(copies).reshape(total, width)
@@ -153,6 +155,7 @@
         out_shape=(out, out),
         in_specs=[VMEM],
         out_specs=(VMEM, VMEM),
+        compiler_params=SMALL,
         name="sum",
     )(parts)
     return pl.pallas_call(
@@ -160,6 +163,7 @@
         out_shape=(out, out),
         in_specs=[SMEM, VMEM, VMEM, VMEM, VMEM],
         out_specs=(VMEM, VMEM),
+        compiler_params=SMALL,
         name="finish",
     )(scalars, own, swap_cores(other), image_emb, text_emb)
 

time: 113 us -> 108 us (0.956)
  Pallas kernels: 13.6 us -> 8.43 us
    pallas_call x1, Pallas kernels: 2.65 us -> 0.28 us  [per_device(): pl.pallas_call(spread_kernel, out_shape=jax.ShapeDtypeStruct((PEERS, 2 *...]
    pallas_call x1, Pallas kernels: 2.63 us -> 0.3 us  [per_device(): pl.pallas_call(sum_kernel, out_shape=(out, out), in_specs=[VMEM], out_spe...]
where the time goes in v4:
time: 108 us
  blocking collectives  76.7 us (71%)
  starting transfers between devices  12.6 us (12%)
  Pallas kernels  8.43 us (8%)
  waiting for transfers between devices  5.36 us (5%)
  between operations  1.98 us (2%)
  local copies, waits for them, and re-layouts  1.77 us (2%)
    all_to_all x2, blocking collectives, exchange(): lax.all_to_all(blocks, NAMES, 0, 0, axis_index_groups=exchange_groups(),...  76.7 us
    ppermute x3, starting transfers between devices, swap_cores(): return lax.ppermute(block, 'c', [(0, 1), (1, 0)])  12.6 us
    pallas_call x1, Pallas kernels, per_device(): pl.pallas_call(lambda *refs: tile_kernel(rows, *refs), out_shape=jax.Shap...  6.4 us
    ppermute x3, waiting for transfers between devices, swap_cores(): return lax.ppermute(block, 'c', [(0, 1), (1, 0)])  5.36 us
  transfers between devices with their start and end apart: 3, of which 3 were waited for; matrix products, arithmetic and copies ran while one was open for 0% of the time, Pallas kernels for 0%

profile of v4, /device:TPU:1, one launch (start us, length us, event | category | flops | bytes accessed | tf_op | source)
XLA Modules:
  0.0 107.9 jit_solution(10609640785651134341)
XLA Ops:
  0.6 0.9 broadcast_select_fusion
  1.5 8.8 %collective-permute-start = (bf16[32,1152]{1,0:T(8,128)(2,1)S(1)}, bf16[32,1152]{1,0:T(8,128)(2,1)S(1)}, u32[]{:S(2)}, u32[]{:S(2)}) collective-permute-start(bf16[32,1152]{1,0:T(8,128)(2,1)S(1)} %broadcast_select_fusion), channel_id=1, source_target_pairs={{0,32},{32,0},{1,33},{33,1},{2,34},{34,2},{3,35},{35,3},{4,36},{36... | collective-permute-start | bytes 221192 | tf_op jit(solution)/shard_map/ppermute | solution.py:41
  10.3 0.9 collective-permute-done.received
  11.2 0.0 copy-start
  11.2 0.9 copy-done
  12.1 0.0 copy-start.2
  12.1 0.9 copy-done.2
  13.0 0.3 spread.1
  13.3 37.9 %all_to_all.10 = bf16[16,64,1152]{2,1,0:T(8,128)(2,1)S(1)} all-to-all(bf16[16,64,1152]{2,1,0:T(8,128)(2,1)S(1)} %spread.1), channel_id=1, replica_groups={{0,4,8,12,16,20,24,28,64,68,72,76,80,84,88,92},{256,260,264,268,272,276..., dimensions={0} | all-to-all | bytes 4718592 | tf_op jit(solution)/shard_map/all_to_all | solution.py:37
  51.2 1.9 %collective-permute-start.1 = (bf16[1024,1152]{1,0:T(8,128)(2,1)S(1)}, bf16[1024,1152]{1,0:T(8,128)(2,1)S(1)}, u32[]{:S(2)}, u32[]{:S(2)}) collective-permute-start(bf16[1024,1152]{1,0:T(8,128)(2,1)S(1)} %bitcast.2), channel_id=1, source_target_pairs={{0,32},{32,0},{1,33},{33,1},{2,34},{34,2},{3,35},{35,3},{4,36},{36... | collective-permute-start | bytes 7077896 | tf_op jit(solution)/shard_map/ppermute | solution.py:41
  54.4 0.1 pad_maximum_fusion.refs_0_.scalars
  54.5 3.1 %collective-permute-done.1.refs_2_ = bf16[1024,1152]{1,0:T(8,128)(2,1)S(1)} collective-permute-done((bf16[1024,1152]{1,0:T(8,128)(2,1)S(1)}, bf16[1024,1152]{1,0:T(8,128)(2,1)S(1)}, u32[]{:S(2)}, u32[]{:S(2)}) %collective-permute-start.1) | collective-permute-done | bytes 2359328 | tf_op jit(solution)/shard_map/ppermute | solution.py:41
  57.6 6.4 %tile.1 = bf16[1024,1152]{1,0:T(8,128)(2,1)S(1)} custom-call(f32[2]{0:T(128)S(1)} %pad_maximum_fusion.refs_0_.scalars, bf16[1024,1152]{1,0:T(8,128)(2,1)S(1)} %bitcast.3, bf16[1024,1152]{1,0:T(8,128)(2,1)S(1)} %collective-permute-done.1.refs_2_), custom_call_target="tpu_custom_call" | custom-call | flops 4831838208 | bytes 7077888 | tf_op jit(solution)/shard_map/tile/pallas_call | solution.py:139
  64.0 38.8 %all_to_all.11.parts = bf16[16,64,1152]{2,1,0:T(8,128)(2,1)S(1)} all-to-all(bf16[16,64,1152]{2,1,0:T(8,128)(2,1)S(1)} %bitcast.4), channel_id=1, replica_groups={{0,4,8,12,16,20,24,28,64,68,72,76,80,84,88,92},{256,260,264,268,272,276..., dimensions={0} | all-to-all | bytes 4718592 | tf_op jit(solution)/shard_map/all_to_all | solution.py:37
  102.9 0.0 copy-start.1
  102.9 0.0 copy-start.3
  102.9 0.3 sum.1
  103.2 1.9 %collective-permute-start.2 = (f32[32,1152]{1,0:T(8,128)S(1)}, f32[32,1152]{1,0:T(8,128)S(1)}, u32[]{:S(2)}, u32[]{:S(2)}) collective-permute-start(f32[32,1152]{1,0:T(8,128)S(1)} %get-tuple-element.5), channel_id=1, source_target_pairs={{0,32},{32,0},{1,33},{33,1},{2,34},{34,2},{3,35},{35,3},{4,36},{36... | collective-permute-start | bytes 442376 | tf_op jit(solution)/shard_map/ppermute | solution.py:41
  105.1 1.3 %collective-permute-done.2.received = f32[32,1152]{1,0:T(8,128)S(1)} collective-permute-done((f32[32,1152]{1,0:T(8,128)S(1)}, f32[32,1152]{1,0:T(8,128)S(1)}, u32[]{:S(2)}, u32[]{:S(2)}) %collective-permute-start.2) | collective-permute-done | bytes 147488 | tf_op jit(solution)/shard_map/ppermute | solution.py:41
  106.4 0.0 copy-done.1
  106.4 0.0 copy-done.3
  106.4 1.5 %finish.1 = (f32[32,1152]{1,0:T(8,128)}, f32[32,1152]{1,0:T(8,128)}) custom-call(f32[2]{0:T(128)S(1)} %pad_maximum_fusion.refs_0_.scalars, f32[32,1152]{1,0:T(8,128)S(1)} %get-tuple-element.4.summed, f32[32,1152]{1,0:T(8,128)S(1)} %collective-permute-done.2.received, bf16[32,1152]{1,0:T(8,128)(2,1)S(1)} %copy-done.1, bf16[32,1152]{1,0:T(8,128)(2,1)S(1)} %copy-done.3), custom_call_target="tpu_custom_call" | custom-call | tf_op jit(solution)/shard_map/finish/pallas_call | solution.py:161
Async XLA Ops:
  1.5 9.7 %collective-permute-start = (bf16[32,1152]{1,0:T(8,128)(2,1)S(1)}, bf16[32,1152]{1,0:T(8,128)(2,1)S(1)}, u32[]{:S(2)}, u32[]{:S(2)}) collective-permute-start(bf16[32,1152]{1,0:T(8,128)(2,1)S(1)} %broadcast_select_fusion), channel_id=1, source_target_pairs={{0,32},{32,0},{1,33},{33,1},{2,34},{34,2},{3,35},{35,3},{4,36},{36... | collective-permute-start | bytes 221192 | tf_op jit(solution)/shard_map/ppermute | solution.py:41
  11.2 0.9 copy-start
  12.1 0.9 copy-start.2
  51.2 6.4 %collective-permute-start.1 = (bf16[1024,1152]{1,0:T(8,128)(2,1)S(1)}, bf16[1024,1152]{1,0:T(8,128)(2,1)S(1)}, u32[]{:S(2)}, u32[]{:S(2)}) collective-permute-start(bf16[1024,1152]{1,0:T(8,128)(2,1)S(1)} %bitcast.2), channel_id=1, source_target_pairs={{0,32},{32,0},{1,33},{33,1},{2,34},{34,2},{3,35},{35,3},{4,36},{36... | collective-permute-start | bytes 7077896 | tf_op jit(solution)/shard_map/ppermute | solution.py:41
  102.9 3.6 %copy-start.1 = (bf16[32,1152]{1,0:T(8,128)(2,1)S(1)}, bf16[32,1152]{1,0:T(8,128)(2,1)}, u32[]{:S(2)}) copy-start(bf16[32,1152]{1,0:T(8,128)(2,1)} %image.3) | copy-start | bytes 221188
  102.9 3.6 %copy-start.3 = (bf16[32,1152]{1,0:T(8,128)(2,1)S(1)}, bf16[32,1152]{1,0:T(8,128)(2,1)}, u32[]{:S(2)}) copy-start(bf16[32,1152]{1,0:T(8,128)(2,1)} %text.3) | copy-start | bytes 221188
  103.2 3.3 %collective-permute-start.2 = (f32[32,1152]{1,0:T(8,128)S(1)}, f32[32,1152]{1,0:T(8,128)S(1)}, u32[]{:S(2)}, u32[]{:S(2)}) collective-permute-start(f32[32,1152]{1,0:T(8,128)S(1)} %get-tuple-element.5), channel_id=1, source_target_pairs={{0,32},{32,0},{1,33},{33,1},{2,34},{34,2},{3,35},{35,3},{4,36},{36... | collective-permute-start | bytes 442376 | tf_op jit(solution)/shard_map/ppermute | solution.py:41

commit v5 on v4

v5 whole, which is shorter than its diff:
```python
import jax
import jax.numpy as jnp
from jax import lax
from jax.experimental import pallas as pl
from jax.experimental.pallas import tpu as pltpu
from jax.sharding import Mesh, PartitionSpec as P

EPS = 1e-06
NAMES = ("zl", "xh", "xl", "c", "y", "zh")
SHAPE = (2, 2, 2, 2, 8, 4)
IMG_ORDER = ("y", "zh", "zl", "xh", "xl", "c")
TXT_ORDER = ("zl", "xh", "xl", "c", "y", "zh")
RING = 8
COLORS = 4
MIB = 1 << 20


def device_index(x, y, z, c):
    return ((((z % 2) * 4 + x) * 2 + c) * 8 + y) * 4 + z // 2


def speaker(kind, line, pair, ring, side):
    if kind == 0:
        return device_index(2 * pair + side, ring % RING, line, 0)
    return device_index(3 - pair if side else pair, line, ring % RING, 1)


def lines():
    return [(kind, line, pair) for kind in (0, 1) for line in range(RING) for pair in (0, 1)]


def color_groups():
    return [
        [speaker(*line, color + ring, side) for ring, side in ((0, 0), (4, 0), (2, 1), (6, 1))]
        for line in lines()
        for color in range(COLORS)
    ]


def links(step, flip):
    return [
        (speaker(*line, ring + step, side ^ flip), speaker(*line, ring, side))
        for line in lines()
        for ring in range(RING)
        for side in (0, 1)
    ]


NEIGHBOURS = ((1, 0), (-1, 0), (0, 1))


def exchange(blocks):
    return lax.all_to_all(blocks, NAMES, 0, 0, axis_index_groups=color_groups(), tiled=False)


def take(block, neighbour):
    return lax.ppermute(block, NAMES, links(*neighbour))


def give(block, neighbour):
    return lax.ppermute(block, NAMES, [(here, there) for there, here in links(*neighbour)])


def swap_cores(block):
    return lax.ppermute(block, "c", [(0, 1), (1, 0)])


def unit_rows(embedded):
    values = embedded.astype(jnp.float32)
    inverse = lax.rsqrt(jnp.sum(values * values, axis=1, keepdims=True) + EPS)
    return (values * inverse, inverse)


def project_back(grad, unit, inverse):
    inner = jnp.sum(unit * grad, axis=1, keepdims=True)
    return (grad - unit * inner) * inverse


def spread_kernel(own, received, copies):
    rows = own.shape[0]
    first = unit_rows(own[...])[0].astype(jnp.bfloat16)
    second = unit_rows(received[...])[0].astype(jnp.bfloat16)
    for peer in range(COLORS):
        copies[peer, :rows, :] = first
        copies[peer, rows:, :] = second


def global_rows(index, is_text, rows):
    x = lax.axis_index("xh") * 2 + lax.axis_index("xl")
    z = lax.axis_index("zh") * 2 + lax.axis_index("zl")
    row = index % rows
    slot = (index // rows) % 2
    member = (index // (2 * rows)) % COLORS
    chunk = index // (2 * rows * COLORS)
    side = member // 2
    shift = chunk ^ (chunk // 2)
    place = jnp.where(
        is_text, lax.axis_index("y") + 2 * lax.axis_index("xl"), z + 2 * lax.axis_index("xh")
    )
    ring = ((place + shift) % COLORS + 4 * (member % 2) + 2 * side) % RING
    text = (
        ((lax.axis_index("zl") * 4 + lax.axis_index("xh") * 2 + side) * 2 + slot) * 8 + ring
    ) * 4 + lax.axis_index("zh")
    low = jnp.minimum(x, 3 - x)
    across = low + side * (3 - 2 * low)
    image = ((lax.axis_index("y") * 8 + ring) * 4 + across) * 2 + 1 - slot
    return jnp.where(is_text, text, image) * rows + row


def tile_kernel(rows, chunk, scalars, mine, theirs, grad):
    speaks_text = lax.axis_index("c") == 0
    scale, bias = scalars[0], scalars[1]
    part, total = mine.shape[0], theirs.shape[0]
    there = theirs[...]
    there_ids = global_rows(
        lax.broadcasted_iota(jnp.int32, (1, total), 1), jnp.logical_not(speaks_text), rows
    )
    here_ids = global_rows(chunk * part + lax.broadcasted_iota(jnp.int32, (part, 1), 0), speaks_text, rows)
    scores = lax.dot_general(mine[...], there, (((1,), (1,)), ((), ())), preferred_element_type=jnp.float32)
    match = jnp.where(here_ids == there_ids, 1.0, 0.0)
    weights = (jax.nn.sigmoid(scale * scores + bias) - match).astype(jnp.bfloat16)
    grad[...] = jnp.dot(weights, there, preferred_element_type=jnp.float32).astype(grad.dtype)


def sum_kernel(parts, own, other):
    rows = own.shape[0]
    own[...] = jnp.sum(parts[:, :rows, :].astype(jnp.float32), axis=0)
    other[...] = jnp.sum(parts[:, rows:, :].astype(jnp.float32), axis=0)


def finish_kernel(scalars, summed, received, image, text, grad_image, grad_text):
    speaks_text = lax.axis_index("c") == 0
    scale = scalars[0]
    own, other = scale * summed[...], scale * received[...]
    img_unit, img_inv = unit_rows(image[...])
    txt_unit, txt_inv = unit_rows(text[...])
    grad_image[...] = project_back(jnp.where(speaks_text, other, own), img_unit, img_inv)
    grad_text[...] = project_back(jnp.where(speaks_text, own, other), txt_unit, txt_inv)


SMEM = pl.BlockSpec(memory_space=pltpu.SMEM)
VMEM = pl.BlockSpec(memory_space=pltpu.VMEM)
SMALL = pltpu.CompilerParams(vmem_limit_bytes=8 * MIB)
LARGE = pltpu.CompilerParams(vmem_limit_bytes=24 * MIB)


def per_device(image_emb, text_emb, logit_scale, logit_bias):
    rows, width = image_emb.shape
    part = COLORS * 2 * rows
    total = COLORS * part
    scalars = jnp.concatenate([logit_scale, logit_bias])

    speaks_text = lax.axis_index("c") == 0
    kept = jnp.where(speaks_text, text_emb, image_emb)
    received = swap_cores(jnp.where(speaks_text, image_emb, text_emb))
    copies = pl.pallas_call(
        spread_kernel,
        out_shape=jax.ShapeDtypeStruct((COLORS, 2 * rows, width), jnp.bfloat16),
        in_specs=[VMEM, VMEM],
        out_specs=VMEM,
        compiler_params=SMALL,
        name="spread",
    )(kept, received)
    own = exchange(copies).reshape(part, width)
    mine = [own] + [take(own, neighbour) for neighbour in NEIGHBOURS]
    theirs = jnp.concatenate([swap_cores(chunk) for chunk in mine], axis=0)

    def tile(chunk, dtype):
        return pl.pallas_call(
            lambda *refs: tile_kernel(rows, chunk, *refs),
            out_shape=jax.ShapeDtypeStruct((part, width), dtype),
            in_specs=[SMEM, VMEM, VMEM],
            out_specs=VMEM,
            compiler_params=LARGE,
            cost_estimate=pl.CostEstimate(
                flops=4 * part * total * width,
                bytes_accessed=2 * (total + 2 * part) * width,
                transcendentals=part * total,
            ),
            name="tile",
        )(scalars, mine[chunk], theirs)

    partial = [give(tile(1 + k, jnp.bfloat16), neighbour) for k, neighbour in enumerate(NEIGHBOURS)]
    summed = tile(0, jnp.float32)
    for block in partial:
        summed = summed + block.astype(jnp.float32)
    parts = exchange(summed.astype(jnp.bfloat16).reshape(COLORS, 2 * rows, width))
    out = jax.ShapeDtypeStruct((rows, width), jnp.float32)
    own, other = pl.pallas_call(
        sum_kernel,
        out_shape=(out, out),
        in_specs=[VMEM],
        out_specs=(VMEM, VMEM),
        compiler_params=SMALL,
        name="sum",
    )(parts)
    return pl.pallas_call(
        finish_kernel,
        out_shape=(out, out),
        in_specs=[SMEM, VMEM, VMEM, VMEM, VMEM],
        out_specs=(VMEM, VMEM),
        compiler_params=SMALL,
        name="finish",
    )(scalars, own, swap_cores(other), image_emb, text_emb)


def solution(mesh):
    fine = Mesh(mesh.devices.reshape(SHAPE), NAMES)
    return jax.shard_map(
        per_device,
        mesh=fine,
        in_specs=(P(IMG_ORDER, None), P(TXT_ORDER, None), P(), P()),
        out_specs=(P(IMG_ORDER, None), P(TXT_ORDER, None)),
        check_vma=False,
    )
```

time: 108 us -> 103 us (0.954)
  blocking collectives: 76.7 us -> 37 us
  starting transfers between devices: 12.6 us -> 39.3 us
  waiting for transfers between devices: 5.36 us -> 10.5 us
  Pallas kernels: 8.43 us -> 11.6 us
  local copies, waits for them, and re-layouts: 1.77 us -> 0.27 us
    all_to_all x2, blocking collectives: 76.7 us -> 37 us  [exchange(): lax.all_to_all(blocks, NAMES, 0, 0, axis_index_groups=color_groups(), til...]
    ppermute x0 -> x6, starting transfers between devices: none -> 20.3 us  [the longest x3 12.7 us: give(): lax.ppermute(block, NAMES, [(here, there) for there, here in links(*neigh...]
    ppermute x0 -> x6, waiting for transfers between devices: none -> 6.62 us  [the longest x3 4.77 us: give(): lax.ppermute(block, NAMES, [(here, there) for there, here in links(*neigh...]
    ppermute x3 -> x6, starting transfers between devices: 12.6 us -> 19 us  [swap_cores(): return lax.ppermute(block, 'c', [(0, 1), (1, 0)])]
    pallas_call x2 -> x5, Pallas kernels: 6.67 us -> 10.1 us  [the longest x4 9.96 us: tile(): pl.pallas_call(lambda *refs: tile_kernel(rows, chunk, *refs), out_shape=j...]
    unnamed x8 -> x7, local copies, waits for them, and re-layouts: 1.77 us -> 0.2 us
    ppermute x3 -> x6, waiting for transfers between devices: 5.36 us -> 3.85 us  [swap_cores(): return lax.ppermute(block, 'c', [(0, 1), (1, 0)])]
  transfers between devices with their start and end apart: 3 -> 12, of which waited for: 3 -> 6; matrix products, arithmetic and copies ran while one was open for 0% -> 0% of each run, Pallas kernels for 0% -> 7%
where the time goes in v5:
time: 103 us; the launch traced here: 102 us
  starting transfers between devices  39.3 us (38%)
  blocking collectives  37 us (36%)
  Pallas kernels  11.6 us (11%)
  waiting for transfers between devices  10.5 us (10%)
  between operations  2.15 us (2%)
  other arithmetic  1.28 us (1%)
    all_to_all x2, blocking collectives, exchange(): lax.all_to_all(blocks, NAMES, 0, 0, axis_index_groups=color_groups(), til...  37 us
    ppermute x6, starting transfers between devices, swap_cores(): return lax.ppermute(block, 'c', [(0, 1), (1, 0)])  19 us
    ppermute x3, starting transfers between devices, give(): lax.ppermute(block, NAMES, [(here, there) for there, here in links(*neigh...  12.7 us
    pallas_call x4, Pallas kernels, tile(): pl.pallas_call(lambda *refs: tile_kernel(rows, chunk, *refs), out_shape=j...  9.96 us
    ppermute x3, starting transfers between devices, take(): return lax.ppermute(block, NAMES, links(*neighbour))  7.61 us
    ppermute x3, waiting for transfers between devices, give(): lax.ppermute(block, NAMES, [(here, there) for there, here in links(*neigh...  4.77 us
    ppermute x6, waiting for transfers between devices, swap_cores(): return lax.ppermute(block, 'c', [(0, 1), (1, 0)])  3.85 us
  transfers between devices with their start and end apart: 12, of which 6 were waited for; matrix products, arithmetic and copies ran while one was open for 0% of the time, Pallas kernels for 7%

profile of v5, /device:TPU:1, one launch (start us, length us, event | category | flops | bytes accessed | tf_op | source)
XLA Modules:
  0.0 102.1 jit_solution(16097839304165832535)
XLA Ops:
  0.6 0.9 broadcast_select_fusion
  1.6 8.8 %collective-permute-start = (bf16[32,1152]{1,0:T(8,128)(2,1)S(1)}, bf16[32,1152]{1,0:T(8,128)(2,1)S(1)}, u32[]{:S(2)}, u32[]{:S(2)}) collective-permute-start(bf16[32,1152]{1,0:T(8,128)(2,1)S(1)} %get-tuple-element.6), channel_id=1, source_target_pairs={{0,32},{32,0},{1,33},{33,1},{2,34},{34,2},{3,35},{35,3},{4,36},{36... | collective-permute-start | bytes 221192 | tf_op jit(solution)/shard_map/ppermute | solution.py:65
  10.4 0.9 collective-permute-done.received
  11.3 0.1 spread.1
  11.4 19.6 %all_to_all.10 = bf16[4,64,1152]{2,1,0:T(8,128)(2,1)S(1)} all-to-all(bf16[4,64,1152]{2,1,0:T(8,128)(2,1)S(1)} %spread.1), channel_id=1, replica_groups={{0,16,72,88},{4,20,76,92},{8,24,80,64},{12,28,84,68},{128,144,200,216},..., dimensions={0} | all-to-all | bytes 1179648 | tf_op jit(solution)/shard_map/all_to_all | solution.py:53
  31.0 2.1 %collective-permute-start.2 = (bf16[256,1152]{1,0:T(8,128)(2,1)S(1)}, bf16[256,1152]{1,0:T(8,128)(2,1)S(1)}, u32[]{:S(2)}, u32[]{:S(2)}) collective-permute-start(bf16[256,1152]{1,0:T(8,128)(2,1)S(1)} %bitcast.2), channel_id=1, source_target_pairs={{4,0},{68,64},{8,4},{72,68},{12,8},{76,72},{16,12},{80,76},{20,16}... | collective-permute-start | bytes 1769480 | tf_op jit(solution)/shard_map/ppermute | solution.py:57
  33.1 3.2 %collective-permute-start.4 = (bf16[256,1152]{1,0:T(8,128)(2,1)S(1)}, bf16[256,1152]{1,0:T(8,128)(2,1)S(1)}, u32[]{:S(2)}, u32[]{:S(2)}) collective-permute-start(bf16[256,1152]{1,0:T(8,128)(2,1)S(1)} %bitcast.3), channel_id=1, source_target_pairs={{28,0},{92,64},{0,4},{64,68},{4,8},{68,72},{8,12},{72,76},{12,16},... | collective-permute-start | bytes 1769480 | tf_op jit(solution)/shard_map/ppermute | solution.py:57
  36.3 2.3 %collective-permute-start.6 = (bf16[256,1152]{1,0:T(8,128)(2,1)S(1)}, bf16[256,1152]{1,0:T(8,128)(2,1)S(1)}, u32[]{:S(2)}, u32[]{:S(2)}) collective-permute-start(bf16[256,1152]{1,0:T(8,128)(2,1)S(1)} %bitcast.4), channel_id=1, source_target_pairs={{64,0},{0,64},{68,4},{4,68},{72,8},{8,72},{76,12},{12,76},{80,16},... | collective-permute-start | bytes 1769480 | tf_op jit(solution)/shard_map/ppermute | solution.py:57
  38.6 1.9 %collective-permute-start.1 = (bf16[256,1152]{1,0:T(8,128)(2,1)S(1)}, bf16[256,1152]{1,0:T(8,128)(2,1)S(1)}, u32[]{:S(2)}, u32[]{:S(2)}) collective-permute-start(bf16[256,1152]{1,0:T(8,128)(2,1)S(1)} %bitcast.5), channel_id=1, source_target_pairs={{0,32},{32,0},{1,33},{33,1},{2,34},{34,2},{3,35},{35,3},{4,36},{36... | collective-permute-start | bytes 1769480 | tf_op jit(solution)/shard_map/ppermute | solution.py:65
  40.6 1.4 %collective-permute-done.2.refs_1_ = bf16[256,1152]{1,0:T(8,128)(2,1)S(1)} collective-permute-done((bf16[256,1152]{1,0:T(8,128)(2,1)S(1)}, bf16[256,1152]{1,0:T(8,128)(2,1)S(1)}, u32[]{:S(2)}, u32[]{:S(2)}) %collective-permute-start.2) | collective-permute-done | bytes 589856 | tf_op jit(solution)/shard_map/ppermute | solution.py:57
  41.9 1.9 %collective-permute-start.3 = (bf16[256,1152]{1,0:T(8,128)(2,1)S(1)}, bf16[256,1152]{1,0:T(8,128)(2,1)S(1)}, u32[]{:S(2)}, u32[]{:S(2)}) collective-permute-start(bf16[256,1152]{1,0:T(8,128)(2,1)S(1)} %collective-permute-done.2.refs_1_), channel_id=1, source_target_pairs={{0,32},{32,0},{1,33},{33,1},{2,34},{34,2},{3,35},{35,3},{4,36},{36... | collective-permute-start | bytes 1769480 | tf_op jit(solution)/shard_map/ppermute | solution.py:65
  45.1 0.0 collective-permute-done.4.refs_1_
  45.1 2.4 %collective-permute-start.5 = (bf16[256,1152]{1,0:T(8,128)(2,1)S(1)}, bf16[256,1152]{1,0:T(8,128)(2,1)S(1)}, u32[]{:S(2)}, u32[]{:S(2)}) collective-permute-start(bf16[256,1152]{1,0:T(8,128)(2,1)S(1)} %collective-permute-done.4.refs_1_), channel_id=1, source_target_pairs={{0,32},{32,0},{1,33},{33,1},{2,34},{34,2},{3,35},{35,3},{4,36},{36... | collective-permute-start | bytes 1769480 | tf_op jit(solution)/shard_map/ppermute | solution.py:65
  47.6 0.1 pad_maximum_fusion.refs_0_.scalars
  47.6 0.5 collective-permute-done.6.refs_1_
  48.1 1.9 %collective-permute-start.7 = (bf16[256,1152]{1,0:T(8,128)(2,1)S(1)}, bf16[256,1152]{1,0:T(8,128)(2,1)S(1)}, u32[]{:S(2)}, u32[]{:S(2)}) collective-permute-start(bf16[256,1152]{1,0:T(8,128)(2,1)S(1)} %collective-permute-done.6.refs_1_), channel_id=1, source_target_pairs={{0,32},{32,0},{1,33},{33,1},{2,34},{34,2},{3,35},{35,3},{4,36},{36... | collective-permute-start | bytes 1769480 | tf_op jit(solution)/shard_map/ppermute | solution.py:65
  50.1 0.0 collective-permute-done.1
  50.1 0.0 collective-permute-done.3
  50.1 0.1 constant_dynamic-update-slice_fusion.2
  50.2 0.0 collective-permute-done.5
  50.2 0.1 constant_dynamic-update-slice_fusion.1
  50.3 1.7 %collective-permute-done.7 = bf16[256,1152]{1,0:T(8,128)(2,1)S(1)} collective-permute-done((bf16[256,1152]{1,0:T(8,128)(2,1)S(1)}, bf16[256,1152]{1,0:T(8,128)(2,1)S(1)}, u32[]{:S(2)}, u32[]{:S(2)}) %collective-permute-start.7) | collective-permute-done | bytes 589856 | tf_op jit(solution)/shard_map/ppermute | solution.py:65
  52.0 0.1 constant_dynamic-update-slice_fusion.refs_2_
  52.1 2.5 %tile.5 = bf16[256,1152]{1,0:T(8,128)(2,1)S(1)} custom-call(f32[2]{0:T(128)S(1)} %pad_maximum_fusion.refs_0_.scalars, bf16[256,1152]{1,0:T(8,128)(2,1)S(1)} %collective-permute-done.2.refs_1_, bf16[1024,1152]{1,0:T(8,128)(2,1)S(1)} %constant_dynamic-update-slice_fusion.refs_2_), custom_call_target="tpu_custom_call" | custom-call | flops 1207959552 | bytes 3538944 | tf_op jit(solution)/shard_map/tile/pallas_call | solution.py:169
  54.6 2.8 %collective-permute-start.8 = (bf16[256,1152]{1,0:T(8,128)(2,1)S(1)}, bf16[256,1152]{1,0:T(8,128)(2,1)S(1)}, u32[]{:S(2)}, u32[]{:S(2)}) collective-permute-start(bf16[256,1152]{1,0:T(8,128)(2,1)S(1)} %tile.5), channel_id=1, source_target_pairs={{0,4},{64,68},{4,8},{68,72},{8,12},{72,76},{12,16},{76,80},{16,20}... | collective-permute-start | bytes 1769480 | tf_op jit(solution)/shard_map/ppermute | solution.py:61
  57.5 2.5 %tile.6 = bf16[256,1152]{1,0:T(8,128)(2,1)S(1)} custom-call(f32[2]{0:T(128)S(1)} %pad_maximum_fusion.refs_0_.scalars, bf16[256,1152]{1,0:T(8,128)(2,1)S(1)} %collective-permute-done.4.refs_1_, bf16[1024,1152]{1,0:T(8,128)(2,1)S(1)} %constant_dynamic-update-slice_fusion.refs_2_), custom_call_target="tpu_custom_call" | custom-call | flops 1207959552 | bytes 3538944 | tf_op jit(solution)/shard_map/tile/pallas_call | solution.py:169
  60.0 4.9 %collective-permute-start.9 = (bf16[256,1152]{1,0:T(8,128)(2,1)S(1)}, bf16[256,1152]{1,0:T(8,128)(2,1)S(1)}, u32[]{:S(2)}, u32[]{:S(2)}) collective-permute-start(bf16[256,1152]{1,0:T(8,128)(2,1)S(1)} %tile.6), channel_id=1, source_target_pairs={{0,28},{64,92},{4,0},{68,64},{8,4},{72,68},{12,8},{76,72},{16,12},... | collective-permute-start | bytes 1769480 | tf_op jit(solution)/shard_map/ppermute | solution.py:61
  64.9 2.5 %tile.7 = bf16[256,1152]{1,0:T(8,128)(2,1)S(1)} custom-call(f32[2]{0:T(128)S(1)} %pad_maximum_fusion.refs_0_.scalars, bf16[256,1152]{1,0:T(8,128)(2,1)S(1)} %collective-permute-done.6.refs_1_, bf16[1024,1152]{1,0:T(8,128)(2,1)S(1)} %constant_dynamic-update-slice_fusion.refs_2_), custom_call_target="tpu_custom_call" | custom-call | flops 1207959552 | bytes 3538944 | tf_op jit(solution)/shard_map/tile/pallas_call | solution.py:169
  67.4 5.0 %collective-permute-start.10 = (bf16[256,1152]{1,0:T(8,128)(2,1)S(1)}, bf16[256,1152]{1,0:T(8,128)(2,1)S(1)}, u32[]{:S(2)}, u32[]{:S(2)}) collective-permute-start(bf16[256,1152]{1,0:T(8,128)(2,1)S(1)} %tile.7), channel_id=1, source_target_pairs={{0,64},{64,0},{4,68},{68,4},{8,72},{72,8},{12,76},{76,12},{16,80},... | collective-permute-start | bytes 1769480 | tf_op jit(solution)/shard_map/ppermute | solution.py:61
  72.4 2.4 %tile.4 = f32[256,1152]{1,0:T(8,128)S(1)} custom-call(f32[2]{0:T(128)S(1)} %pad_maximum_fusion.refs_0_.scalars, bf16[256,1152]{1,0:T(8,128)(2,1)S(1)} %bitcast.6, bf16[1024,1152]{1,0:T(8,128)(2,1)S(1)} %constant_dynamic-update-slice_fusion.refs_2_), custom_call_target="tpu_custom_call" | custom-call | flops 1207959552 | bytes 3538944 | tf_op jit(solution)/shard_map/tile/pallas_call | solution.py:169
  74.8 0.0 copy-start
  74.8 0.0 copy-start.1
  74.9 0.0 collective-permute-done.8
  74.9 0.0 collective-permute-done.9
  74.9 4.8 %collective-permute-done.10 = bf16[256,1152]{1,0:T(8,128)(2,1)S(1)} collective-permute-done((bf16[256,1152]{1,0:T(8,128)(2,1)S(1)}, bf16[256,1152]{1,0:T(8,128)(2,1)S(1)}, u32[]{:S(2)}, u32[]{:S(2)}) %collective-permute-start.10) | collective-permute-done | bytes 589856 | tf_op jit(solution)/shard_map/ppermute | solution.py:61
  79.6 0.3 add_convert_fusion
  79.9 17.4 %all_to_all.11.parts = bf16[4,64,1152]{2,1,0:T(8,128)(2,1)S(1)} all-to-all(bf16[4,64,1152]{2,1,0:T(8,128)(2,1)S(1)} %bitcast.7), channel_id=1, replica_groups={{0,16,72,88},{4,20,76,92},{8,24,80,64},{12,28,84,68},{128,144,200,216},..., dimensions={0} | all-to-all | bytes 1179648 | tf_op jit(solution)/shard_map/all_to_all | solution.py:53
  97.3 0.1 sum.1
  97.3 2.0 %collective-permute-start.11 = (f32[32,1152]{1,0:T(8,128)S(1)}, f32[32,1152]{1,0:T(8,128)S(1)}, u32[]{:S(2)}, u32[]{:S(2)}) collective-permute-start(f32[32,1152]{1,0:T(8,128)S(1)} %get-tuple-element.5), channel_id=1, source_target_pairs={{0,32},{32,0},{1,33},{33,1},{2,34},{34,2},{3,35},{35,3},{4,36},{36... | collective-permute-start | bytes 442376 | tf_op jit(solution)/shard_map/ppermute | solution.py:65
  99.4 1.2 %collective-permute-done.11.received = f32[32,1152]{1,0:T(8,128)S(1)} collective-permute-done((f32[32,1152]{1,0:T(8,128)S(1)}, f32[32,1152]{1,0:T(8,128)S(1)}, u32[]{:S(2)}, u32[]{:S(2)}) %collective-permute-start.11) | collective-permute-done | bytes 147488 | tf_op jit(solution)/shard_map/ppermute | solution.py:65
  100.6 0.0 copy-done
  100.6 0.0 copy-done.1
  100.6 1.5 %finish.1 = (f32[32,1152]{1,0:T(8,128)}, f32[32,1152]{1,0:T(8,128)}) custom-call(f32[2]{0:T(128)S(1)} %pad_maximum_fusion.refs_0_.scalars, f32[32,1152]{1,0:T(8,128)S(1)} %get-tuple-element.4.summed, f32[32,1152]{1,0:T(8,128)S(1)} %collective-permute-done.11.received, bf16[32,1152]{1,0:T(8,128)(2,1)S(1)} %copy-done, bf16[32,1152]{1,0:T(8,128)(2,1)S(1)} %copy-done.1), custom_call_target="tpu_custom_call" | custom-call | tf_op jit(solution)/shard_map/finish/pallas_call | solution.py:197
  (1 shorter events, 0.0 us)
Async XLA Ops:
  1.6 9.7 %collective-permute-start = (bf16[32,1152]{1,0:T(8,128)(2,1)S(1)}, bf16[32,1152]{1,0:T(8,128)(2,1)S(1)}, u32[]{:S(2)}, u32[]{:S(2)}) collective-permute-start(bf16[32,1152]{1,0:T(8,128)(2,1)S(1)} %get-tuple-element.6), channel_id=1, source_target_pairs={{0,32},{32,0},{1,33},{33,1},{2,34},{34,2},{3,35},{35,3},{4,36},{36... | collective-permute-start | bytes 221192 | tf_op jit(solution)/shard_map/ppermute | solution.py:65
  31.0 10.9 %collective-permute-start.2 = (bf16[256,1152]{1,0:T(8,128)(2,1)S(1)}, bf16[256,1152]{1,0:T(8,128)(2,1)S(1)}, u32[]{:S(2)}, u32[]{:S(2)}) collective-permute-start(bf16[256,1152]{1,0:T(8,128)(2,1)S(1)} %bitcast.2), channel_id=1, source_target_pairs={{4,0},{68,64},{8,4},{72,68},{12,8},{76,72},{16,12},{80,76},{20,16}... | collective-permute-start | bytes 1769480 | tf_op jit(solution)/shard_map/ppermute | solution.py:57
  33.1 12.1 %collective-permute-start.4 = (bf16[256,1152]{1,0:T(8,128)(2,1)S(1)}, bf16[256,1152]{1,0:T(8,128)(2,1)S(1)}, u32[]{:S(2)}, u32[]{:S(2)}) collective-permute-start(bf16[256,1152]{1,0:T(8,128)(2,1)S(1)} %bitcast.3), channel_id=1, source_target_pairs={{28,0},{92,64},{0,4},{64,68},{4,8},{68,72},{8,12},{72,76},{12,16},... | collective-permute-start | bytes 1769480 | tf_op jit(solution)/shard_map/ppermute | solution.py:57
  36.3 11.8 %collective-permute-start.6 = (bf16[256,1152]{1,0:T(8,128)(2,1)S(1)}, bf16[256,1152]{1,0:T(8,128)(2,1)S(1)}, u32[]{:S(2)}, u32[]{:S(2)}) collective-permute-start(bf16[256,1152]{1,0:T(8,128)(2,1)S(1)} %bitcast.4), channel_id=1, source_target_pairs={{64,0},{0,64},{68,4},{4,68},{72,8},{8,72},{76,12},{12,76},{80,16},... | collective-permute-start | bytes 1769480 | tf_op jit(solution)/shard_map/ppermute | solution.py:57
  38.6 11.4 %collective-permute-start.1 = (bf16[256,1152]{1,0:T(8,128)(2,1)S(1)}, bf16[256,1152]{1,0:T(8,128)(2,1)S(1)}, u32[]{:S(2)}, u32[]{:S(2)}) collective-permute-start(bf16[256,1152]{1,0:T(8,128)(2,1)S(1)} %bitcast.5), channel_id=1, source_target_pairs={{0,32},{32,0},{1,33},{33,1},{2,34},{34,2},{3,35},{35,3},{4,36},{36... | collective-permute-start | bytes 1769480 | tf_op jit(solution)/shard_map/ppermute | solution.py:65
  41.9 8.2 %collective-permute-start.3 = (bf16[256,1152]{1,0:T(8,128)(2,1)S(1)}, bf16[256,1152]{1,0:T(8,128)(2,1)S(1)}, u32[]{:S(2)}, u32[]{:S(2)}) collective-permute-start(bf16[256,1152]{1,0:T(8,128)(2,1)S(1)} %collective-permute-done.2.refs_1_), channel_id=1, source_target_pairs={{0,32},{32,0},{1,33},{33,1},{2,34},{34,2},{3,35},{35,3},{4,36},{36... | collective-permute-start | bytes 1769480 | tf_op jit(solution)/shard_map/ppermute | solution.py:65
  45.1 5.1 %collective-permute-start.5 = (bf16[256,1152]{1,0:T(8,128)(2,1)S(1)}, bf16[256,1152]{1,0:T(8,128)(2,1)S(1)}, u32[]{:S(2)}, u32[]{:S(2)}) collective-permute-start(bf16[256,1152]{1,0:T(8,128)(2,1)S(1)} %collective-permute-done.4.refs_1_), channel_id=1, source_target_pairs={{0,32},{32,0},{1,33},{33,1},{2,34},{34,2},{3,35},{35,3},{4,36},{36... | collective-permute-start | bytes 1769480 | tf_op jit(solution)/shard_map/ppermute | solution.py:65
  48.1 3.9 %collective-permute-start.7 = (bf16[256,1152]{1,0:T(8,128)(2,1)S(1)}, bf16[256,1152]{1,0:T(8,128)(2,1)S(1)}, u32[]{:S(2)}, u32[]{:S(2)}) collective-permute-start(bf16[256,1152]{1,0:T(8,128)(2,1)S(1)} %collective-permute-done.6.refs_1_), channel_id=1, source_target_pairs={{0,32},{32,0},{1,33},{33,1},{2,34},{34,2},{3,35},{35,3},{4,36},{36... | collective-permute-start | bytes 1769480 | tf_op jit(solution)/shard_map/ppermute | solution.py:65
  54.6 20.2 %collective-permute-start.8 = (bf16[256,1152]{1,0:T(8,128)(2,1)S(1)}, bf16[256,1152]{1,0:T(8,128)(2,1)S(1)}, u32[]{:S(2)}, u32[]{:S(2)}) collective-permute-start(bf16[256,1152]{1,0:T(8,128)(2,1)S(1)} %tile.5), channel_id=1, source_target_pairs={{0,4},{64,68},{4,8},{68,72},{8,12},{72,76},{12,16},{76,80},{16,20}... | collective-permute-start | bytes 1769480 | tf_op jit(solution)/shard_map/ppermute | solution.py:61
  60.0 14.9 %collective-permute-start.9 = (bf16[256,1152]{1,0:T(8,128)(2,1)S(1)}, bf16[256,1152]{1,0:T(8,128)(2,1)S(1)}, u32[]{:S(2)}, u32[]{:S(2)}) collective-permute-start(bf16[256,1152]{1,0:T(8,128)(2,1)S(1)} %tile.6), channel_id=1, source_target_pairs={{0,28},{64,92},{4,0},{68,64},{8,4},{72,68},{12,8},{76,72},{16,12},... | collective-permute-start | bytes 1769480 | tf_op jit(solution)/shard_map/ppermute | solution.py:61
  67.4 12.3 %collective-permute-start.10 = (bf16[256,1152]{1,0:T(8,128)(2,1)S(1)}, bf16[256,1152]{1,0:T(8,128)(2,1)S(1)}, u32[]{:S(2)}, u32[]{:S(2)}) collective-permute-start(bf16[256,1152]{1,0:T(8,128)(2,1)S(1)} %tile.7), channel_id=1, source_target_pairs={{0,64},{64,0},{4,68},{68,4},{8,72},{72,8},{12,76},{76,12},{16,80},... | collective-permute-start | bytes 1769480 | tf_op jit(solution)/shard_map/ppermute | solution.py:61
  74.8 25.8 %copy-start = (bf16[32,1152]{1,0:T(8,128)(2,1)S(1)}, bf16[32,1152]{1,0:T(8,128)(2,1)}, u32[]{:S(2)}) copy-start(bf16[32,1152]{1,0:T(8,128)(2,1)} %image.1) | copy-start | bytes 221188
  74.8 25.8 %copy-start.1 = (bf16[32,1152]{1,0:T(8,128)(2,1)S(1)}, bf16[32,1152]{1,0:T(8,128)(2,1)}, u32[]{:S(2)}) copy-start(bf16[32,1152]{1,0:T(8,128)(2,1)} %text.1) | copy-start | bytes 221188
  97.3 3.3 %collective-permute-start.11 = (f32[32,1152]{1,0:T(8,128)S(1)}, f32[32,1152]{1,0:T(8,128)S(1)}, u32[]{:S(2)}, u32[]{:S(2)}) collective-permute-start(f32[32,1152]{1,0:T(8,128)S(1)} %get-tuple-element.5), channel_id=1, source_target_pairs={{0,32},{32,0},{1,33},{33,1},{2,34},{34,2},{3,35},{35,3},{4,36},{36... | collective-permute-start | bytes 442376 | tf_op jit(solution)/shard_map/ppermute | solution.py:65

commit v6 on v5

--- a/solution.py
+++ b/solution.py
@@ -86,40 +86,63 @@
 
 
 def global_rows(index, is_text, rows):
+    bits = rows.bit_length() - 1
     x = lax.axis_index("xh") * 2 + lax.axis_index("xl")
     z = lax.axis_index("zh") * 2 + lax.axis_index("zl")
-    row = index % rows
-    slot = (index // rows) % 2
-    member = (index // (2 * rows)) % COLORS
-    chunk = index // (2 * rows * COLORS)
-    side = member // 2
-    shift = chunk ^ (chunk // 2)
+    low = jnp.minimum(x, 3 - x)
+    text = ((lax.axis_index("zl") * 4 + lax.axis_index("xh") * 2) * 2 * 8) * 4 + lax.axis_index("zh")
+    image = (lax.axis_index("y") * 8 * 4 + low) * 2 + 1
     place = jnp.where(
         is_text, lax.axis_index("y") + 2 * lax.axis_index("xl"), z + 2 * lax.axis_index("xh")
     )
-    ring = ((place + shift) % COLORS + 4 * (member % 2) + 2 * side) % RING
-    text = (
-        ((lax.axis_index("zl") * 4 + lax.axis_index("xh") * 2 + side) * 2 + slot) * 8 + ring
-    ) * 4 + lax.axis_index("zh")
-    low = jnp.minimum(x, 3 - x)
-    across = low + side * (3 - 2 * low)
-    image = ((lax.axis_index("y") * 8 + ring) * 4 + across) * 2 + 1 - slot
-    return jnp.where(is_text, text, image) * rows + row
-
-
-def tile_kernel(rows, chunk, scalars, mine, theirs, grad):
+    first = jnp.where(is_text, text, image) * rows
+    per_side = jnp.where(is_text, 64, 2 * (3 - 2 * low)) * rows
+    per_slot = jnp.where(is_text, 32, -1) * rows
+    per_ring = jnp.where(is_text, 4, 8) * rows
+
+    member = (index >> (bits + 1)) & (COLORS - 1)
+    chunk = index >> (bits + 3)
+    side = member >> 1
+    color = (place + (chunk ^ (chunk >> 1))) & (COLORS - 1)
+    ring = (color + ((member & 1) << 2) + (side << 1)) & (RING - 1)
+    slot = (index >> bits) & 1
+    return first + per_side * side + per_slot * slot + per_ring * ring + (index & (rows - 1))
+
+
+LOG2_E = 1.4426950408889634
+
+
+def tile_kernel(rows, chunks, scalars, *refs):
+    mine, theirs, grads = refs[: len(chunks)], refs[len(chunks)], refs[len(chunks) + 1 :]
     speaks_text = lax.axis_index("c") == 0
-    scale, bias = scalars[0], scalars[1]
-    part, total = mine.shape[0], theirs.shape[0]
-    there = theirs[...]
+    slope, offset = -LOG2_E * scalars[0:1, 0:1], -LOG2_E * scalars[0:1, 1:2]
+    part, total = mine[0].shape[0], theirs.shape[0]
     there_ids = global_rows(
         lax.broadcasted_iota(jnp.int32, (1, total), 1), jnp.logical_not(speaks_text), rows
     )
-    here_ids = global_rows(chunk * part + lax.broadcasted_iota(jnp.int32, (part, 1), 0), speaks_text, rows)
-    scores = lax.dot_general(mine[...], there, (((1,), (1,)), ((), ())), preferred_element_type=jnp.float32)
-    match = jnp.where(here_ids == there_ids, 1.0, 0.0)
-    weights = (jax.nn.sigmoid(scale * scores + bias) - match).astype(jnp.bfloat16)
-    grad[...] = jnp.dot(weights, there, preferred_element_type=jnp.float32).astype(grad.dtype)
+
+    def weigh(k):
+        scores = lax.dot_general(
+            mine[k][...], theirs[...], (((1,), (1,)), ((), ())), preferred_element_type=jnp.float32
+        )
+        here_ids = global_rows(
+            chunks[k] * part + lax.broadcasted_iota(jnp.int32, (part, 1), 0), speaks_text, rows
+        )
+        match = jnp.where(here_ids == there_ids, 1.0, 0.0)
+        return (1.0 / (1.0 + jnp.exp2(scores * slope + offset)) - match).astype(jnp.bfloat16)
+
+    def finish(k, weights):
+        grads[k][...] = jnp.dot(weights, theirs[...], preferred_element_type=jnp.float32).astype(
+            grads[k].dtype
+        )
+
+    before = None
+    for k in range(len(chunks)):
+        weights = weigh(k)
+        if k > 0:
+            finish(k - 1, before)
+        before = weights
+    finish(len(chunks) - 1, before)
 
 
 def sum_kernel(parts, own, other):
@@ -130,7 +153,7 @@
 
 def finish_kernel(scalars, summed, received, image, text, grad_image, grad_text):
     speaks_text = lax.axis_index("c") == 0
-    scale = scalars[0]
+    scale = scalars[0:1, 0:1]
     own, other = scale * summed[...], scale * received[...]
     img_unit, img_inv = unit_rows(image[...])
     txt_unit, txt_inv = unit_rows(text[...])
@@ -138,7 +161,6 @@
     grad_text[...] = project_back(jnp.where(speaks_text, own, other), txt_unit, txt_inv)
 
 
-SMEM = pl.BlockSpec(memory_space=pltpu.SMEM)
 VMEM = pl.BlockSpec(memory_space=pltpu.VMEM)
 SMALL = pltpu.CompilerParams(vmem_limit_bytes=8 * MIB)
 LARGE = pltpu.CompilerParams(vmem_limit_bytes=24 * MIB)
@@ -148,7 +170,7 @@
     rows, width = image_emb.shape
     part = COLORS * 2 * rows
     total = COLORS * part
-    scalars = jnp.concatenate([logit_scale, logit_bias])
+    scalars = jnp.concatenate([logit_scale, logit_bias]).reshape(1, 2)
 
     speaks_text = lax.axis_index("c") == 0
     kept = jnp.where(speaks_text, text_emb, image_emb)
@@ -163,25 +185,29 @@
     )(kept, received)
     own = exchange(copies).reshape(part, width)
     mine = [own] + [take(own, neighbour) for neighbour in NEIGHBOURS]
-    theirs = jnp.concatenate([swap_cores(chunk) for chunk in mine], axis=0)
-
-    def tile(chunk, dtype):
+    theirs = [swap_cores(chunk) for chunk in mine]
+    theirs = jnp.concatenate(theirs, axis=0)
+
+    def tile(chunks, dtype):
+        count = len(chunks)
         return pl.pallas_call(
-            lambda *refs: tile_kernel(rows, chunk, *refs),
-            out_shape=jax.ShapeDtypeStruct((part, width), dtype),
-            in_specs=[SMEM, VMEM, VMEM],
-            out_specs=VMEM,
+            lambda *refs: tile_kernel(rows, chunks, *refs),
+            out_shape=[jax.ShapeDtypeStruct((part, width), dtype)] * count,
+            in_specs=[VMEM] * (count + 2),
+            out_specs=[VMEM] * count,
             compiler_params=LARGE,
             cost_estimate=pl.CostEstimate(
-                flops=4 * part * total * width,
-                bytes_accessed=2 * (total + 2 * part) * width,
-                transcendentals=part * total,
+                flops=4 * count * part * total * width,
+                bytes_accessed=2 * (total + 2 * count * part) * width,
+                transcendentals=count * part * total,
             ),
             name="tile",
-        )(scalars, mine[chunk], theirs)
-
-    partial = [give(tile(1 + k, jnp.bfloat16), neighbour) for k, neighbour in enumerate(NEIGHBOURS)]
-    summed = tile(0, jnp.float32)
+        )(scalars, *[mine[chunk] for chunk in chunks], theirs)
+
+    partial = [
+        give(block, neighbour) for block, neighbour in zip(tile((1, 2, 3), jnp.bfloat16), NEIGHBOURS)
+    ]
+    (summed,) = tile((0,), jnp.float32)
     for block in partial:
         summed = summed + block.astype(jnp.float32)
     parts = exchange(summed.astype(jnp.bfloat16).reshape(COLORS, 2 * rows, width))
@@ -197,7 +223,7 @@
     return pl.pallas_call(
         finish_kernel,
         out_shape=(out, out),
-        in_specs=[SMEM, VMEM, VMEM, VMEM, VMEM],
+        in_specs=[VMEM] * 5,
         out_specs=(VMEM, VMEM),
         compiler_params=SMALL,
         name="finish",

time: 103 us -> 98.9 us (0.960)
  Pallas kernels: 11.6 us -> 7.19 us
    pallas_call x5 -> x3, Pallas kernels: 11.4 us -> 6.99 us  [the longest x2 6.04 us: tile(): pl.pallas_call(lambda *refs: tile_kernel(rows, chunks, *refs), out_shape=...]
  transfers between devices with their start and end apart: 12 -> 12, of which waited for: 6 -> 7; matrix products, arithmetic and copies ran while one was open for 0% -> 0% of each run, Pallas kernels for 7% -> 2%
where the time goes in v6:
time: 98.9 us; the launch traced here: 97.4 us
  starting transfers between devices  39.2 us (40%)
  blocking collectives  36.3 us (37%)
  waiting for transfers between devices  11 us (11%)
  Pallas kernels  7.19 us (7%)
  between operations  2.13 us (2%)
  other arithmetic  1.31 us (1%)
    all_to_all x2, blocking collectives, exchange(): lax.all_to_all(blocks, NAMES, 0, 0, axis_index_groups=color_groups(), til...  36.3 us
    ppermute x6, starting transfers between devices, swap_cores(): return lax.ppermute(block, 'c', [(0, 1), (1, 0)])  18.9 us
    ppermute x3, starting transfers between devices, give(): lax.ppermute(block, NAMES, [(here, there) for there, here in links(*neigh...  12.7 us
    ppermute x3, starting transfers between devices, take(): return lax.ppermute(block, NAMES, links(*neighbour))  7.61 us
    pallas_call x2, Pallas kernels, tile(): pl.pallas_call(lambda *refs: tile_kernel(rows, chunks, *refs), out_shape=...  6.04 us
    ppermute x3, waiting for transfers between devices, give(): lax.ppermute(block, NAMES, [(here, there) for there, here in links(*neigh...  5.18 us
    ppermute x6, waiting for transfers between devices, swap_cores(): return lax.ppermute(block, 'c', [(0, 1), (1, 0)])  3.96 us
  transfers between devices with their start and end apart: 12, of which 7 were waited for; matrix products, arithmetic and copies ran while one was open for 0% of the time, Pallas kernels for 2%

profile of v6, /device:TPU:1, one launch (start us, length us, event | category | flops | bytes accessed | tf_op | source)
XLA Modules:
  0.0 97.4 jit_solution(13036103684720371953)
XLA Ops:
  0.6 0.9 broadcast_select_fusion
  1.6 8.8 %collective-permute-start = (bf16[32,1152]{1,0:T(8,128)(2,1)S(1)}, bf16[32,1152]{1,0:T(8,128)(2,1)S(1)}, u32[]{:S(2)}, u32[]{:S(2)}) collective-permute-start(bf16[32,1152]{1,0:T(8,128)(2,1)S(1)} %get-tuple-element.12), channel_id=1, source_target_pairs={{0,32},{32,0},{1,33},{33,1},{2,34},{34,2},{3,35},{35,3},{4,36},{36... | collective-permute-start | bytes 221192 | tf_op jit(solution)/shard_map/ppermute | solution.py:65
  10.4 0.9 collective-permute-done.received
  11.3 0.1 spread.1
  11.4 19.6 %all_to_all.10 = bf16[4,64,1152]{2,1,0:T(8,128)(2,1)S(1)} all-to-all(bf16[4,64,1152]{2,1,0:T(8,128)(2,1)S(1)} %spread.1), channel_id=1, replica_groups={{0,16,72,88},{4,20,76,92},{8,24,80,64},{12,28,84,68},{128,144,200,216},..., dimensions={0} | all-to-all | bytes 1179648 | tf_op jit(solution)/shard_map/all_to_all | solution.py:53
  31.0 2.1 %collective-permute-start.2 = (bf16[256,1152]{1,0:T(8,128)(2,1)S(1)}, bf16[256,1152]{1,0:T(8,128)(2,1)S(1)}, u32[]{:S(2)}, u32[]{:S(2)}) collective-permute-start(bf16[256,1152]{1,0:T(8,128)(2,1)S(1)} %bitcast.4), channel_id=1, source_target_pairs={{4,0},{68,64},{8,4},{72,68},{12,8},{76,72},{16,12},{80,76},{20,16}... | collective-permute-start | bytes 1769480 | tf_op jit(solution)/shard_map/ppermute | solution.py:57
  33.1 3.2 %collective-permute-start.4 = (bf16[256,1152]{1,0:T(8,128)(2,1)S(1)}, bf16[256,1152]{1,0:T(8,128)(2,1)S(1)}, u32[]{:S(2)}, u32[]{:S(2)}) collective-permute-start(bf16[256,1152]{1,0:T(8,128)(2,1)S(1)} %bitcast.5), channel_id=1, source_target_pairs={{28,0},{92,64},{0,4},{64,68},{4,8},{68,72},{8,12},{72,76},{12,16},... | collective-permute-start | bytes 1769480 | tf_op jit(solution)/shard_map/ppermute | solution.py:57
  36.3 2.3 %collective-permute-start.6 = (bf16[256,1152]{1,0:T(8,128)(2,1)S(1)}, bf16[256,1152]{1,0:T(8,128)(2,1)S(1)}, u32[]{:S(2)}, u32[]{:S(2)}) collective-permute-start(bf16[256,1152]{1,0:T(8,128)(2,1)S(1)} %bitcast.6), channel_id=1, source_target_pairs={{64,0},{0,64},{68,4},{4,68},{72,8},{8,72},{76,12},{12,76},{80,16},... | collective-permute-start | bytes 1769480 | tf_op jit(solution)/shard_map/ppermute | solution.py:57
  38.6 1.9 %collective-permute-start.1 = (bf16[256,1152]{1,0:T(8,128)(2,1)S(1)}, bf16[256,1152]{1,0:T(8,128)(2,1)S(1)}, u32[]{:S(2)}, u32[]{:S(2)}) collective-permute-start(bf16[256,1152]{1,0:T(8,128)(2,1)S(1)} %bitcast.7), channel_id=1, source_target_pairs={{0,32},{32,0},{1,33},{33,1},{2,34},{34,2},{3,35},{35,3},{4,36},{36... | collective-permute-start | bytes 1769480 | tf_op jit(solution)/shard_map/ppermute | solution.py:65
  40.6 1.4 %collective-permute-done.2.refs_1_ = bf16[256,1152]{1,0:T(8,128)(2,1)S(1)} collective-permute-done((bf16[256,1152]{1,0:T(8,128)(2,1)S(1)}, bf16[256,1152]{1,0:T(8,128)(2,1)S(1)}, u32[]{:S(2)}, u32[]{:S(2)}) %collective-permute-start.2) | collective-permute-done | bytes 589856 | tf_op jit(solution)/shard_map/ppermute | solution.py:57
  41.9 1.9 %collective-permute-start.3 = (bf16[256,1152]{1,0:T(8,128)(2,1)S(1)}, bf16[256,1152]{1,0:T(8,128)(2,1)S(1)}, u32[]{:S(2)}, u32[]{:S(2)}) collective-permute-start(bf16[256,1152]{1,0:T(8,128)(2,1)S(1)} %collective-permute-done.2.refs_1_), channel_id=1, source_target_pairs={{0,32},{32,0},{1,33},{33,1},{2,34},{34,2},{3,35},{35,3},{4,36},{36... | collective-permute-start | bytes 1769480 | tf_op jit(solution)/shard_map/ppermute | solution.py:65
  45.1 0.0 collective-permute-done.4.refs_2_
  45.1 2.4 %collective-permute-start.5 = (bf16[256,1152]{1,0:T(8,128)(2,1)S(1)}, bf16[256,1152]{1,0:T(8,128)(2,1)S(1)}, u32[]{:S(2)}, u32[]{:S(2)}) collective-permute-start(bf16[256,1152]{1,0:T(8,128)(2,1)S(1)} %collective-permute-done.4.refs_2_), channel_id=1, source_target_pairs={{0,32},{32,0},{1,33},{33,1},{2,34},{34,2},{3,35},{35,3},{4,36},{36... | collective-permute-start | bytes 1769480 | tf_op jit(solution)/shard_map/ppermute | solution.py:65
  47.6 0.1 maximum_bitcast_fusion.refs_0_.scalars
  47.6 0.5 collective-permute-done.6.refs_3_
  48.1 1.9 %collective-permute-start.7 = (bf16[256,1152]{1,0:T(8,128)(2,1)S(1)}, bf16[256,1152]{1,0:T(8,128)(2,1)S(1)}, u32[]{:S(2)}, u32[]{:S(2)}) collective-permute-start(bf16[256,1152]{1,0:T(8,128)(2,1)S(1)} %collective-permute-done.6.refs_3_), channel_id=1, source_target_pairs={{0,32},{32,0},{1,33},{33,1},{2,34},{34,2},{3,35},{35,3},{4,36},{36... | collective-permute-start | bytes 1769480 | tf_op jit(solution)/shard_map/ppermute | solution.py:65
  50.1 0.0 collective-permute-done.1
  50.1 0.0 collective-permute-done.3
  50.1 0.1 constant_dynamic-update-slice_fusion.2
  50.2 0.0 collective-permute-done.5
  50.2 0.1 constant_dynamic-update-slice_fusion.1
  50.3 1.7 %collective-permute-done.7 = bf16[256,1152]{1,0:T(8,128)(2,1)S(1)} collective-permute-done((bf16[256,1152]{1,0:T(8,128)(2,1)S(1)}, bf16[256,1152]{1,0:T(8,128)(2,1)S(1)}, u32[]{:S(2)}, u32[]{:S(2)}) %collective-permute-start.7) | collective-permute-done | bytes 589856 | tf_op jit(solution)/shard_map/ppermute | solution.py:65
  52.0 0.1 constant_dynamic-update-slice_fusion.refs_2_.refs_4_
  52.1 4.5 %tile.3 = (bf16[256,1152]{1,0:T(8,128)(2,1)S(1)}, bf16[256,1152]{1,0:T(8,128)(2,1)S(1)}, bf16[256,1152]{1,0:T(8,128)(2,1)S(1)}) custom-call(f32[1,2]{1,0:T(1,128)S(1)} %maximum_bitcast_fusion.refs_0_.scalars, bf16[256,1152]{1,0:T(8,128)(2,1)S(1)} %collective-permute-done.2.refs_1_, bf16[256,1152]{1,0:T(8,128)(2,1)S(1)} %collective-permute-done.4.refs_2_, ...), custom_call_target="tpu_custom_call" | custom-call | flops 3623878656 | bytes 5898240 | tf_op jit(solution)/shard_map/tile/pallas_call | solution.py:193
  56.6 2.5 %collective-permute-start.10 = (bf16[256,1152]{1,0:T(8,128)(2,1)S(1)}, bf16[256,1152]{1,0:T(8,128)(2,1)S(1)}, u32[]{:S(2)}, u32[]{:S(2)}) collective-permute-start(bf16[256,1152]{1,0:T(8,128)(2,1)S(1)} %get-tuple-element.9), channel_id=1, source_target_pairs={{0,64},{64,0},{4,68},{68,4},{8,72},{72,8},{12,76},{76,12},{16,80},... | collective-permute-start | bytes 1769480 | tf_op jit(solution)/shard_map/ppermute | solution.py:61
  59.1 2.8 %collective-permute-start.8 = (bf16[256,1152]{1,0:T(8,128)(2,1)S(1)}, bf16[256,1152]{1,0:T(8,128)(2,1)S(1)}, u32[]{:S(2)}, u32[]{:S(2)}) collective-permute-start(bf16[256,1152]{1,0:T(8,128)(2,1)S(1)} %get-tuple-element.7), channel_id=1, source_target_pairs={{0,4},{64,68},{4,8},{68,72},{8,12},{72,76},{12,16},{76,80},{16,20}... | collective-permute-start | bytes 1769480 | tf_op jit(solution)/shard_map/ppermute | solution.py:61
  61.9 7.4 %collective-permute-start.9 = (bf16[256,1152]{1,0:T(8,128)(2,1)S(1)}, bf16[256,1152]{1,0:T(8,128)(2,1)S(1)}, u32[]{:S(2)}, u32[]{:S(2)}) collective-permute-start(bf16[256,1152]{1,0:T(8,128)(2,1)S(1)} %get-tuple-element.8), channel_id=1, source_target_pairs={{0,28},{64,92},{4,0},{68,64},{8,4},{72,68},{12,8},{76,72},{16,12},... | collective-permute-start | bytes 1769480 | tf_op jit(solution)/shard_map/ppermute | solution.py:61
  69.3 1.6 %tile.2 = f32[256,1152]{1,0:T(8,128)S(1)} custom-call(f32[1,2]{1,0:T(1,128)S(1)} %maximum_bitcast_fusion.refs_0_.scalars, bf16[256,1152]{1,0:T(8,128)(2,1)S(1)} %bitcast.8, bf16[1024,1152]{1,0:T(8,128)(2,1)S(1)} %constant_dynamic-update-slice_fusion.refs_2_.refs_4_), custom_call_target="tpu_custom_call" | custom-call | flops 1207959552 | bytes 3538944 | tf_op jit(solution)/shard_map/tile/pallas_call | solution.py:193
  70.9 0.0 copy-start
  70.9 0.0 copy-start.1
  70.9 0.0 collective-permute-done.10
  70.9 3.7 %collective-permute-done.8 = bf16[256,1152]{1,0:T(8,128)(2,1)S(1)} collective-permute-done((bf16[256,1152]{1,0:T(8,128)(2,1)S(1)}, bf16[256,1152]{1,0:T(8,128)(2,1)S(1)}, u32[]{:S(2)}, u32[]{:S(2)}) %collective-permute-start.8) | collective-permute-done | bytes 589856 | tf_op jit(solution)/shard_map/ppermute | solution.py:61
  74.6 1.5 %collective-permute-done.9 = bf16[256,1152]{1,0:T(8,128)(2,1)S(1)} collective-permute-done((bf16[256,1152]{1,0:T(8,128)(2,1)S(1)}, bf16[256,1152]{1,0:T(8,128)(2,1)S(1)}, u32[]{:S(2)}, u32[]{:S(2)}) %collective-permute-start.9) | collective-permute-done | bytes 589856 | tf_op jit(solution)/shard_map/ppermute | solution.py:61
  76.1 0.3 add_convert_fusion
  76.4 16.7 %all_to_all.11.parts = bf16[4,64,1152]{2,1,0:T(8,128)(2,1)S(1)} all-to-all(bf16[4,64,1152]{2,1,0:T(8,128)(2,1)S(1)} %bitcast.9), channel_id=1, replica_groups={{0,16,72,88},{4,20,76,92},{8,24,80,64},{12,28,84,68},{128,144,200,216},..., dimensions={0} | all-to-all | bytes 1179648 | tf_op jit(solution)/shard_map/all_to_all | solution.py:53
  93.1 0.1 sum.1
  93.2 1.9 %collective-permute-start.11 = (f32[32,1152]{1,0:T(8,128)S(1)}, f32[32,1152]{1,0:T(8,128)S(1)}, u32[]{:S(2)}, u32[]{:S(2)}) collective-permute-start(f32[32,1152]{1,0:T(8,128)S(1)} %get-tuple-element.11), channel_id=1, source_target_pairs={{0,32},{32,0},{1,33},{33,1},{2,34},{34,2},{3,35},{35,3},{4,36},{36... | collective-permute-start | bytes 442376 | tf_op jit(solution)/shard_map/ppermute | solution.py:65
  95.1 1.3 %collective-permute-done.11.received = f32[32,1152]{1,0:T(8,128)S(1)} collective-permute-done((f32[32,1152]{1,0:T(8,128)S(1)}, f32[32,1152]{1,0:T(8,128)S(1)}, u32[]{:S(2)}, u32[]{:S(2)}) %collective-permute-start.11) | collective-permute-done | bytes 147488 | tf_op jit(solution)/shard_map/ppermute | solution.py:65
  96.5 0.0 copy-done
  96.5 0.0 copy-done.1
  96.5 0.9 finish.1
  (1 shorter events, 0.0 us)
Async XLA Ops:
  1.6 9.7 %collective-permute-start = (bf16[32,1152]{1,0:T(8,128)(2,1)S(1)}, bf16[32,1152]{1,0:T(8,128)(2,1)S(1)}, u32[]{:S(2)}, u32[]{:S(2)}) collective-permute-start(bf16[32,1152]{1,0:T(8,128)(2,1)S(1)} %get-tuple-element.12), channel_id=1, source_target_pairs={{0,32},{32,0},{1,33},{33,1},{2,34},{34,2},{3,35},{35,3},{4,36},{36... | collective-permute-start | bytes 221192 | tf_op jit(solution)/shard_map/ppermute | solution.py:65
  31.0 10.9 %collective-permute-start.2 = (bf16[256,1152]{1,0:T(8,128)(2,1)S(1)}, bf16[256,1152]{1,0:T(8,128)(2,1)S(1)}, u32[]{:S(2)}, u32[]{:S(2)}) collective-permute-start(bf16[256,1152]{1,0:T(8,128)(2,1)S(1)} %bitcast.4), channel_id=1, source_target_pairs={{4,0},{68,64},{8,4},{72,68},{12,8},{76,72},{16,12},{80,76},{20,16}... | collective-permute-start | bytes 1769480 | tf_op jit(solution)/shard_map/ppermute | solution.py:57
  33.1 12.1 %collective-permute-start.4 = (bf16[256,1152]{1,0:T(8,128)(2,1)S(1)}, bf16[256,1152]{1,0:T(8,128)(2,1)S(1)}, u32[]{:S(2)}, u32[]{:S(2)}) collective-permute-start(bf16[256,1152]{1,0:T(8,128)(2,1)S(1)} %bitcast.5), channel_id=1, source_target_pairs={{28,0},{92,64},{0,4},{64,68},{4,8},{68,72},{8,12},{72,76},{12,16},... | collective-permute-start | bytes 1769480 | tf_op jit(solution)/shard_map/ppermute | solution.py:57
  36.3 11.8 %collective-permute-start.6 = (bf16[256,1152]{1,0:T(8,128)(2,1)S(1)}, bf16[256,1152]{1,0:T(8,128)(2,1)S(1)}, u32[]{:S(2)}, u32[]{:S(2)}) collective-permute-start(bf16[256,1152]{1,0:T(8,128)(2,1)S(1)} %bitcast.6), channel_id=1, source_target_pairs={{64,0},{0,64},{68,4},{4,68},{72,8},{8,72},{76,12},{12,76},{80,16},... | collective-permute-start | bytes 1769480 | tf_op jit(solution)/shard_map/ppermute | solution.py:57
  38.6 11.4 %collective-permute-start.1 = (bf16[256,1152]{1,0:T(8,128)(2,1)S(1)}, bf16[256,1152]{1,0:T(8,128)(2,1)S(1)}, u32[]{:S(2)}, u32[]{:S(2)}) collective-permute-start(bf16[256,1152]{1,0:T(8,128)(2,1)S(1)} %bitcast.7), channel_id=1, source_target_pairs={{0,32},{32,0},{1,33},{33,1},{2,34},{34,2},{3,35},{35,3},{4,36},{36... | collective-permute-start | bytes 1769480 | tf_op jit(solution)/shard_map/ppermute | solution.py:65
  41.9 8.2 %collective-permute-start.3 = (bf16[256,1152]{1,0:T(8,128)(2,1)S(1)}, bf16[256,1152]{1,0:T(8,128)(2,1)S(1)}, u32[]{:S(2)}, u32[]{:S(2)}) collective-permute-start(bf16[256,1152]{1,0:T(8,128)(2,1)S(1)} %collective-permute-done.2.refs_1_), channel_id=1, source_target_pairs={{0,32},{32,0},{1,33},{33,1},{2,34},{34,2},{3,35},{35,3},{4,36},{36... | collective-permute-start | bytes 1769480 | tf_op jit(solution)/shard_map/ppermute | solution.py:65
  45.1 5.1 %collective-permute-start.5 = (bf16[256,1152]{1,0:T(8,128)(2,1)S(1)}, bf16[256,1152]{1,0:T(8,128)(2,1)S(1)}, u32[]{:S(2)}, u32[]{:S(2)}) collective-permute-start(bf16[256,1152]{1,0:T(8,128)(2,1)S(1)} %collective-permute-done.4.refs_2_), channel_id=1, source_target_pairs={{0,32},{32,0},{1,33},{33,1},{2,34},{34,2},{3,35},{35,3},{4,36},{36... | collective-permute-start | bytes 1769480 | tf_op jit(solution)/shard_map/ppermute | solution.py:65
  48.1 3.9 %collective-permute-start.7 = (bf16[256,1152]{1,0:T(8,128)(2,1)S(1)}, bf16[256,1152]{1,0:T(8,128)(2,1)S(1)}, u32[]{:S(2)}, u32[]{:S(2)}) collective-permute-start(bf16[256,1152]{1,0:T(8,128)(2,1)S(1)} %collective-permute-done.6.refs_3_), channel_id=1, source_target_pairs={{0,32},{32,0},{1,33},{33,1},{2,34},{34,2},{3,35},{35,3},{4,36},{36... | collective-permute-start | bytes 1769480 | tf_op jit(solution)/shard_map/ppermute | solution.py:65
  56.6 14.4 %collective-permute-start.10 = (bf16[256,1152]{1,0:T(8,128)(2,1)S(1)}, bf16[256,1152]{1,0:T(8,128)(2,1)S(1)}, u32[]{:S(2)}, u32[]{:S(2)}) collective-permute-start(bf16[256,1152]{1,0:T(8,128)(2,1)S(1)} %get-tuple-element.9), channel_id=1, source_target_pairs={{0,64},{64,0},{4,68},{68,4},{8,72},{72,8},{12,76},{76,12},{16,80},... | collective-permute-start | bytes 1769480 | tf_op jit(solution)/shard_map/ppermute | solution.py:61
  59.1 15.5 %collective-permute-start.8 = (bf16[256,1152]{1,0:T(8,128)(2,1)S(1)}, bf16[256,1152]{1,0:T(8,128)(2,1)S(1)}, u32[]{:S(2)}, u32[]{:S(2)}) collective-permute-start(bf16[256,1152]{1,0:T(8,128)(2,1)S(1)} %get-tuple-element.7), channel_id=1, source_target_pairs={{0,4},{64,68},{4,8},{68,72},{8,12},{72,76},{12,16},{76,80},{16,20}... | collective-permute-start | bytes 1769480 | tf_op jit(solution)/shard_map/ppermute | solution.py:61
  61.9 14.3 %collective-permute-start.9 = (bf16[256,1152]{1,0:T(8,128)(2,1)S(1)}, bf16[256,1152]{1,0:T(8,128)(2,1)S(1)}, u32[]{:S(2)}, u32[]{:S(2)}) collective-permute-start(bf16[256,1152]{1,0:T(8,128)(2,1)S(1)} %get-tuple-element.8), channel_id=1, source_target_pairs={{0,28},{64,92},{4,0},{68,64},{8,4},{72,68},{12,8},{76,72},{16,12},... | collective-permute-start | bytes 1769480 | tf_op jit(solution)/shard_map/ppermute | solution.py:61
  70.9 25.6 %copy-start = (bf16[32,1152]{1,0:T(8,128)(2,1)S(1)}, bf16[32,1152]{1,0:T(8,128)(2,1)}, u32[]{:S(2)}) copy-start(bf16[32,1152]{1,0:T(8,128)(2,1)} %image.1) | copy-start | bytes 221188
  70.9 25.6 %copy-start.1 = (bf16[32,1152]{1,0:T(8,128)(2,1)S(1)}, bf16[32,1152]{1,0:T(8,128)(2,1)}, u32[]{:S(2)}) copy-start(bf16[32,1152]{1,0:T(8,128)(2,1)} %text.1) | copy-start | bytes 221188
  93.2 3.3 %collective-permute-start.11 = (f32[32,1152]{1,0:T(8,128)S(1)}, f32[32,1152]{1,0:T(8,128)S(1)}, u32[]{:S(2)}, u32[]{:S(2)}) collective-permute-start(f32[32,1152]{1,0:T(8,128)S(1)} %get-tuple-element.11), channel_id=1, source_target_pairs={{0,32},{32,0},{1,33},{33,1},{2,34},{34,2},{3,35},{35,3},{4,36},{36... | collective-permute-start | bytes 442376 | tf_op jit(solution)/shard_map/ppermute | solution.py:65

commit v7 on v6

--- a/solution.py
+++ b/solution.py
@@ -65,6 +65,10 @@
     return lax.ppermute(block, "c", [(0, 1), (1, 0)])
 
 
+def gather_cores(block):
+    return lax.all_gather(block, "c", axis=0, tiled=True)
+
+
 def unit_rows(embedded):
     values = embedded.astype(jnp.float32)
     inverse = lax.rsqrt(jnp.sum(values * values, axis=1, keepdims=True) + EPS)
@@ -76,10 +80,15 @@
     return (grad - unit * inner) * inverse
 
 
-def spread_kernel(own, received, copies):
+def from_other_core(pair):
+    rows = pair.shape[0] // 2
+    return pair[pl.ds(pl.multiple_of((1 - lax.axis_index("c")) * rows, rows), rows), :]
+
+
+def spread_kernel(own, pair, copies):
     rows = own.shape[0]
     first = unit_rows(own[...])[0].astype(jnp.bfloat16)
-    second = unit_rows(received[...])[0].astype(jnp.bfloat16)
+    second = unit_rows(from_other_core(pair))[0].astype(jnp.bfloat16)
     for peer in range(COLORS):
         copies[peer, :rows, :] = first
         copies[peer, rows:, :] = second
@@ -151,10 +160,10 @@
     other[...] = jnp.sum(parts[:, rows:, :].astype(jnp.float32), axis=0)
 
 
-def finish_kernel(scalars, summed, received, image, text, grad_image, grad_text):
+def finish_kernel(scalars, summed, pair, image, text, grad_image, grad_text):
     speaks_text = lax.axis_index("c") == 0
     scale = scalars[0:1, 0:1]
-    own, other = scale * summed[...], scale * received[...]
+    own, other = scale * summed[...], scale * from_other_core(pair)
     img_unit, img_inv = unit_rows(image[...])
     txt_unit, txt_inv = unit_rows(text[...])
     grad_image[...] = project_back(jnp.where(speaks_text, other, own), img_unit, img_inv)
@@ -174,7 +183,7 @@
 
     speaks_text = lax.axis_index("c") == 0
     kept = jnp.where(speaks_text, text_emb, image_emb)
-    received = swap_cores(jnp.where(speaks_text, image_emb, text_emb))
+    pair = gather_cores(jnp.where(speaks_text, image_emb, text_emb))
     copies = pl.pallas_call(
         spread_kernel,
         out_shape=jax.ShapeDtypeStruct((COLORS, 2 * rows, width), jnp.bfloat16),
@@ -182,7 +191,7 @@
         out_specs=VMEM,
         compiler_params=SMALL,
         name="spread",
-    )(kept, received)
+    )(kept, pair)
     own = exchange(copies).reshape(part, width)
     mine = [own] + [take(own, neighbour) for neighbour in NEIGHBOURS]
     theirs = [swap_cores(chunk) for chunk in mine]
@@ -227,7 +236,7 @@
         out_specs=(VMEM, VMEM),
         compiler_params=SMALL,
         name="finish",
-    )(scalars, own, swap_cores(other), image_emb, text_emb)
+    )(scalars, own, gather_cores(other), image_emb, text_emb)
 
 
 def solution(mesh):

time: 98.9 us -> 96.5 us (0.976)
  blocking collectives: 36.3 us -> 47.4 us
  starting transfers between devices: 39.2 us -> 28.5 us
  waiting for transfers between devices: 11 us -> 9.23 us
    ppermute x6 -> x4, starting transfers between devices: 18.9 us -> 8.14 us  [swap_cores(): return lax.ppermute(block, 'c', [(0, 1), (1, 0)])]
    all_gather x0 -> x2, blocking collectives: none -> 10.5 us  [gather_cores(): return lax.all_gather(block, 'c', axis=0, tiled=True)]
    ppermute x6 -> x4, waiting for transfers between devices: 3.96 us -> 1.74 us  [swap_cores(): return lax.ppermute(block, 'c', [(0, 1), (1, 0)])]
  transfers between devices with their start and end apart: 12 -> 10, of which waited for: 7 -> 5; matrix products, arithmetic and copies ran while one was open for 0% -> 0% of each run, Pallas kernels for 2% -> 2%
where the time goes in v7:
time: 96.5 us; the launch traced here: 96 us
  blocking collectives  47.4 us (49%)
  starting transfers between devices  28.5 us (30%)
  waiting for transfers between devices  9.23 us (10%)
  Pallas kernels  7.19 us (7%)
  between operations  2.12 us (2%)
  other arithmetic  1.31 us (1%)
    all_to_all x2, blocking collectives, exchange(): lax.all_to_all(blocks, NAMES, 0, 0, axis_index_groups=color_groups(), til...  37 us
    ppermute x3, starting transfers between devices, give(): lax.ppermute(block, NAMES, [(here, there) for there, here in links(*neigh...  12.7 us
    all_gather x2, blocking collectives, gather_cores(): return lax.all_gather(block, 'c', axis=0, tiled=True)  10.5 us
    ppermute x4, starting transfers between devices, swap_cores(): return lax.ppermute(block, 'c', [(0, 1), (1, 0)])  8.14 us
    ppermute x3, starting transfers between devices, take(): return lax.ppermute(block, NAMES, links(*neighbour))  7.61 us
    pallas_call x2, Pallas kernels, tile(): pl.pallas_call(lambda *refs: tile_kernel(rows, chunks, *refs), out_shape=...  6.04 us
    ppermute x3, waiting for transfers between devices, give(): lax.ppermute(block, NAMES, [(here, there) for there, here in links(*neigh...  5.63 us
  transfers between devices with their start and end apart: 10, of which 5 were waited for; matrix products, arithmetic and copies ran while one was open for 0% of the time, Pallas kernels for 2%

profile of v7, /device:TPU:1, one launch (start us, length us, event | category | flops | bytes accessed | tf_op | source)
XLA Modules:
  0.0 96.0 jit_solution(8462961905234359377)
XLA Ops:
  0.6 0.9 broadcast_select_fusion
  1.6 8.4 %all_gather.6.pair = bf16[64,1152]{1,0:T(8,128)(2,1)S(1)} all-gather(bf16[32,1152]{1,0:T(8,128)(2,1)S(1)} %get-tuple-element.12), channel_id=1, replica_groups=mesh['zl'=2,'xh'=2,'xl'=2,'c'=2,'y'=8,'zh'=4] {'c'}, dimensions={0}, use_global_device_ids=true | all-gather | bytes 221184 | tf_op jit(solution)/shard_map/all_gather | solution.py:69
  10.0 0.1 spread.1
  10.2 19.6 %all_to_all.10 = bf16[4,64,1152]{2,1,0:T(8,128)(2,1)S(1)} all-to-all(bf16[4,64,1152]{2,1,0:T(8,128)(2,1)S(1)} %spread.1), channel_id=1, replica_groups={{0,16,72,88},{4,20,76,92},{8,24,80,64},{12,28,84,68},{128,144,200,216},..., dimensions={0} | all-to-all | bytes 1179648 | tf_op jit(solution)/shard_map/all_to_all | solution.py:53
  29.8 2.1 %collective-permute-start.1 = (bf16[256,1152]{1,0:T(8,128)(2,1)S(1)}, bf16[256,1152]{1,0:T(8,128)(2,1)S(1)}, u32[]{:S(2)}, u32[]{:S(2)}) collective-permute-start(bf16[256,1152]{1,0:T(8,128)(2,1)S(1)} %bitcast.4), channel_id=1, source_target_pairs={{4,0},{68,64},{8,4},{72,68},{12,8},{76,72},{16,12},{80,76},{20,16}... | collective-permute-start | bytes 1769480 | tf_op jit(solution)/shard_map/ppermute | solution.py:57
  31.8 3.2 %collective-permute-start.3 = (bf16[256,1152]{1,0:T(8,128)(2,1)S(1)}, bf16[256,1152]{1,0:T(8,128)(2,1)S(1)}, u32[]{:S(2)}, u32[]{:S(2)}) collective-permute-start(bf16[256,1152]{1,0:T(8,128)(2,1)S(1)} %bitcast.5), channel_id=1, source_target_pairs={{28,0},{92,64},{0,4},{64,68},{4,8},{68,72},{8,12},{72,76},{12,16},... | collective-permute-start | bytes 1769480 | tf_op jit(solution)/shard_map/ppermute | solution.py:57
  35.0 2.3 %collective-permute-start.5 = (bf16[256,1152]{1,0:T(8,128)(2,1)S(1)}, bf16[256,1152]{1,0:T(8,128)(2,1)S(1)}, u32[]{:S(2)}, u32[]{:S(2)}) collective-permute-start(bf16[256,1152]{1,0:T(8,128)(2,1)S(1)} %bitcast.6), channel_id=1, source_target_pairs={{64,0},{0,64},{68,4},{4,68},{72,8},{8,72},{76,12},{12,76},{80,16},... | collective-permute-start | bytes 1769480 | tf_op jit(solution)/shard_map/ppermute | solution.py:57
  37.4 1.9 %collective-permute-start = (bf16[256,1152]{1,0:T(8,128)(2,1)S(1)}, bf16[256,1152]{1,0:T(8,128)(2,1)S(1)}, u32[]{:S(2)}, u32[]{:S(2)}) collective-permute-start(bf16[256,1152]{1,0:T(8,128)(2,1)S(1)} %bitcast.7), channel_id=1, source_target_pairs={{0,32},{32,0},{1,33},{33,1},{2,34},{34,2},{3,35},{35,3},{4,36},{36... | collective-permute-start | bytes 1769480 | tf_op jit(solution)/shard_map/ppermute | solution.py:65
  39.3 1.4 %collective-permute-done.1.refs_1_ = bf16[256,1152]{1,0:T(8,128)(2,1)S(1)} collective-permute-done((bf16[256,1152]{1,0:T(8,128)(2,1)S(1)}, bf16[256,1152]{1,0:T(8,128)(2,1)S(1)}, u32[]{:S(2)}, u32[]{:S(2)}) %collective-permute-start.1) | collective-permute-done | bytes 589856 | tf_op jit(solution)/shard_map/ppermute | solution.py:57
  40.7 1.9 %collective-permute-start.2 = (bf16[256,1152]{1,0:T(8,128)(2,1)S(1)}, bf16[256,1152]{1,0:T(8,128)(2,1)S(1)}, u32[]{:S(2)}, u32[]{:S(2)}) collective-permute-start(bf16[256,1152]{1,0:T(8,128)(2,1)S(1)} %collective-permute-done.1.refs_1_), channel_id=1, source_target_pairs={{0,32},{32,0},{1,33},{33,1},{2,34},{34,2},{3,35},{35,3},{4,36},{36... | collective-permute-start | bytes 1769480 | tf_op jit(solution)/shard_map/ppermute | solution.py:65
  43.9 0.0 collective-permute-done.3.refs_2_
  43.9 2.4 %collective-permute-start.4 = (bf16[256,1152]{1,0:T(8,128)(2,1)S(1)}, bf16[256,1152]{1,0:T(8,128)(2,1)S(1)}, u32[]{:S(2)}, u32[]{:S(2)}) collective-permute-start(bf16[256,1152]{1,0:T(8,128)(2,1)S(1)} %collective-permute-done.3.refs_2_), channel_id=1, source_target_pairs={{0,32},{32,0},{1,33},{33,1},{2,34},{34,2},{3,35},{35,3},{4,36},{36... | collective-permute-start | bytes 1769480 | tf_op jit(solution)/shard_map/ppermute | solution.py:65
  46.3 0.1 maximum_bitcast_fusion.refs_0_.scalars
  46.4 0.5 collective-permute-done.5.refs_3_
  46.9 1.9 %collective-permute-start.6 = (bf16[256,1152]{1,0:T(8,128)(2,1)S(1)}, bf16[256,1152]{1,0:T(8,128)(2,1)S(1)}, u32[]{:S(2)}, u32[]{:S(2)}) collective-permute-start(bf16[256,1152]{1,0:T(8,128)(2,1)S(1)} %collective-permute-done.5.refs_3_), channel_id=1, source_target_pairs={{0,32},{32,0},{1,33},{33,1},{2,34},{34,2},{3,35},{35,3},{4,36},{36... | collective-permute-start | bytes 1769480 | tf_op jit(solution)/shard_map/ppermute | solution.py:65
  48.8 0.0 collective-permute-done
  48.9 0.0 collective-permute-done.2
  48.9 0.1 constant_dynamic-update-slice_fusion.2
  49.0 0.0 collective-permute-done.4
  49.0 0.1 constant_dynamic-update-slice_fusion.1
  49.0 1.7 %collective-permute-done.6 = bf16[256,1152]{1,0:T(8,128)(2,1)S(1)} collective-permute-done((bf16[256,1152]{1,0:T(8,128)(2,1)S(1)}, bf16[256,1152]{1,0:T(8,128)(2,1)S(1)}, u32[]{:S(2)}, u32[]{:S(2)}) %collective-permute-start.6) | collective-permute-done | bytes 589856 | tf_op jit(solution)/shard_map/ppermute | solution.py:65
  50.8 0.1 constant_dynamic-update-slice_fusion.refs_2_.refs_4_
  50.8 4.5 %tile.3 = (bf16[256,1152]{1,0:T(8,128)(2,1)S(1)}, bf16[256,1152]{1,0:T(8,128)(2,1)S(1)}, bf16[256,1152]{1,0:T(8,128)(2,1)S(1)}) custom-call(f32[1,2]{1,0:T(1,128)S(1)} %maximum_bitcast_fusion.refs_0_.scalars, bf16[256,1152]{1,0:T(8,128)(2,1)S(1)} %collective-permute-done.1.refs_1_, bf16[256,1152]{1,0:T(8,128)(2,1)S(1)} %collective-permute-done.3.refs_2_, ...), custom_call_target="tpu_custom_call" | custom-call | flops 3623878656 | bytes 5898240 | tf_op jit(solution)/shard_map/tile/pallas_call | solution.py:202
  55.3 2.8 %collective-permute-start.7 = (bf16[256,1152]{1,0:T(8,128)(2,1)S(1)}, bf16[256,1152]{1,0:T(8,128)(2,1)S(1)}, u32[]{:S(2)}, u32[]{:S(2)}) collective-permute-start(bf16[256,1152]{1,0:T(8,128)(2,1)S(1)} %get-tuple-element.7), channel_id=1, source_target_pairs={{0,4},{64,68},{4,8},{68,72},{8,12},{72,76},{12,16},{76,80},{16,20}... | collective-permute-start | bytes 1769480 | tf_op jit(solution)/shard_map/ppermute | solution.py:61
  58.1 4.9 %collective-permute-start.8 = (bf16[256,1152]{1,0:T(8,128)(2,1)S(1)}, bf16[256,1152]{1,0:T(8,128)(2,1)S(1)}, u32[]{:S(2)}, u32[]{:S(2)}) collective-permute-start(bf16[256,1152]{1,0:T(8,128)(2,1)S(1)} %get-tuple-element.8), channel_id=1, source_target_pairs={{0,28},{64,92},{4,0},{68,64},{8,4},{72,68},{12,8},{76,72},{16,12},... | collective-permute-start | bytes 1769480 | tf_op jit(solution)/shard_map/ppermute | solution.py:61
  63.1 5.0 %collective-permute-start.9 = (bf16[256,1152]{1,0:T(8,128)(2,1)S(1)}, bf16[256,1152]{1,0:T(8,128)(2,1)S(1)}, u32[]{:S(2)}, u32[]{:S(2)}) collective-permute-start(bf16[256,1152]{1,0:T(8,128)(2,1)S(1)} %get-tuple-element.9), channel_id=1, source_target_pairs={{0,64},{64,0},{4,68},{68,4},{8,72},{72,8},{12,76},{76,12},{16,80},... | collective-permute-start | bytes 1769480 | tf_op jit(solution)/shard_map/ppermute | solution.py:61
  68.1 1.6 %tile.2 = f32[256,1152]{1,0:T(8,128)S(1)} custom-call(f32[1,2]{1,0:T(1,128)S(1)} %maximum_bitcast_fusion.refs_0_.scalars, bf16[256,1152]{1,0:T(8,128)(2,1)S(1)} %bitcast.8, bf16[1024,1152]{1,0:T(8,128)(2,1)S(1)} %constant_dynamic-update-slice_fusion.refs_2_.refs_4_), custom_call_target="tpu_custom_call" | custom-call | flops 1207959552 | bytes 3538944 | tf_op jit(solution)/shard_map/tile/pallas_call | solution.py:202
  69.6 0.0 copy-start
  69.7 0.0 copy-start.1
  69.7 0.0 collective-permute-done.7
  69.7 0.2 collective-permute-done.8
  69.9 5.4 %collective-permute-done.9 = bf16[256,1152]{1,0:T(8,128)(2,1)S(1)} collective-permute-done((bf16[256,1152]{1,0:T(8,128)(2,1)S(1)}, bf16[256,1152]{1,0:T(8,128)(2,1)S(1)}, u32[]{:S(2)}, u32[]{:S(2)}) %collective-permute-start.9) | collective-permute-done | bytes 589856 | tf_op jit(solution)/shard_map/ppermute | solution.py:61
  75.3 0.3 add_convert_fusion
  75.6 17.4 %all_to_all.11.parts = bf16[4,64,1152]{2,1,0:T(8,128)(2,1)S(1)} all-to-all(bf16[4,64,1152]{2,1,0:T(8,128)(2,1)S(1)} %bitcast.9), channel_id=1, replica_groups={{0,16,72,88},{4,20,76,92},{8,24,80,64},{12,28,84,68},{128,144,200,216},..., dimensions={0} | all-to-all | bytes 1179648 | tf_op jit(solution)/shard_map/all_to_all | solution.py:53
  93.0 0.1 sum.1
  93.0 2.0 %all_gather.7.pair = f32[64,1152]{1,0:T(8,128)S(1)} all-gather(f32[32,1152]{1,0:T(8,128)S(1)} %get-tuple-element.11), channel_id=1, replica_groups=mesh['zl'=2,'xh'=2,'xl'=2,'c'=2,'y'=8,'zh'=4] {'c'}, dimensions={0}, use_global_device_ids=true | all-gather | bytes 442368 | tf_op jit(solution)/shard_map/all_gather | solution.py:69
  95.1 0.0 copy-done
  95.1 0.0 copy-done.1
  95.1 0.9 finish.1
  (1 shorter events, 0.0 us)
Async XLA Ops:
  29.8 10.9 %collective-permute-start.1 = (bf16[256,1152]{1,0:T(8,128)(2,1)S(1)}, bf16[256,1152]{1,0:T(8,128)(2,1)S(1)}, u32[]{:S(2)}, u32[]{:S(2)}) collective-permute-start(bf16[256,1152]{1,0:T(8,128)(2,1)S(1)} %bitcast.4), channel_id=1, source_target_pairs={{4,0},{68,64},{8,4},{72,68},{12,8},{76,72},{16,12},{80,76},{20,16}... | collective-permute-start | bytes 1769480 | tf_op jit(solution)/shard_map/ppermute | solution.py:57
  31.8 12.1 %collective-permute-start.3 = (bf16[256,1152]{1,0:T(8,128)(2,1)S(1)}, bf16[256,1152]{1,0:T(8,128)(2,1)S(1)}, u32[]{:S(2)}, u32[]{:S(2)}) collective-permute-start(bf16[256,1152]{1,0:T(8,128)(2,1)S(1)} %bitcast.5), channel_id=1, source_target_pairs={{28,0},{92,64},{0,4},{64,68},{4,8},{68,72},{8,12},{72,76},{12,16},... | collective-permute-start | bytes 1769480 | tf_op jit(solution)/shard_map/ppermute | solution.py:57
  35.0 11.8 %collective-permute-start.5 = (bf16[256,1152]{1,0:T(8,128)(2,1)S(1)}, bf16[256,1152]{1,0:T(8,128)(2,1)S(1)}, u32[]{:S(2)}, u32[]{:S(2)}) collective-permute-start(bf16[256,1152]{1,0:T(8,128)(2,1)S(1)} %bitcast.6), channel_id=1, source_target_pairs={{64,0},{0,64},{68,4},{4,68},{72,8},{8,72},{76,12},{12,76},{80,16},... | collective-permute-start | bytes 1769480 | tf_op jit(solution)/shard_map/ppermute | solution.py:57
  37.4 11.4 %collective-permute-start = (bf16[256,1152]{1,0:T(8,128)(2,1)S(1)}, bf16[256,1152]{1,0:T(8,128)(2,1)S(1)}, u32[]{:S(2)}, u32[]{:S(2)}) collective-permute-start(bf16[256,1152]{1,0:T(8,128)(2,1)S(1)} %bitcast.7), channel_id=1, source_target_pairs={{0,32},{32,0},{1,33},{33,1},{2,34},{34,2},{3,35},{35,3},{4,36},{36... | collective-permute-start | bytes 1769480 | tf_op jit(solution)/shard_map/ppermute | solution.py:65
  40.7 8.2 %collective-permute-start.2 = (bf16[256,1152]{1,0:T(8,128)(2,1)S(1)}, bf16[256,1152]{1,0:T(8,128)(2,1)S(1)}, u32[]{:S(2)}, u32[]{:S(2)}) collective-permute-start(bf16[256,1152]{1,0:T(8,128)(2,1)S(1)} %collective-permute-done.1.refs_1_), channel_id=1, source_target_pairs={{0,32},{32,0},{1,33},{33,1},{2,34},{34,2},{3,35},{35,3},{4,36},{36... | collective-permute-start | bytes 1769480 | tf_op jit(solution)/shard_map/ppermute | solution.py:65
  43.9 5.1 %collective-permute-start.4 = (bf16[256,1152]{1,0:T(8,128)(2,1)S(1)}, bf16[256,1152]{1,0:T(8,128)(2,1)S(1)}, u32[]{:S(2)}, u32[]{:S(2)}) collective-permute-start(bf16[256,1152]{1,0:T(8,128)(2,1)S(1)} %collective-permute-done.3.refs_2_), channel_id=1, source_target_pairs={{0,32},{32,0},{1,33},{33,1},{2,34},{34,2},{3,35},{35,3},{4,36},{36... | collective-permute-start | bytes 1769480 | tf_op jit(solution)/shard_map/ppermute | solution.py:65
  46.9 3.9 %collective-permute-start.6 = (bf16[256,1152]{1,0:T(8,128)(2,1)S(1)}, bf16[256,1152]{1,0:T(8,128)(2,1)S(1)}, u32[]{:S(2)}, u32[]{:S(2)}) collective-permute-start(bf16[256,1152]{1,0:T(8,128)(2,1)S(1)} %collective-permute-done.5.refs_3_), channel_id=1, source_target_pairs={{0,32},{32,0},{1,33},{33,1},{2,34},{34,2},{3,35},{35,3},{4,36},{36... | collective-permute-start | bytes 1769480 | tf_op jit(solution)/shard_map/ppermute | solution.py:65
  55.3 14.4 %collective-permute-start.7 = (bf16[256,1152]{1,0:T(8,128)(2,1)S(1)}, bf16[256,1152]{1,0:T(8,128)(2,1)S(1)}, u32[]{:S(2)}, u32[]{:S(2)}) collective-permute-start(bf16[256,1152]{1,0:T(8,128)(2,1)S(1)} %get-tuple-element.7), channel_id=1, source_target_pairs={{0,4},{64,68},{4,8},{68,72},{8,12},{72,76},{12,16},{76,80},{16,20}... | collective-permute-start | bytes 1769480 | tf_op jit(solution)/shard_map/ppermute | solution.py:61
  58.1 11.7 %collective-permute-start.8 = (bf16[256,1152]{1,0:T(8,128)(2,1)S(1)}, bf16[256,1152]{1,0:T(8,128)(2,1)S(1)}, u32[]{:S(2)}, u32[]{:S(2)}) collective-permute-start(bf16[256,1152]{1,0:T(8,128)(2,1)S(1)} %get-tuple-element.8), channel_id=1, source_target_pairs={{0,28},{64,92},{4,0},{68,64},{8,4},{72,68},{12,8},{76,72},{16,12},... | collective-permute-start | bytes 1769480 | tf_op jit(solution)/shard_map/ppermute | solution.py:61
  63.1 12.2 %collective-permute-start.9 = (bf16[256,1152]{1,0:T(8,128)(2,1)S(1)}, bf16[256,1152]{1,0:T(8,128)(2,1)S(1)}, u32[]{:S(2)}, u32[]{:S(2)}) collective-permute-start(bf16[256,1152]{1,0:T(8,128)(2,1)S(1)} %get-tuple-element.9), channel_id=1, source_target_pairs={{0,64},{64,0},{4,68},{68,4},{8,72},{72,8},{12,76},{76,12},{16,80},... | collective-permute-start | bytes 1769480 | tf_op jit(solution)/shard_map/ppermute | solution.py:61
  69.6 25.4 %copy-start = (bf16[32,1152]{1,0:T(8,128)(2,1)S(1)}, bf16[32,1152]{1,0:T(8,128)(2,1)}, u32[]{:S(2)}) copy-start(bf16[32,1152]{1,0:T(8,128)(2,1)} %image.1) | copy-start | bytes 221188
  69.7 25.4 %copy-start.1 = (bf16[32,1152]{1,0:T(8,128)(2,1)S(1)}, bf16[32,1152]{1,0:T(8,128)(2,1)}, u32[]{:S(2)}) copy-start(bf16[32,1152]{1,0:T(8,128)(2,1)} %text.1) | copy-start | bytes 221188

commit v8 on v7

--- a/solution.py
+++ b/solution.py
@@ -37,28 +37,25 @@
     ]
 
 
-def links(step, flip):
-    return [
-        (speaker(*line, ring + step, side ^ flip), speaker(*line, ring, side))
+NEIGHBOURS = (
+    lambda ring, side: (ring ^ 1, side),
+    lambda ring, side: (((ring + 1) ^ 1) - 1, side),
+    lambda ring, side: (ring, 1 - side),
+)
+
+
+def swap_with(block, neighbour):
+    pairs = [
+        (speaker(*line, *neighbour(ring, side)), speaker(*line, ring, side))
         for line in lines()
         for ring in range(RING)
         for side in (0, 1)
     ]
-
-
-NEIGHBOURS = ((1, 0), (-1, 0), (0, 1))
+    return lax.ppermute(block, NAMES, pairs)
 
 
 def exchange(blocks):
     return lax.all_to_all(blocks, NAMES, 0, 0, axis_index_groups=color_groups(), tiled=False)
-
-
-def take(block, neighbour):
-    return lax.ppermute(block, NAMES, links(*neighbour))
-
-
-def give(block, neighbour):
-    return lax.ppermute(block, NAMES, [(here, there) for there, here in links(*neighbour)])
 
 
 def swap_cores(block):
@@ -112,7 +109,9 @@
     member = (index >> (bits + 1)) & (COLORS - 1)
     chunk = index >> (bits + 3)
     side = member >> 1
-    color = (place + (chunk ^ (chunk >> 1))) & (COLORS - 1)
+    odd = jnp.where(is_text, lax.axis_index("y") & 1, lax.axis_index("zl"))
+    step = chunk ^ (chunk >> 1)
+    color = (place + step + ((odd * step) & 1) * 2) & (COLORS - 1)
     ring = (color + ((member & 1) << 2) + (side << 1)) & (RING - 1)
     slot = (index >> bits) & 1
     return first + per_side * side + per_slot * slot + per_ring * ring + (index & (rows - 1))
@@ -121,24 +120,41 @@
 LOG2_E = 1.4426950408889634
 
 
-def tile_kernel(rows, chunks, scalars, *refs):
-    mine, theirs, grads = refs[: len(chunks)], refs[len(chunks)], refs[len(chunks) + 1 :]
+def weigh(rows, scalars, mine, here_start, theirs, there_start):
     speaks_text = lax.axis_index("c") == 0
     slope, offset = -LOG2_E * scalars[0:1, 0:1], -LOG2_E * scalars[0:1, 1:2]
-    part, total = mine[0].shape[0], theirs.shape[0]
+    scores = lax.dot_general(mine, theirs, (((1,), (1,)), ((), ())), preferred_element_type=jnp.float32)
+    here_ids = global_rows(
+        here_start + lax.broadcasted_iota(jnp.int32, (mine.shape[0], 1), 0), speaks_text, rows
+    )
     there_ids = global_rows(
-        lax.broadcasted_iota(jnp.int32, (1, total), 1), jnp.logical_not(speaks_text), rows
-    )
-
-    def weigh(k):
-        scores = lax.dot_general(
-            mine[k][...], theirs[...], (((1,), (1,)), ((), ())), preferred_element_type=jnp.float32
-        )
-        here_ids = global_rows(
-            chunks[k] * part + lax.broadcasted_iota(jnp.int32, (part, 1), 0), speaks_text, rows
-        )
-        match = jnp.where(here_ids == there_ids, 1.0, 0.0)
-        return (1.0 / (1.0 + jnp.exp2(scores * slope + offset)) - match).astype(jnp.bfloat16)
+        there_start + lax.broadcasted_iota(jnp.int32, (1, theirs.shape[0]), 1),
+        jnp.logical_not(speaks_text),
+        rows,
+    )
+    match = jnp.where(here_ids == there_ids, 1.0, 0.0)
+    return (1.0 / (1.0 + jnp.exp2(scores * slope + offset)) - match).astype(jnp.bfloat16)
+
+
+def weigh_kernel(rows, chunks, count, scalars, *refs):
+    mine, theirs, weights = refs[: len(chunks)], refs[len(chunks) : -len(chunks)], refs[-len(chunks) :]
+    part = mine[0].shape[0]
+    for k in range(len(chunks)):
+        for j in range(count):
+            weights[k][:, j * part : (j + 1) * part] = weigh(
+                rows, scalars, mine[k][...], chunks[k] * part, theirs[j][...], j * part
+            )
+
+
+def tile_kernel(rows, chunks, early, scalars, *refs):
+    count = len(chunks)
+    mine, ready, theirs, grads = refs[:count], refs[count : -count - 1], refs[-count - 1], refs[-count:]
+    part = mine[0].shape[0]
+    done = early * part
+
+    def weights_of(k):
+        late = weigh(rows, scalars, mine[k][...], chunks[k] * part, theirs[done:, :], done)
+        return jnp.concatenate([ready[k][...], late], axis=1) if early else late
 
     def finish(k, weights):
         grads[k][...] = jnp.dot(weights, theirs[...], preferred_element_type=jnp.float32).astype(
@@ -146,12 +162,12 @@
         )
 
     before = None
-    for k in range(len(chunks)):
-        weights = weigh(k)
+    for k in range(count):
+        weights = weights_of(k)
         if k > 0:
             finish(k - 1, before)
         before = weights
-    finish(len(chunks) - 1, before)
+    finish(count - 1, before)
 
 
 def sum_kernel(parts, own, other):
@@ -193,30 +209,46 @@
         name="spread",
     )(kept, pair)
     own = exchange(copies).reshape(part, width)
-    mine = [own] + [take(own, neighbour) for neighbour in NEIGHBOURS]
-    theirs = [swap_cores(chunk) for chunk in mine]
-    theirs = jnp.concatenate(theirs, axis=0)
-
-    def tile(chunks, dtype):
-        count = len(chunks)
+    mine = [own] + [swap_with(own, neighbour) for neighbour in NEIGHBOURS]
+    chunks = [swap_cores(chunk) for chunk in mine]
+    theirs = jnp.concatenate(chunks, axis=0)
+    near, early = (1, 2, 3), 3
+
+    def call(kernel, out_shape, operands, products, name):
         return pl.pallas_call(
-            lambda *refs: tile_kernel(rows, chunks, *refs),
-            out_shape=[jax.ShapeDtypeStruct((part, width), dtype)] * count,
-            in_specs=[VMEM] * (count + 2),
-            out_specs=[VMEM] * count,
+            kernel,
+            out_shape=out_shape,
+            in_specs=[VMEM] * len(operands),
+            out_specs=[VMEM] * len(out_shape),
             compiler_params=LARGE,
             cost_estimate=pl.CostEstimate(
-                flops=4 * count * part * total * width,
-                bytes_accessed=2 * (total + 2 * count * part) * width,
-                transcendentals=count * part * total,
+                flops=2 * products * part * part * width,
+                bytes_accessed=2 * sum(operand.size for operand in operands),
+                transcendentals=products * part * part // 2,
             ),
-            name="tile",
-        )(scalars, *[mine[chunk] for chunk in chunks], theirs)
-
+            name=name,
+        )(*operands)
+
+    def tile(rows_of, ready, dtype):
+        return call(
+            lambda *refs: tile_kernel(rows, rows_of, early if ready else 0, *refs),
+            [jax.ShapeDtypeStruct((part, width), dtype)] * len(rows_of),
+            [scalars, *[mine[chunk] for chunk in rows_of], *ready, theirs],
+            len(rows_of) * (8 - (early if ready else 0)),
+            "tile",
+        )
+
+    ready = call(
+        lambda *refs: weigh_kernel(rows, near, early, *refs),
+        [jax.ShapeDtypeStruct((part, early * part), jnp.bfloat16)] * len(near),
+        [scalars, *[mine[chunk] for chunk in near], *chunks[:early]],
+        len(near) * early,
+        "weigh",
+    )
     partial = [
-        give(block, neighbour) for block, neighbour in zip(tile((1, 2, 3), jnp.bfloat16), NEIGHBOURS)
+        swap_with(block, neighbour) for block, neighbour in zip(tile(near, ready, jnp.bfloat16), NEIGHBOURS)
     ]
-    (summed,) = tile((0,), jnp.float32)
+    (summed,) = tile((0,), [], jnp.float32)
     for block in partial:
         summed = summed + block.astype(jnp.float32)
     parts = exchange(summed.astype(jnp.bfloat16).reshape(COLORS, 2 * rows, width))

time: 96.5 us -> 95.1 us (0.985)
  blocking collectives: 47.4 us -> 44.9 us
    all_to_all x2, blocking collectives: 37 us -> 34.4 us  [exchange(): lax.all_to_all(blocks, NAMES, 0, 0, axis_index_groups=color_groups(), til...]
    ppermute x6, waiting for transfers between devices: 7.49 us -> 9.29 us  [swap_with(): return lax.ppermute(block, NAMES, pairs)]
    ppermute x4, waiting for transfers between devices: 1.74 us -> 0.01 us  [swap_cores(): return lax.ppermute(block, 'c', [(0, 1), (1, 0)])]
    pallas_call x2 -> x3, Pallas kernels: 6.04 us -> 6.32 us  [call(): pl.pallas_call(kernel, out_shape=out_shape, in_specs=[VMEM] * len(operand...]
  transfers between devices with their start and end apart: 10 -> 10, of which waited for: 5 -> 4; matrix products, arithmetic and copies ran while one was open for 0% -> 0% of each run, Pallas kernels for 2% -> 4%
where the time goes in v8:
time: 95.1 us; the launch traced here: 94.1 us
  blocking collectives  44.9 us (47%)
  starting transfers between devices  28.7 us (30%)
  waiting for transfers between devices  9.3 us (10%)
  Pallas kernels  7.47 us (8%)
  between operations  2.13 us (2%)
  other arithmetic  1.32 us (1%)
    all_to_all x2, blocking collectives, exchange(): lax.all_to_all(blocks, NAMES, 0, 0, axis_index_groups=color_groups(), til...  34.4 us
    ppermute x6, starting transfers between devices, swap_with(): return lax.ppermute(block, NAMES, pairs)  20.4 us
    all_gather x2, blocking collectives, gather_cores(): return lax.all_gather(block, 'c', axis=0, tiled=True)  10.5 us
    ppermute x6, waiting for transfers between devices, swap_with(): return lax.ppermute(block, NAMES, pairs)  9.29 us
    ppermute x4, starting transfers between devices, swap_cores(): return lax.ppermute(block, 'c', [(0, 1), (1, 0)])  8.36 us
    pallas_call x3, Pallas kernels, call(): pl.pallas_call(kernel, out_shape=out_shape, in_specs=[VMEM] * len(operand...  6.32 us
  transfers between devices with their start and end apart: 10, of which 4 were waited for; matrix products, arithmetic and copies ran while one was open for 0% of the time, Pallas kernels for 4%

profile of v8, /device:TPU:1, one launch (start us, length us, event | category | flops | bytes accessed | tf_op | source)
XLA Modules:
  0.0 94.1 jit_solution(10388010647075648136)
XLA Ops:
  0.6 0.9 %broadcast_select_fusion = (bf16[32,1152]{1,0:T(8,128)(2,1)S(1)}, bf16[32,1152]{1,0:T(8,128)(2,1)S(1)}) fusion(bf16[32,1152]{1,0:T(8,128)(2,1)} %image.1, bf16[32,1152]{1,0:T(8,128)(2,1)} %text.1, pred[]{:T(512)S(6)} %eq.3), kind=kLoop, calls=%fused_computation.1 | loop fusion | flops 73728 | bytes 294913 | tf_op jit(solution)/shard_map/jit(_where)/select_n | solution.py:202
  1.6 8.4 %all_gather.6.pair = bf16[64,1152]{1,0:T(8,128)(2,1)S(1)} all-gather(bf16[32,1152]{1,0:T(8,128)(2,1)S(1)} %get-tuple-element.18), channel_id=1, replica_groups=mesh['zl'=2,'xh'=2,'xl'=2,'c'=2,'y'=8,'zh'=4] {'c'}, dimensions={0}, use_global_device_ids=true | all-gather | bytes 221184 | tf_op jit(solution)/shard_map/all_gather | solution.py:66
  10.0 0.1 spread.1
  10.2 19.6 %all_to_all.10 = bf16[4,64,1152]{2,1,0:T(8,128)(2,1)S(1)} all-to-all(bf16[4,64,1152]{2,1,0:T(8,128)(2,1)S(1)} %spread.1), channel_id=1, replica_groups={{0,16,72,88},{4,20,76,92},{8,24,80,64},{12,28,84,68},{128,144,200,216},..., dimensions={0} | all-to-all | bytes 1179648 | tf_op jit(solution)/shard_map/all_to_all | solution.py:58
  29.8 2.8 %collective-permute-start.1 = (bf16[256,1152]{1,0:T(8,128)(2,1)S(1)}, bf16[256,1152]{1,0:T(8,128)(2,1)S(1)}, u32[]{:S(2)}, u32[]{:S(2)}) collective-permute-start(bf16[256,1152]{1,0:T(8,128)(2,1)S(1)} %bitcast.4), channel_id=1, source_target_pairs={{4,0},{68,64},{0,4},{64,68},{12,8},{76,72},{8,12},{72,76},{20,16},... | collective-permute-start | bytes 1769480 | tf_op jit(solution)/shard_map/ppermute | solution.py:54
  32.6 1.9 %collective-permute-start.3 = (bf16[256,1152]{1,0:T(8,128)(2,1)S(1)}, bf16[256,1152]{1,0:T(8,128)(2,1)S(1)}, u32[]{:S(2)}, u32[]{:S(2)}) collective-permute-start(bf16[256,1152]{1,0:T(8,128)(2,1)S(1)} %bitcast.5), channel_id=1, source_target_pairs={{28,0},{92,64},{8,4},{72,68},{4,8},{68,72},{16,12},{80,76},{12,16}... | collective-permute-start | bytes 1769480 | tf_op jit(solution)/shard_map/ppermute | solution.py:54
  34.5 3.9 %collective-permute-start.5 = (bf16[256,1152]{1,0:T(8,128)(2,1)S(1)}, bf16[256,1152]{1,0:T(8,128)(2,1)S(1)}, u32[]{:S(2)}, u32[]{:S(2)}) collective-permute-start(bf16[256,1152]{1,0:T(8,128)(2,1)S(1)} %bitcast.6), channel_id=1, source_target_pairs={{64,0},{0,64},{68,4},{4,68},{72,8},{8,72},{76,12},{12,76},{80,16},... | collective-permute-start | bytes 1769480 | tf_op jit(solution)/shard_map/ppermute | solution.py:54
  38.5 1.9 %collective-permute-start = (bf16[256,1152]{1,0:T(8,128)(2,1)S(1)}, bf16[256,1152]{1,0:T(8,128)(2,1)S(1)}, u32[]{:S(2)}, u32[]{:S(2)}) collective-permute-start(bf16[256,1152]{1,0:T(8,128)(2,1)S(1)} %bitcast.7), channel_id=1, source_target_pairs={{0,32},{32,0},{1,33},{33,1},{2,34},{34,2},{3,35},{35,3},{4,36},{36... | collective-permute-start | bytes 1769480 | tf_op jit(solution)/shard_map/ppermute | solution.py:62
  40.4 0.3 collective-permute-done.1.refs_1_
  40.7 2.1 %collective-permute-start.2 = (bf16[256,1152]{1,0:T(8,128)(2,1)S(1)}, bf16[256,1152]{1,0:T(8,128)(2,1)S(1)}, u32[]{:S(2)}, u32[]{:S(2)}) collective-permute-start(bf16[256,1152]{1,0:T(8,128)(2,1)S(1)} %collective-permute-done.1.refs_1_), channel_id=1, source_target_pairs={{0,32},{32,0},{1,33},{33,1},{2,34},{34,2},{3,35},{35,3},{4,36},{36... | collective-permute-start | bytes 1769480 | tf_op jit(solution)/shard_map/ppermute | solution.py:62
  42.8 1.6 %collective-permute-done.3.refs_2_ = bf16[256,1152]{1,0:T(8,128)(2,1)S(1)} collective-permute-done((bf16[256,1152]{1,0:T(8,128)(2,1)S(1)}, bf16[256,1152]{1,0:T(8,128)(2,1)S(1)}, u32[]{:S(2)}, u32[]{:S(2)}) %collective-permute-start.3) | collective-permute-done | bytes 589856 | tf_op jit(solution)/shard_map/ppermute | solution.py:54
  44.4 1.9 %collective-permute-start.4 = (bf16[256,1152]{1,0:T(8,128)(2,1)S(1)}, bf16[256,1152]{1,0:T(8,128)(2,1)S(1)}, u32[]{:S(2)}, u32[]{:S(2)}) collective-permute-start(bf16[256,1152]{1,0:T(8,128)(2,1)S(1)} %collective-permute-done.3.refs_2_), channel_id=1, source_target_pairs={{0,32},{32,0},{1,33},{33,1},{2,34},{34,2},{3,35},{35,3},{4,36},{36... | collective-permute-start | bytes 1769480 | tf_op jit(solution)/shard_map/ppermute | solution.py:62
  47.6 0.1 maximum_bitcast_fusion.refs_0_.scalars
  47.7 0.0 collective-permute-done.5.refs_3_
  47.7 2.4 %collective-permute-start.6 = (bf16[256,1152]{1,0:T(8,128)(2,1)S(1)}, bf16[256,1152]{1,0:T(8,128)(2,1)S(1)}, u32[]{:S(2)}, u32[]{:S(2)}) collective-permute-start(bf16[256,1152]{1,0:T(8,128)(2,1)S(1)} %collective-permute-done.5.refs_3_), channel_id=1, source_target_pairs={{0,32},{32,0},{1,33},{33,1},{2,34},{34,2},{3,35},{35,3},{4,36},{36... | collective-permute-start | bytes 1769480 | tf_op jit(solution)/shard_map/ppermute | solution.py:62
  50.1 0.0 collective-permute-done.refs_4_
  50.2 0.0 collective-permute-done.2.refs_5_
  50.2 0.0 collective-permute-done.4.refs_6_
  50.2 2.0 %weigh.1 = (bf16[256,768]{1,0:T(8,128)(2,1)S(1)}, bf16[256,768]{1,0:T(8,128)(2,1)S(1)}, bf16[256,768]{1,0:T(8,128)(2,1)S(1)}) custom-call(f32[1,2]{1,0:T(1,128)S(1)} %maximum_bitcast_fusion.refs_0_.scalars, bf16[256,1152]{1,0:T(8,128)(2,1)S(1)} %collective-permute-done.1.refs_1_, bf16[256,1152]{1,0:T(8,128)(2,1)S(1)} %collective-permute-done.3.refs_2_, ...), custom_call_target="tpu_custom_call" | custom-call | flops 1358954496 | bytes 3538948 | tf_op jit(solution)/shard_map/weigh/pallas_call | solution.py:218
  52.2 0.1 constant_dynamic-update-slice_fusion.2
  52.2 0.1 constant_dynamic-update-slice_fusion.1
  52.3 0.0 collective-permute-done.6
  52.3 0.1 constant_dynamic-update-slice_fusion.refs_2_.refs_7_
  52.4 2.8 %tile.3 = (bf16[256,1152]{1,0:T(8,128)(2,1)S(1)}, bf16[256,1152]{1,0:T(8,128)(2,1)S(1)}, bf16[256,1152]{1,0:T(8,128)(2,1)S(1)}) custom-call(f32[1,2]{1,0:T(1,128)S(1)} %maximum_bitcast_fusion.refs_0_.scalars, bf16[256,1152]{1,0:T(8,128)(2,1)S(1)} %collective-permute-done.1.refs_1_, bf16[256,1152]{1,0:T(8,128)(2,1)S(1)} %collective-permute-done.3.refs_2_, ...), custom_call_target="tpu_custom_call" | custom-call | flops 2264924160 | bytes 5308420 | tf_op jit(solution)/shard_map/tile/pallas_call | solution.py:218
  55.2 1.9 %collective-permute-start.7 = (bf16[256,1152]{1,0:T(8,128)(2,1)S(1)}, bf16[256,1152]{1,0:T(8,128)(2,1)S(1)}, u32[]{:S(2)}, u32[]{:S(2)}) collective-permute-start(bf16[256,1152]{1,0:T(8,128)(2,1)S(1)} %get-tuple-element.13), channel_id=1, source_target_pairs={{4,0},{68,64},{0,4},{64,68},{12,8},{76,72},{8,12},{72,76},{20,16},... | collective-permute-start | bytes 1769480 | tf_op jit(solution)/shard_map/ppermute | solution.py:54
  57.1 7.0 %collective-permute-start.8 = (bf16[256,1152]{1,0:T(8,128)(2,1)S(1)}, bf16[256,1152]{1,0:T(8,128)(2,1)S(1)}, u32[]{:S(2)}, u32[]{:S(2)}) collective-permute-start(bf16[256,1152]{1,0:T(8,128)(2,1)S(1)} %get-tuple-element.14), channel_id=1, source_target_pairs={{28,0},{92,64},{8,4},{72,68},{4,8},{68,72},{16,12},{80,76},{12,16}... | collective-permute-start | bytes 1769480 | tf_op jit(solution)/shard_map/ppermute | solution.py:54
  64.1 2.8 %collective-permute-start.9 = (bf16[256,1152]{1,0:T(8,128)(2,1)S(1)}, bf16[256,1152]{1,0:T(8,128)(2,1)S(1)}, u32[]{:S(2)}, u32[]{:S(2)}) collective-permute-start(bf16[256,1152]{1,0:T(8,128)(2,1)S(1)} %get-tuple-element.15), channel_id=1, source_target_pairs={{64,0},{0,64},{68,4},{4,68},{72,8},{8,72},{76,12},{12,76},{80,16},... | collective-permute-start | bytes 1769480 | tf_op jit(solution)/shard_map/ppermute | solution.py:54
  66.9 1.6 %tile.2 = f32[256,1152]{1,0:T(8,128)S(1)} custom-call(f32[1,2]{1,0:T(1,128)S(1)} %maximum_bitcast_fusion.refs_0_.scalars, bf16[256,1152]{1,0:T(8,128)(2,1)S(1)} %bitcast.8, bf16[1024,1152]{1,0:T(8,128)(2,1)S(1)} %constant_dynamic-update-slice_fusion.refs_2_.refs_7_), custom_call_target="tpu_custom_call" | custom-call | flops 1207959552 | bytes 2949124 | tf_op jit(solution)/shard_map/tile/pallas_call | solution.py:218
  68.5 0.0 copy-start
  68.5 0.0 copy-start.1
  68.5 0.0 collective-permute-done.7
  68.5 2.8 %collective-permute-done.8 = bf16[256,1152]{1,0:T(8,128)(2,1)S(1)} collective-permute-done((bf16[256,1152]{1,0:T(8,128)(2,1)S(1)}, bf16[256,1152]{1,0:T(8,128)(2,1)S(1)}, u32[]{:S(2)}, u32[]{:S(2)}) %collective-permute-start.8) | collective-permute-done | bytes 589856 | tf_op jit(solution)/shard_map/ppermute | solution.py:54
  71.4 4.6 %collective-permute-done.9 = bf16[256,1152]{1,0:T(8,128)(2,1)S(1)} collective-permute-done((bf16[256,1152]{1,0:T(8,128)(2,1)S(1)}, bf16[256,1152]{1,0:T(8,128)(2,1)S(1)}, u32[]{:S(2)}, u32[]{:S(2)}) %collective-permute-start.9) | collective-permute-done | bytes 589856 | tf_op jit(solution)/shard_map/ppermute | solution.py:54
  75.9 0.3 add_convert_fusion
  76.2 14.8 %all_to_all.11.parts = bf16[4,64,1152]{2,1,0:T(8,128)(2,1)S(1)} all-to-all(bf16[4,64,1152]{2,1,0:T(8,128)(2,1)S(1)} %bitcast.9), channel_id=1, replica_groups={{0,16,72,88},{4,20,76,92},{8,24,80,64},{12,28,84,68},{128,144,200,216},..., dimensions={0} | all-to-all | bytes 1179648 | tf_op jit(solution)/shard_map/all_to_all | solution.py:58
  91.1 0.1 sum.1
  91.1 2.0 %all_gather.7.pair = f32[64,1152]{1,0:T(8,128)S(1)} all-gather(f32[32,1152]{1,0:T(8,128)S(1)} %get-tuple-element.17), channel_id=1, replica_groups=mesh['zl'=2,'xh'=2,'xl'=2,'c'=2,'y'=8,'zh'=4] {'c'}, dimensions={0}, use_global_device_ids=true | all-gather | bytes 442368 | tf_op jit(solution)/shard_map/all_gather | solution.py:66
  93.1 0.0 copy-done
  93.1 0.0 copy-done.1
  93.1 0.9 %finish.1 = (f32[32,1152]{1,0:T(8,128)}, f32[32,1152]{1,0:T(8,128)}) custom-call(f32[1,2]{1,0:T(1,128)S(1)} %maximum_bitcast_fusion.refs_0_.scalars, f32[32,1152]{1,0:T(8,128)S(1)} %get-tuple-element.16.summed, f32[64,1152]{1,0:T(8,128)S(1)} %all_gather.7.pair, bf16[32,1152]{1,0:T(8,128)(2,1)S(1)} %copy-done, bf16[32,1152]{1,0:T(8,128)(2,1)S(1)} %copy-done.1), custom_call_target="tpu_custom_call" | custom-call | tf_op jit(solution)/shard_map/finish/pallas_call | solution.py:264
  (1 shorter events, 0.0 us)
Async XLA Ops:
  29.8 10.9 %collective-permute-start.1 = (bf16[256,1152]{1,0:T(8,128)(2,1)S(1)}, bf16[256,1152]{1,0:T(8,128)(2,1)S(1)}, u32[]{:S(2)}, u32[]{:S(2)}) collective-permute-start(bf16[256,1152]{1,0:T(8,128)(2,1)S(1)} %bitcast.4), channel_id=1, source_target_pairs={{4,0},{68,64},{0,4},{64,68},{12,8},{76,72},{8,12},{72,76},{20,16},... | collective-permute-start | bytes 1769480 | tf_op jit(solution)/shard_map/ppermute | solution.py:54
  32.6 11.8 %collective-permute-start.3 = (bf16[256,1152]{1,0:T(8,128)(2,1)S(1)}, bf16[256,1152]{1,0:T(8,128)(2,1)S(1)}, u32[]{:S(2)}, u32[]{:S(2)}) collective-permute-start(bf16[256,1152]{1,0:T(8,128)(2,1)S(1)} %bitcast.5), channel_id=1, source_target_pairs={{28,0},{92,64},{8,4},{72,68},{4,8},{68,72},{16,12},{80,76},{12,16}... | collective-permute-start | bytes 1769480 | tf_op jit(solution)/shard_map/ppermute | solution.py:54
  34.5 13.2 %collective-permute-start.5 = (bf16[256,1152]{1,0:T(8,128)(2,1)S(1)}, bf16[256,1152]{1,0:T(8,128)(2,1)S(1)}, u32[]{:S(2)}, u32[]{:S(2)}) collective-permute-start(bf16[256,1152]{1,0:T(8,128)(2,1)S(1)} %bitcast.6), channel_id=1, source_target_pairs={{64,0},{0,64},{68,4},{4,68},{72,8},{8,72},{76,12},{12,76},{80,16},... | collective-permute-start | bytes 1769480 | tf_op jit(solution)/shard_map/ppermute | solution.py:54
  38.5 11.7 %collective-permute-start = (bf16[256,1152]{1,0:T(8,128)(2,1)S(1)}, bf16[256,1152]{1,0:T(8,128)(2,1)S(1)}, u32[]{:S(2)}, u32[]{:S(2)}) collective-permute-start(bf16[256,1152]{1,0:T(8,128)(2,1)S(1)} %bitcast.7), channel_id=1, source_target_pairs={{0,32},{32,0},{1,33},{33,1},{2,34},{34,2},{3,35},{35,3},{4,36},{36... | collective-permute-start | bytes 1769480 | tf_op jit(solution)/shard_map/ppermute | solution.py:62
  40.7 9.5 %collective-permute-start.2 = (bf16[256,1152]{1,0:T(8,128)(2,1)S(1)}, bf16[256,1152]{1,0:T(8,128)(2,1)S(1)}, u32[]{:S(2)}, u32[]{:S(2)}) collective-permute-start(bf16[256,1152]{1,0:T(8,128)(2,1)S(1)} %collective-permute-done.1.refs_1_), channel_id=1, source_target_pairs={{0,32},{32,0},{1,33},{33,1},{2,34},{34,2},{3,35},{35,3},{4,36},{36... | collective-permute-start | bytes 1769480 | tf_op jit(solution)/shard_map/ppermute | solution.py:62
  44.4 5.8 %collective-permute-start.4 = (bf16[256,1152]{1,0:T(8,128)(2,1)S(1)}, bf16[256,1152]{1,0:T(8,128)(2,1)S(1)}, u32[]{:S(2)}, u32[]{:S(2)}) collective-permute-start(bf16[256,1152]{1,0:T(8,128)(2,1)S(1)} %collective-permute-done.3.refs_2_), channel_id=1, source_target_pairs={{0,32},{32,0},{1,33},{33,1},{2,34},{34,2},{3,35},{35,3},{4,36},{36... | collective-permute-start | bytes 1769480 | tf_op jit(solution)/shard_map/ppermute | solution.py:62
  47.7 4.6 %collective-permute-start.6 = (bf16[256,1152]{1,0:T(8,128)(2,1)S(1)}, bf16[256,1152]{1,0:T(8,128)(2,1)S(1)}, u32[]{:S(2)}, u32[]{:S(2)}) collective-permute-start(bf16[256,1152]{1,0:T(8,128)(2,1)S(1)} %collective-permute-done.5.refs_3_), channel_id=1, source_target_pairs={{0,32},{32,0},{1,33},{33,1},{2,34},{34,2},{3,35},{35,3},{4,36},{36... | collective-permute-start | bytes 1769480 | tf_op jit(solution)/shard_map/ppermute | solution.py:62
  55.2 13.4 %collective-permute-start.7 = (bf16[256,1152]{1,0:T(8,128)(2,1)S(1)}, bf16[256,1152]{1,0:T(8,128)(2,1)S(1)}, u32[]{:S(2)}, u32[]{:S(2)}) collective-permute-start(bf16[256,1152]{1,0:T(8,128)(2,1)S(1)} %get-tuple-element.13), channel_id=1, source_target_pairs={{4,0},{68,64},{0,4},{64,68},{12,8},{76,72},{8,12},{72,76},{20,16},... | collective-permute-start | bytes 1769480 | tf_op jit(solution)/shard_map/ppermute | solution.py:54
  57.1 14.3 %collective-permute-start.8 = (bf16[256,1152]{1,0:T(8,128)(2,1)S(1)}, bf16[256,1152]{1,0:T(8,128)(2,1)S(1)}, u32[]{:S(2)}, u32[]{:S(2)}) collective-permute-start(bf16[256,1152]{1,0:T(8,128)(2,1)S(1)} %get-tuple-element.14), channel_id=1, source_target_pairs={{28,0},{92,64},{8,4},{72,68},{4,8},{68,72},{16,12},{80,76},{12,16}... | collective-permute-start | bytes 1769480 | tf_op jit(solution)/shard_map/ppermute | solution.py:54
  64.1 11.8 %collective-permute-start.9 = (bf16[256,1152]{1,0:T(8,128)(2,1)S(1)}, bf16[256,1152]{1,0:T(8,128)(2,1)S(1)}, u32[]{:S(2)}, u32[]{:S(2)}) collective-permute-start(bf16[256,1152]{1,0:T(8,128)(2,1)S(1)} %get-tuple-element.15), channel_id=1, source_target_pairs={{64,0},{0,64},{68,4},{4,68},{72,8},{8,72},{76,12},{12,76},{80,16},... | collective-permute-start | bytes 1769480 | tf_op jit(solution)/shard_map/ppermute | solution.py:54
  68.5 24.6 %copy-start = (bf16[32,1152]{1,0:T(8,128)(2,1)S(1)}, bf16[32,1152]{1,0:T(8,128)(2,1)}, u32[]{:S(2)}) copy-start(bf16[32,1152]{1,0:T(8,128)(2,1)} %image.1) | copy-start | bytes 221188
  68.5 24.6 %copy-start.1 = (bf16[32,1152]{1,0:T(8,128)(2,1)S(1)}, bf16[32,1152]{1,0:T(8,128)(2,1)}, u32[]{:S(2)}) copy-start(bf16[32,1152]{1,0:T(8,128)(2,1)} %text.1) | copy-start | bytes 221188

commit v9 on v8

--- a/solution.py
+++ b/solution.py
@@ -170,10 +170,40 @@
     finish(count - 1, before)
 
 
-def sum_kernel(parts, own, other):
+def own_member(flip):
+    speaks_text = lax.axis_index("c") == 0
+    ring = jnp.where(speaks_text, lax.axis_index("y"), lax.axis_index("zh") * 2 + lax.axis_index("zl"))
+    side = jnp.where(speaks_text, lax.axis_index("xl"), lax.axis_index("xh")) ^ flip
+    low = jnp.where(ring >= 4, 1, 0)
+    high = jnp.where(jnp.logical_and(ring >= 2, ring < 6), 2, 3)
+    return jnp.where(side == 0, low, high)
+
+
+def split_kernel(grad, head, tail):
+    size = head.shape[0]
+    member = own_member(1)
+    head[...] = grad[pl.ds(pl.multiple_of(member * size, size), size), :]
+    for j in range(1, COLORS):
+        start = pl.multiple_of((member ^ j) * size, size)
+        tail[(j - 1) * size : j * size, :] = grad[pl.ds(start, size), :]
+
+
+def merge_kernel(mine, first, second, tail, blocks):
+    size = blocks.shape[1]
+    member = own_member(0)
+    for j in range(COLORS):
+        place = pl.ds(pl.multiple_of((member ^ j) * size, size), size)
+        total = mine[place, :] + first[place, :].astype(jnp.float32) + second[place, :].astype(jnp.float32)
+        if j > 0:
+            total = total + tail[(j - 1) * size : j * size, :].astype(jnp.float32)
+        blocks[member ^ j] = total.astype(blocks.dtype)
+
+
+def sum_kernel(parts, head, own, other):
     rows = own.shape[0]
-    own[...] = jnp.sum(parts[:, :rows, :].astype(jnp.float32), axis=0)
-    other[...] = jnp.sum(parts[:, rows:, :].astype(jnp.float32), axis=0)
+    total = head[...].astype(jnp.float32) + jnp.sum(parts[...].astype(jnp.float32), axis=0)
+    own[...] = total[:rows, :]
+    other[...] = total[rows:, :]
 
 
 def finish_kernel(scalars, summed, pair, image, text, grad_image, grad_text):
@@ -245,22 +275,31 @@
         len(near) * early,
         "weigh",
     )
-    partial = [
-        swap_with(block, neighbour) for block, neighbour in zip(tile(near, ready, jnp.bfloat16), NEIGHBOURS)
+    size = 2 * rows
+
+    def small_call(kernel, out_shape, operands, name):
+        return pl.pallas_call(
+            kernel,
+            out_shape=out_shape,
+            in_specs=[VMEM] * len(operands),
+            out_specs=[VMEM] * len(out_shape),
+            compiler_params=SMALL,
+            name=name,
+        )(*operands)
+
+    def half(*shape):
+        return jax.ShapeDtypeStruct((*shape, width), jnp.bfloat16)
+
+    blocks = tile(near, ready, jnp.bfloat16)
+    late, tail = small_call(split_kernel, [half(size), half(part - size)], [blocks[2]], "split")
+    first, second, tail = [
+        swap_with(block, neighbour) for block, neighbour in zip((blocks[0], blocks[1], tail), NEIGHBOURS)
     ]
+    head = swap_with(late, NEIGHBOURS[2])
     (summed,) = tile((0,), [], jnp.float32)
-    for block in partial:
-        summed = summed + block.astype(jnp.float32)
-    parts = exchange(summed.astype(jnp.bfloat16).reshape(COLORS, 2 * rows, width))
+    (merged,) = small_call(merge_kernel, [half(COLORS, size)], [summed, first, second, tail], "merge")
     out = jax.ShapeDtypeStruct((rows, width), jnp.float32)
-    own, other = pl.pallas_call(
-        sum_kernel,
-        out_shape=(out, out),
-        in_specs=[VMEM],
-        out_specs=(VMEM, VMEM),
-        compiler_params=SMALL,
-        name="sum",
-    )(parts)
+    own, other = small_call(sum_kernel, [out, out], [exchange(merged), head], "sum")
     return pl.pallas_call(
         finish_kernel,
         out_shape=(out, out),

time: 95.1 us -> 94.5 us (level)
  blocking collectives: 44.9 us -> 30.8 us
  starting transfers between devices: 28.7 us -> 37.3 us
  waiting for transfers between devices: 9.3 us -> 13.4 us
  Pallas kernels: 7.47 us -> 8.64 us
    all_to_all x2 -> x1, blocking collectives: 34.4 us -> 19.6 us  [exchange(): lax.all_to_all(blocks, NAMES, 0, 0, axis_index_groups=color_groups(), til...]
    ppermute x6 -> x7, starting transfers between devices: 20.4 us -> 25.5 us  [swap_with(): return lax.ppermute(block, NAMES, pairs)]
    ppermute x6 -> x7, waiting for transfers between devices: 9.29 us -> 13.4 us  [swap_with(): return lax.ppermute(block, NAMES, pairs)]
    all_to_all x0 -> x1, starting transfers between devices: none -> 3.48 us  [exchange(): lax.all_to_all(blocks, NAMES, 0, 0, axis_index_groups=color_groups(), til...]
    pallas_call x1 -> x3, Pallas kernels: 0.07 us -> 1.24 us  [small_call(): pl.pallas_call(kernel, out_shape=out_shape, in_specs=[VMEM] * len(operand...]
  transfers between devices with their start and end apart: 10 -> 12, of which waited for: 4 -> 4; matrix products, arithmetic and copies ran while one was open for 0% -> 0% of each run, Pallas kernels for 4% -> 4%
where the time goes in v9:
time: 94.5 us; the launch traced here: 93.6 us
  starting transfers between devices  37.3 us (39%)
  blocking collectives  30.8 us (33%)
  waiting for transfers between devices  13.4 us (14%)
  Pallas kernels  8.64 us (9%)
  between operations  2.14 us (2%)
  other arithmetic  1.02 us (1%)
    ppermute x7, starting transfers between devices, swap_with(): return lax.ppermute(block, NAMES, pairs)  25.5 us
    all_to_all x1, blocking collectives, exchange(): lax.all_to_all(blocks, NAMES, 0, 0, axis_index_groups=color_groups(), til...  19.6 us
    ppermute x7, waiting for transfers between devices, swap_with(): return lax.ppermute(block, NAMES, pairs)  13.4 us
    all_gather x2, blocking collectives, gather_cores(): return lax.all_gather(block, 'c', axis=0, tiled=True)  11.2 us
    ppermute x4, starting transfers between devices, swap_cores(): return lax.ppermute(block, 'c', [(0, 1), (1, 0)])  8.36 us
    pallas_call x3, Pallas kernels, call(): pl.pallas_call(kernel, out_shape=out_shape, in_specs=[VMEM] * len(operand...  6.32 us
    all_to_all x1, starting transfers between devices, exchange(): lax.all_to_all(blocks, NAMES, 0, 0, axis_index_groups=color_groups(), til...  3.48 us
  transfers between devices with their start and end apart: 12, of which 4 were waited for; matrix products, arithmetic and copies ran while one was open for 0% of the time, Pallas kernels for 4%

profile of v9, /device:TPU:1, one launch (start us, length us, event | category | flops | bytes accessed | tf_op | source)
XLA Modules:
  0.0 93.6 jit_solution(52944635972526509)
XLA Ops:
  0.6 0.9 %broadcast_select_fusion = (bf16[32,1152]{1,0:T(8,128)(2,1)S(1)}, bf16[32,1152]{1,0:T(8,128)(2,1)S(1)}) fusion(bf16[32,1152]{1,0:T(8,128)(2,1)} %image.1, bf16[32,1152]{1,0:T(8,128)(2,1)} %text.1, pred[]{:T(512)S(6)} %eq.3), kind=kLoop, calls=%fused_computation | loop fusion | flops 73728 | bytes 294913 | tf_op jit(solution)/shard_map/jit(_where)/select_n | solution.py:232
  1.6 8.4 %all_gather.6.pair = bf16[64,1152]{1,0:T(8,128)(2,1)S(1)} all-gather(bf16[32,1152]{1,0:T(8,128)(2,1)S(1)} %get-tuple-element.22), channel_id=1, replica_groups=mesh['zl'=2,'xh'=2,'xl'=2,'c'=2,'y'=8,'zh'=4] {'c'}, dimensions={0}, use_global_device_ids=true | all-gather | bytes 221184 | tf_op jit(solution)/shard_map/all_gather | solution.py:66
  10.0 0.1 spread.1
  10.2 19.6 %all_to_all.10 = bf16[4,64,1152]{2,1,0:T(8,128)(2,1)S(1)} all-to-all(bf16[4,64,1152]{2,1,0:T(8,128)(2,1)S(1)} %spread.1), channel_id=1, replica_groups={{0,16,72,88},{4,20,76,92},{8,24,80,64},{12,28,84,68},{128,144,200,216},..., dimensions={0} | all-to-all | bytes 1179648 | tf_op jit(solution)/shard_map/all_to_all | solution.py:58
  29.8 2.8 %collective-permute-start.1 = (bf16[256,1152]{1,0:T(8,128)(2,1)S(1)}, bf16[256,1152]{1,0:T(8,128)(2,1)S(1)}, u32[]{:S(2)}, u32[]{:S(2)}) collective-permute-start(bf16[256,1152]{1,0:T(8,128)(2,1)S(1)} %bitcast.3), channel_id=1, source_target_pairs={{4,0},{68,64},{0,4},{64,68},{12,8},{76,72},{8,12},{72,76},{20,16},... | collective-permute-start | bytes 1769480 | tf_op jit(solution)/shard_map/ppermute | solution.py:54
  32.6 1.9 %collective-permute-start.3 = (bf16[256,1152]{1,0:T(8,128)(2,1)S(1)}, bf16[256,1152]{1,0:T(8,128)(2,1)S(1)}, u32[]{:S(2)}, u32[]{:S(2)}) collective-permute-start(bf16[256,1152]{1,0:T(8,128)(2,1)S(1)} %bitcast.4), channel_id=1, source_target_pairs={{28,0},{92,64},{8,4},{72,68},{4,8},{68,72},{16,12},{80,76},{12,16}... | collective-permute-start | bytes 1769480 | tf_op jit(solution)/shard_map/ppermute | solution.py:54
  34.5 3.9 %collective-permute-start.5 = (bf16[256,1152]{1,0:T(8,128)(2,1)S(1)}, bf16[256,1152]{1,0:T(8,128)(2,1)S(1)}, u32[]{:S(2)}, u32[]{:S(2)}) collective-permute-start(bf16[256,1152]{1,0:T(8,128)(2,1)S(1)} %bitcast.5), channel_id=1, source_target_pairs={{64,0},{0,64},{68,4},{4,68},{72,8},{8,72},{76,12},{12,76},{80,16},... | collective-permute-start | bytes 1769480 | tf_op jit(solution)/shard_map/ppermute | solution.py:54
  38.5 1.9 %collective-permute-start = (bf16[256,1152]{1,0:T(8,128)(2,1)S(1)}, bf16[256,1152]{1,0:T(8,128)(2,1)S(1)}, u32[]{:S(2)}, u32[]{:S(2)}) collective-permute-start(bf16[256,1152]{1,0:T(8,128)(2,1)S(1)} %bitcast.6), channel_id=1, source_target_pairs={{0,32},{32,0},{1,33},{33,1},{2,34},{34,2},{3,35},{35,3},{4,36},{36... | collective-permute-start | bytes 1769480 | tf_op jit(solution)/shard_map/ppermute | solution.py:62
  40.4 0.3 collective-permute-done.1.refs_1_
  40.7 2.1 %collective-permute-start.2 = (bf16[256,1152]{1,0:T(8,128)(2,1)S(1)}, bf16[256,1152]{1,0:T(8,128)(2,1)S(1)}, u32[]{:S(2)}, u32[]{:S(2)}) collective-permute-start(bf16[256,1152]{1,0:T(8,128)(2,1)S(1)} %collective-permute-done.1.refs_1_), channel_id=1, source_target_pairs={{0,32},{32,0},{1,33},{33,1},{2,34},{34,2},{3,35},{35,3},{4,36},{36... | collective-permute-start | bytes 1769480 | tf_op jit(solution)/shard_map/ppermute | solution.py:62
  42.8 1.6 %collective-permute-done.3.refs_2_ = bf16[256,1152]{1,0:T(8,128)(2,1)S(1)} collective-permute-done((bf16[256,1152]{1,0:T(8,128)(2,1)S(1)}, bf16[256,1152]{1,0:T(8,128)(2,1)S(1)}, u32[]{:S(2)}, u32[]{:S(2)}) %collective-permute-start.3) | collective-permute-done | bytes 589856 | tf_op jit(solution)/shard_map/ppermute | solution.py:54
  44.4 1.9 %collective-permute-start.4 = (bf16[256,1152]{1,0:T(8,128)(2,1)S(1)}, bf16[256,1152]{1,0:T(8,128)(2,1)S(1)}, u32[]{:S(2)}, u32[]{:S(2)}) collective-permute-start(bf16[256,1152]{1,0:T(8,128)(2,1)S(1)} %collective-permute-done.3.refs_2_), channel_id=1, source_target_pairs={{0,32},{32,0},{1,33},{33,1},{2,34},{34,2},{3,35},{35,3},{4,36},{36... | collective-permute-start | bytes 1769480 | tf_op jit(solution)/shard_map/ppermute | solution.py:62
  47.6 0.1 maximum_bitcast_fusion.refs_0_.scalars
  47.7 0.0 collective-permute-done.5.refs_3_
  47.7 2.4 %collective-permute-start.6 = (bf16[256,1152]{1,0:T(8,128)(2,1)S(1)}, bf16[256,1152]{1,0:T(8,128)(2,1)S(1)}, u32[]{:S(2)}, u32[]{:S(2)}) collective-permute-start(bf16[256,1152]{1,0:T(8,128)(2,1)S(1)} %collective-permute-done.5.refs_3_), channel_id=1, source_target_pairs={{0,32},{32,0},{1,33},{33,1},{2,34},{34,2},{3,35},{35,3},{4,36},{36... | collective-permute-start | bytes 1769480 | tf_op jit(solution)/shard_map/ppermute | solution.py:62
  50.1 0.0 collective-permute-done.refs_4_
  50.2 0.0 collective-permute-done.2.refs_5_
  50.2 0.0 collective-permute-done.4.refs_6_
  50.2 2.0 %weigh.1 = (bf16[256,768]{1,0:T(8,128)(2,1)S(1)}, bf16[256,768]{1,0:T(8,128)(2,1)S(1)}, bf16[256,768]{1,0:T(8,128)(2,1)S(1)}) custom-call(f32[1,2]{1,0:T(1,128)S(1)} %maximum_bitcast_fusion.refs_0_.scalars, bf16[256,1152]{1,0:T(8,128)(2,1)S(1)} %collective-permute-done.1.refs_1_, bf16[256,1152]{1,0:T(8,128)(2,1)S(1)} %collective-permute-done.3.refs_2_, ...), custom_call_target="tpu_custom_call" | custom-call | flops 1358954496 | bytes 3538948 | tf_op jit(solution)/shard_map/weigh/pallas_call | solution.py:248
  52.2 0.1 constant_dynamic-update-slice_fusion.2
  52.2 0.1 constant_dynamic-update-slice_fusion.1
  52.3 0.0 collective-permute-done.6
  52.3 0.1 constant_dynamic-update-slice_fusion.refs_2_.refs_7_
  52.4 2.8 %tile.3 = (bf16[256,1152]{1,0:T(8,128)(2,1)S(1)}, bf16[256,1152]{1,0:T(8,128)(2,1)S(1)}, bf16[256,1152]{1,0:T(8,128)(2,1)S(1)}) custom-call(f32[1,2]{1,0:T(1,128)S(1)} %maximum_bitcast_fusion.refs_0_.scalars, bf16[256,1152]{1,0:T(8,128)(2,1)S(1)} %collective-permute-done.1.refs_1_, bf16[256,1152]{1,0:T(8,128)(2,1)S(1)} %collective-permute-done.3.refs_2_, ...), custom_call_target="tpu_custom_call" | custom-call | flops 2264924160 | bytes 5308420 | tf_op jit(solution)/shard_map/tile/pallas_call | solution.py:248
  55.2 1.9 %collective-permute-start.7 = (bf16[256,1152]{1,0:T(8,128)(2,1)S(1)}, bf16[256,1152]{1,0:T(8,128)(2,1)S(1)}, u32[]{:S(2)}, u32[]{:S(2)}) collective-permute-start(bf16[256,1152]{1,0:T(8,128)(2,1)S(1)} %get-tuple-element.15), channel_id=1, source_target_pairs={{4,0},{68,64},{0,4},{64,68},{12,8},{76,72},{8,12},{72,76},{20,16},... | collective-permute-start | bytes 1769480 | tf_op jit(solution)/shard_map/ppermute | solution.py:54
  57.1 7.0 %collective-permute-start.8 = (bf16[256,1152]{1,0:T(8,128)(2,1)S(1)}, bf16[256,1152]{1,0:T(8,128)(2,1)S(1)}, u32[]{:S(2)}, u32[]{:S(2)}) collective-permute-start(bf16[256,1152]{1,0:T(8,128)(2,1)S(1)} %get-tuple-element.16), channel_id=1, source_target_pairs={{28,0},{92,64},{8,4},{72,68},{4,8},{68,72},{16,12},{80,76},{12,16}... | collective-permute-start | bytes 1769480 | tf_op jit(solution)/shard_map/ppermute | solution.py:54
  64.1 0.1 split.1
  64.2 2.8 %collective-permute-start.9 = (bf16[192,1152]{1,0:T(8,128)(2,1)S(1)}, bf16[192,1152]{1,0:T(8,128)(2,1)S(1)}, u32[]{:S(2)}, u32[]{:S(2)}) collective-permute-start(bf16[192,1152]{1,0:T(8,128)(2,1)S(1)} %get-tuple-element.18), channel_id=1, source_target_pairs={{64,0},{0,64},{68,4},{4,68},{72,8},{8,72},{76,12},{12,76},{80,16},... | collective-permute-start | bytes 1327112 | tf_op jit(solution)/shard_map/ppermute | solution.py:54
  67.0 1.6 %tile.2.mine = f32[256,1152]{1,0:T(8,128)S(1)} custom-call(f32[1,2]{1,0:T(1,128)S(1)} %maximum_bitcast_fusion.refs_0_.scalars, bf16[256,1152]{1,0:T(8,128)(2,1)S(1)} %bitcast.7, bf16[1024,1152]{1,0:T(8,128)(2,1)S(1)} %constant_dynamic-update-slice_fusion.refs_2_.refs_7_), custom_call_target="tpu_custom_call" | custom-call | flops 1207959552 | bytes 2949124 | tf_op jit(solution)/shard_map/tile/pallas_call | solution.py:248
  68.6 0.0 copy-start
  68.6 0.0 copy-start.1
  68.6 5.8 %collective-permute-done.9.tail = bf16[192,1152]{1,0:T(8,128)(2,1)S(1)} collective-permute-done((bf16[192,1152]{1,0:T(8,128)(2,1)S(1)}, bf16[192,1152]{1,0:T(8,128)(2,1)S(1)}, u32[]{:S(2)}, u32[]{:S(2)}) %collective-permute-start.9) | collective-permute-done | bytes 442400 | tf_op jit(solution)/shard_map/ppermute | solution.py:54
  74.4 0.0 collective-permute-done.7.first
  74.4 0.0 collective-permute-done.8.second
  74.4 1.1 %merge.1 = bf16[4,64,1152]{2,1,0:T(8,128)(2,1)} custom-call(f32[256,1152]{1,0:T(8,128)S(1)} %tile.2.mine, bf16[256,1152]{1,0:T(8,128)(2,1)S(1)} %collective-permute-done.7.first, bf16[256,1152]{1,0:T(8,128)(2,1)S(1)} %collective-permute-done.8.second, bf16[192,1152]{1,0:T(8,128)(2,1)S(1)} %collective-permute-done.9.tail), custom_call_target="tpu_custom_call" | custom-call | tf_op jit(solution)/shard_map/merge/pallas_call | solution.py:281
  75.5 3.5 %all-to-all-start.1 = ((bf16[4,64,1152]{2,1,0:T(8,128)(2,1)}), bf16[4,64,1152]{2,1,0:T(8,128)(2,1)S(1)}, u32[]{:S(2)}, u32[]{:S(2)}) async-start(bf16[4,64,1152]{2,1,0:T(8,128)(2,1)} %merge.1), calls=%async_computation.1 | async-start | bytes 1179648 | tf_op jit(solution)/shard_map/all_to_all | solution.py:58
  79.0 5.1 %collective-permute-start.10 = (bf16[64,1152]{1,0:T(8,128)(2,1)S(1)}, bf16[64,1152]{1,0:T(8,128)(2,1)S(1)}, u32[]{:S(2)}, u32[]{:S(2)}) collective-permute-start(bf16[64,1152]{1,0:T(8,128)(2,1)S(1)} %get-tuple-element.19), channel_id=1, source_target_pairs={{64,0},{0,64},{68,4},{4,68},{72,8},{8,72},{76,12},{12,76},{80,16},... | collective-permute-start | bytes 442376 | tf_op jit(solution)/shard_map/ppermute | solution.py:54
  84.1 5.6 %collective-permute-done.10.head = bf16[64,1152]{1,0:T(8,128)(2,1)S(1)} collective-permute-done((bf16[64,1152]{1,0:T(8,128)(2,1)S(1)}, bf16[64,1152]{1,0:T(8,128)(2,1)S(1)}, u32[]{:S(2)}, u32[]{:S(2)}) %collective-permute-start.10) | collective-permute-done | bytes 147488 | tf_op jit(solution)/shard_map/ppermute | solution.py:54
  89.7 0.0 all-to-all-done.1.parts
  89.7 0.1 sum.1
  89.8 2.8 %all_gather.7.pair = f32[64,1152]{1,0:T(8,128)S(1)} all-gather(f32[32,1152]{1,0:T(8,128)S(1)} %get-tuple-element.21), channel_id=1, replica_groups=mesh['zl'=2,'xh'=2,'xl'=2,'c'=2,'y'=8,'zh'=4] {'c'}, dimensions={0}, use_global_device_ids=true | all-gather | bytes 442368 | tf_op jit(solution)/shard_map/all_gather | solution.py:66
  92.6 0.0 copy-done
  92.6 0.0 copy-done.1
  92.6 0.9 %finish.1 = (f32[32,1152]{1,0:T(8,128)}, f32[32,1152]{1,0:T(8,128)}) custom-call(f32[1,2]{1,0:T(1,128)S(1)} %maximum_bitcast_fusion.refs_0_.scalars, f32[32,1152]{1,0:T(8,128)S(1)} %get-tuple-element.20.summed, f32[64,1152]{1,0:T(8,128)S(1)} %all_gather.7.pair, bf16[32,1152]{1,0:T(8,128)(2,1)S(1)} %copy-done, bf16[32,1152]{1,0:T(8,128)(2,1)S(1)} %copy-done.1), custom_call_target="tpu_custom_call" | custom-call | tf_op jit(solution)/shard_map/finish/pallas_call | solution.py:303
  (1 shorter events, 0.0 us)
Async XLA Ops:
  29.8 10.9 %collective-permute-start.1 = (bf16[256,1152]{1,0:T(8,128)(2,1)S(1)}, bf16[256,1152]{1,0:T(8,128)(2,1)S(1)}, u32[]{:S(2)}, u32[]{:S(2)}) collective-permute-start(bf16[256,1152]{1,0:T(8,128)(2,1)S(1)} %bitcast.3), channel_id=1, source_target_pairs={{4,0},{68,64},{0,4},{64,68},{12,8},{76,72},{8,12},{72,76},{20,16},... | collective-permute-start | bytes 1769480 | tf_op jit(solution)/shard_map/ppermute | solution.py:54
  32.6 11.8 %collective-permute-start.3 = (bf16[256,1152]{1,0:T(8,128)(2,1)S(1)}, bf16[256,1152]{1,0:T(8,128)(2,1)S(1)}, u32[]{:S(2)}, u32[]{:S(2)}) collective-permute-start(bf16[256,1152]{1,0:T(8,128)(2,1)S(1)} %bitcast.4), channel_id=1, source_target_pairs={{28,0},{92,64},{8,4},{72,68},{4,8},{68,72},{16,12},{80,76},{12,16}... | collective-permute-start | bytes 1769480 | tf_op jit(solution)/shard_map/ppermute | solution.py:54
  34.5 13.2 %collective-permute-start.5 = (bf16[256,1152]{1,0:T(8,128)(2,1)S(1)}, bf16[256,1152]{1,0:T(8,128)(2,1)S(1)}, u32[]{:S(2)}, u32[]{:S(2)}) collective-permute-start(bf16[256,1152]{1,0:T(8,128)(2,1)S(1)} %bitcast.5), channel_id=1, source_target_pairs={{64,0},{0,64},{68,4},{4,68},{72,8},{8,72},{76,12},{12,76},{80,16},... | collective-permute-start | bytes 1769480 | tf_op jit(solution)/shard_map/ppermute | solution.py:54
  38.5 11.7 %collective-permute-start = (bf16[256,1152]{1,0:T(8,128)(2,1)S(1)}, bf16[256,1152]{1,0:T(8,128)(2,1)S(1)}, u32[]{:S(2)}, u32[]{:S(2)}) collective-permute-start(bf16[256,1152]{1,0:T(8,128)(2,1)S(1)} %bitcast.6), channel_id=1, source_target_pairs={{0,32},{32,0},{1,33},{33,1},{2,34},{34,2},{3,35},{35,3},{4,36},{36... | collective-permute-start | bytes 1769480 | tf_op jit(solution)/shard_map/ppermute | solution.py:62
  40.7 9.5 %collective-permute-start.2 = (bf16[256,1152]{1,0:T(8,128)(2,1)S(1)}, bf16[256,1152]{1,0:T(8,128)(2,1)S(1)}, u32[]{:S(2)}, u32[]{:S(2)}) collective-permute-start(bf16[256,1152]{1,0:T(8,128)(2,1)S(1)} %collective-permute-done.1.refs_1_), channel_id=1, source_target_pairs={{0,32},{32,0},{1,33},{33,1},{2,34},{34,2},{3,35},{35,3},{4,36},{36... | collective-permute-start | bytes 1769480 | tf_op jit(solution)/shard_map/ppermute | solution.py:62
  44.4 5.8 %collective-permute-start.4 = (bf16[256,1152]{1,0:T(8,128)(2,1)S(1)}, bf16[256,1152]{1,0:T(8,128)(2,1)S(1)}, u32[]{:S(2)}, u32[]{:S(2)}) collective-permute-start(bf16[256,1152]{1,0:T(8,128)(2,1)S(1)} %collective-permute-done.3.refs_2_), channel_id=1, source_target_pairs={{0,32},{32,0},{1,33},{33,1},{2,34},{34,2},{3,35},{35,3},{4,36},{36... | collective-permute-start | bytes 1769480 | tf_op jit(solution)/shard_map/ppermute | solution.py:62
  47.7 4.6 %collective-permute-start.6 = (bf16[256,1152]{1,0:T(8,128)(2,1)S(1)}, bf16[256,1152]{1,0:T(8,128)(2,1)S(1)}, u32[]{:S(2)}, u32[]{:S(2)}) collective-permute-start(bf16[256,1152]{1,0:T(8,128)(2,1)S(1)} %collective-permute-done.5.refs_3_), channel_id=1, source_target_pairs={{0,32},{32,0},{1,33},{33,1},{2,34},{34,2},{3,35},{35,3},{4,36},{36... | collective-permute-start | bytes 1769480 | tf_op jit(solution)/shard_map/ppermute | solution.py:62
  55.2 19.3 %collective-permute-start.7 = (bf16[256,1152]{1,0:T(8,128)(2,1)S(1)}, bf16[256,1152]{1,0:T(8,128)(2,1)S(1)}, u32[]{:S(2)}, u32[]{:S(2)}) collective-permute-start(bf16[256,1152]{1,0:T(8,128)(2,1)S(1)} %get-tuple-element.15), channel_id=1, source_target_pairs={{4,0},{68,64},{0,4},{64,68},{12,8},{76,72},{8,12},{72,76},{20,16},... | collective-permute-start | bytes 1769480 | tf_op jit(solution)/shard_map/ppermute | solution.py:54
  57.1 17.3 %collective-permute-start.8 = (bf16[256,1152]{1,0:T(8,128)(2,1)S(1)}, bf16[256,1152]{1,0:T(8,128)(2,1)S(1)}, u32[]{:S(2)}, u32[]{:S(2)}) collective-permute-start(bf16[256,1152]{1,0:T(8,128)(2,1)S(1)} %get-tuple-element.16), channel_id=1, source_target_pairs={{28,0},{92,64},{8,4},{72,68},{4,8},{68,72},{16,12},{80,76},{12,16}... | collective-permute-start | bytes 1769480 | tf_op jit(solution)/shard_map/ppermute | solution.py:54
  64.2 10.3 %collective-permute-start.9 = (bf16[192,1152]{1,0:T(8,128)(2,1)S(1)}, bf16[192,1152]{1,0:T(8,128)(2,1)S(1)}, u32[]{:S(2)}, u32[]{:S(2)}) collective-permute-start(bf16[192,1152]{1,0:T(8,128)(2,1)S(1)} %get-tuple-element.18), channel_id=1, source_target_pairs={{64,0},{0,64},{68,4},{4,68},{72,8},{8,72},{76,12},{12,76},{80,16},... | collective-permute-start | bytes 1327112 | tf_op jit(solution)/shard_map/ppermute | solution.py:54
  68.6 24.0 %copy-start = (bf16[32,1152]{1,0:T(8,128)(2,1)S(1)}, bf16[32,1152]{1,0:T(8,128)(2,1)}, u32[]{:S(2)}) copy-start(bf16[32,1152]{1,0:T(8,128)(2,1)} %image.1) | copy-start | bytes 221188
  68.6 24.0 %copy-start.1 = (bf16[32,1152]{1,0:T(8,128)(2,1)S(1)}, bf16[32,1152]{1,0:T(8,128)(2,1)}, u32[]{:S(2)}) copy-start(bf16[32,1152]{1,0:T(8,128)(2,1)} %text.1) | copy-start | bytes 221188
  75.5 14.2 %all-to-all-start.1 = ((bf16[4,64,1152]{2,1,0:T(8,128)(2,1)}), bf16[4,64,1152]{2,1,0:T(8,128)(2,1)S(1)}, u32[]{:S(2)}, u32[]{:S(2)}) async-start(bf16[4,64,1152]{2,1,0:T(8,128)(2,1)} %merge.1), calls=%async_computation.1 | async-start | bytes 1179648 | tf_op jit(solution)/shard_map/all_to_all | solution.py:58
  79.0 10.7 %collective-permute-start.10 = (bf16[64,1152]{1,0:T(8,128)(2,1)S(1)}, bf16[64,1152]{1,0:T(8,128)(2,1)S(1)}, u32[]{:S(2)}, u32[]{:S(2)}) collective-permute-start(bf16[64,1152]{1,0:T(8,128)(2,1)S(1)} %get-tuple-element.19), channel_id=1, source_target_pairs={{64,0},{0,64},{68,4},{4,68},{72,8},{8,72},{76,12},{12,76},{80,16},... | collective-permute-start | bytes 442376 | tf_op jit(solution)/shard_map/ppermute | solution.py:54

commit v10 on v8

--- a/solution.py
+++ b/solution.py
@@ -82,25 +82,47 @@
     return pair[pl.ds(pl.multiple_of((1 - lax.axis_index("c")) * rows, rows), rows), :]
 
 
-def spread_kernel(own, pair, copies):
+def spread_kernel(own, pair, copies, block):
     rows = own.shape[0]
     first = unit_rows(own[...])[0].astype(jnp.bfloat16)
     second = unit_rows(from_other_core(pair))[0].astype(jnp.bfloat16)
-    for peer in range(COLORS):
-        copies[peer, :rows, :] = first
-        copies[peer, rows:, :] = second
+    for member in range(COLORS):
+        copies[member, :rows, :] = first
+        copies[member, rows:, :] = second
+    block[:rows, :] = first
+    block[rows:, :] = second
+
+
+def own_node(is_text):
+    ring = jnp.where(is_text, lax.axis_index("y"), lax.axis_index("zh") * 2 + lax.axis_index("zl"))
+    side = jnp.where(is_text, lax.axis_index("xl"), lax.axis_index("xh"))
+    return ring, side
+
+
+def own_member():
+    ring, side = own_node(lax.axis_index("c") == 0)
+    low = jnp.where(ring >= 4, 1, 0)
+    high = jnp.where(jnp.logical_and(ring >= 2, ring < 6), 2, 3)
+    return jnp.where(side == 0, low, high)
+
+
+def order_kernel(gathered, block, rest):
+    size = gathered.shape[1]
+    member = own_member()
+    for j in range(COLORS):
+        rows = gathered[member ^ j]
+        block[j * size : (j + 1) * size, :] = rows
+        if j > 0:
+            rest[(j - 1) * size : j * size, :] = rows
 
 
 def global_rows(index, is_text, rows):
     bits = rows.bit_length() - 1
     x = lax.axis_index("xh") * 2 + lax.axis_index("xl")
-    z = lax.axis_index("zh") * 2 + lax.axis_index("zl")
     low = jnp.minimum(x, 3 - x)
     text = ((lax.axis_index("zl") * 4 + lax.axis_index("xh") * 2) * 2 * 8) * 4 + lax.axis_index("zh")
     image = (lax.axis_index("y") * 8 * 4 + low) * 2 + 1
-    place = jnp.where(
-        is_text, lax.axis_index("y") + 2 * lax.axis_index("xl"), z + 2 * lax.axis_index("xh")
-    )
+    own_ring, own_side = own_node(is_text)
     first = jnp.where(is_text, text, image) * rows
     per_side = jnp.where(is_text, 64, 2 * (3 - 2 * low)) * rows
     per_slot = jnp.where(is_text, 32, -1) * rows
@@ -108,11 +130,13 @@
 
     member = (index >> (bits + 1)) & (COLORS - 1)
     chunk = index >> (bits + 3)
-    side = member >> 1
-    odd = jnp.where(is_text, lax.axis_index("y") & 1, lax.axis_index("zl"))
-    step = chunk ^ (chunk >> 1)
-    color = (place + step + ((odd * step) & 1) * 2) & (COLORS - 1)
-    ring = (color + ((member & 1) << 2) + (side << 1)) & (RING - 1)
+    node_ring = jnp.where(
+        chunk == 1, own_ring ^ 1, jnp.where(chunk == 2, ((own_ring + 1) ^ 1) - 1, own_ring)
+    )
+    node_side = jnp.where(chunk == 3, 1 - own_side, own_side)
+    turn = member >> 1
+    side = node_side ^ turn
+    ring = (node_ring + 4 * (member & 1) + 2 * (1 - 2 * node_side) * turn) & (RING - 1)
     slot = (index >> bits) & 1
     return first + per_side * side + per_slot * slot + per_ring * ring + (index & (rows - 1))
 
@@ -170,10 +194,22 @@
     finish(count - 1, before)
 
 
-def sum_kernel(parts, own, other):
+def merge_kernel(mine, first, second, tail, blocks):
+    size = blocks.shape[1]
+    member = own_member()
+    for j in range(COLORS):
+        place = slice(j * size, (j + 1) * size)
+        total = mine[place, :] + first[place, :].astype(jnp.float32) + second[place, :].astype(jnp.float32)
+        if j > 0:
+            total = total + tail[(j - 1) * size : j * size, :].astype(jnp.float32)
+        blocks[member ^ j] = total.astype(blocks.dtype)
+
+
+def sum_kernel(parts, head, own, other):
     rows = own.shape[0]
-    own[...] = jnp.sum(parts[:, :rows, :].astype(jnp.float32), axis=0)
-    other[...] = jnp.sum(parts[:, rows:, :].astype(jnp.float32), axis=0)
+    total = head[...].astype(jnp.float32) + jnp.sum(parts[...].astype(jnp.float32), axis=0)
+    own[...] = total[:rows, :]
+    other[...] = total[rows:, :]
 
 
 def finish_kernel(scalars, summed, pair, image, text, grad_image, grad_text):
@@ -200,16 +236,29 @@
     speaks_text = lax.axis_index("c") == 0
     kept = jnp.where(speaks_text, text_emb, image_emb)
     pair = gather_cores(jnp.where(speaks_text, image_emb, text_emb))
-    copies = pl.pallas_call(
-        spread_kernel,
-        out_shape=jax.ShapeDtypeStruct((COLORS, 2 * rows, width), jnp.bfloat16),
-        in_specs=[VMEM, VMEM],
-        out_specs=VMEM,
-        compiler_params=SMALL,
-        name="spread",
-    )(kept, pair)
-    own = exchange(copies).reshape(part, width)
-    mine = [own] + [swap_with(own, neighbour) for neighbour in NEIGHBOURS]
+    size = 2 * rows
+    spread = jax.ShapeDtypeStruct((COLORS, size, width), jnp.bfloat16)
+
+    def small_call(kernel, out_shape, operands, name):
+        return pl.pallas_call(
+            kernel,
+            out_shape=out_shape,
+            in_specs=[VMEM] * len(operands),
+            out_specs=[VMEM] * len(out_shape),
+            compiler_params=SMALL,
+            name=name,
+        )(*operands)
+
+    def half(count):
+        return jax.ShapeDtypeStruct((count, width), jnp.bfloat16)
+
+    copies, block = small_call(spread_kernel, [spread, half(size)], [kept, pair], "spread")
+    heads = [swap_with(block, neighbour) for neighbour in NEIGHBOURS]
+    own, rest = small_call(order_kernel, [half(part), half(part - size)], [exchange(copies)], "order")
+    mine = [own] + [
+        jnp.concatenate([head, swap_with(rest, neighbour)], axis=0)
+        for head, neighbour in zip(heads, NEIGHBOURS)
+    ]
     chunks = [swap_cores(chunk) for chunk in mine]
     theirs = jnp.concatenate(chunks, axis=0)
     near, early = (1, 2, 3), 3
@@ -245,22 +294,16 @@
         len(near) * early,
         "weigh",
     )
-    partial = [
-        swap_with(block, neighbour) for block, neighbour in zip(tile(near, ready, jnp.bfloat16), NEIGHBOURS)
+    blocks = tile(near, ready, jnp.bfloat16)
+    first, second, tail = [
+        swap_with(block, neighbour)
+        for block, neighbour in zip((blocks[0], blocks[1], blocks[2][size:]), NEIGHBOURS)
     ]
+    head = swap_with(blocks[2][:size], NEIGHBOURS[2])
     (summed,) = tile((0,), [], jnp.float32)
-    for block in partial:
-        summed = summed + block.astype(jnp.float32)
-    parts = exchange(summed.astype(jnp.bfloat16).reshape(COLORS, 2 * rows, width))
+    (merged,) = small_call(merge_kernel, [spread], [summed, first, second, tail], "merge")
     out = jax.ShapeDtypeStruct((rows, width), jnp.float32)
-    own, other = pl.pallas_call(
-        sum_kernel,
-        out_shape=(out, out),
-        in_specs=[VMEM],
-        out_specs=(VMEM, VMEM),
-        compiler_params=SMALL,
-        name="sum",
-    )(parts)
+    own, other = small_call(sum_kernel, [out, out], [exchange(merged), head], "sum")
     return pl.pallas_call(
         finish_kernel,
         out_shape=(out, out),

time: 95.1 us -> 94 us (0.988)
  blocking collectives: 44.9 us -> 10.7 us
  starting transfers between devices: 28.7 us -> 57.9 us
  Pallas kernels: 7.47 us -> 9.53 us
  waiting for transfers between devices: 9.3 us -> 11 us
    all_to_all x2 -> x0, blocking collectives: 34.4 us -> none  [exchange(): lax.all_to_all(blocks, NAMES, 0, 0, axis_index_groups=color_groups(), til...]
    ppermute x6 -> x10, starting transfers between devices: 20.4 us -> 38.7 us  [swap_with(): return lax.ppermute(block, NAMES, pairs)]
    all_to_all x0 -> x2, starting transfers between devices: none -> 10.6 us  [exchange(): lax.all_to_all(blocks, NAMES, 0, 0, axis_index_groups=color_groups(), til...]
    pallas_call x2 -> x4, Pallas kernels: 0.21 us -> 2.23 us  [small_call(): pl.pallas_call(kernel, out_shape=out_shape, in_specs=[VMEM] * len(operand...]
    ppermute x6 -> x10, waiting for transfers between devices: 9.29 us -> 11 us  [swap_with(): return lax.ppermute(block, NAMES, pairs)]
  transfers between devices with their start and end apart: 10 -> 16, of which waited for: 4 -> 3; matrix products, arithmetic and copies ran while one was open for 0% -> 1% of each run, Pallas kernels for 4% -> 4%
where the time goes in v10:
time: 94 us; the launch traced here: 92.9 us
  starting transfers between devices  57.9 us (62%)
  waiting for transfers between devices  11 us (12%)
  blocking collectives  10.7 us (11%)
  Pallas kernels  9.53 us (10%)
  between operations  2.25 us (2%)
  other arithmetic  1.02 us (1%)
    ppermute x10, starting transfers between devices, swap_with(): return lax.ppermute(block, NAMES, pairs)  38.7 us
    ppermute x10, waiting for transfers between devices, swap_with(): return lax.ppermute(block, NAMES, pairs)  11 us
    all_gather x2, blocking collectives, gather_cores(): return lax.all_gather(block, 'c', axis=0, tiled=True)  10.7 us
    all_to_all x2, starting transfers between devices, exchange(): lax.all_to_all(blocks, NAMES, 0, 0, axis_index_groups=color_groups(), til...  10.6 us
    ppermute x4, starting transfers between devices, swap_cores(): return lax.ppermute(block, 'c', [(0, 1), (1, 0)])  8.65 us
    pallas_call x3, Pallas kernels, call(): pl.pallas_call(kernel, out_shape=out_shape, in_specs=[VMEM] * len(operand...  6.36 us
    pallas_call x4, Pallas kernels, small_call(): pl.pallas_call(kernel, out_shape=out_shape, in_specs=[VMEM] * len(operand...  2.23 us
  transfers between devices with their start and end apart: 16, of which 3 were waited for; matrix products, arithmetic and copies ran while one was open for 1% of the time, Pallas kernels for 4%

profile of v10, /device:TPU:1, one launch (start us, length us, event | category | flops | bytes accessed | tf_op | source)
XLA Modules:
  0.0 92.9 jit_solution(14925359869164767357)
XLA Ops:
  0.6 0.9 %broadcast_select_fusion = (bf16[32,1152]{1,0:T(8,128)(2,1)S(1)}, bf16[32,1152]{1,0:T(8,128)(2,1)S(1)}) fusion(bf16[32,1152]{1,0:T(8,128)(2,1)} %image.1, bf16[32,1152]{1,0:T(8,128)(2,1)} %text.1, pred[]{:T(512)S(6)} %eq.3), kind=kLoop, calls=%fused_computation | loop fusion | flops 73728 | bytes 294913 | tf_op jit(solution)/shard_map/jit(_where)/select_n | solution.py:238
  1.6 8.4 %all_gather.6.pair = bf16[64,1152]{1,0:T(8,128)(2,1)S(1)} all-gather(bf16[32,1152]{1,0:T(8,128)(2,1)S(1)} %get-tuple-element.26), channel_id=1, replica_groups=mesh['zl'=2,'xh'=2,'xl'=2,'c'=2,'y'=8,'zh'=4] {'c'}, dimensions={0}, use_global_device_ids=true | all-gather | bytes 221184 | tf_op jit(solution)/shard_map/all_gather | solution.py:66
  10.0 1.0 %spread.1 = (bf16[4,64,1152]{2,1,0:T(8,128)(2,1)}, bf16[64,1152]{1,0:T(8,128)(2,1)S(1)}) custom-call(bf16[32,1152]{1,0:T(8,128)(2,1)S(1)} %get-tuple-element.27.own, bf16[64,1152]{1,0:T(8,128)(2,1)S(1)} %all_gather.6.pair), custom_call_target="tpu_custom_call" | custom-call | tf_op jit(solution)/shard_map/spread/pallas_call | solution.py:243
  11.0 6.8 %all-to-all-start = ((bf16[4,64,1152]{2,1,0:T(8,128)(2,1)}), bf16[4,64,1152]{2,1,0:T(8,128)(2,1)S(1)}, u32[]{:S(2)}, u32[]{:S(2)}) async-start(bf16[4,64,1152]{2,1,0:T(8,128)(2,1)} %get-tuple-element.14), calls=%async_computation | async-start | bytes 1179648 | tf_op jit(solution)/shard_map/all_to_all | solution.py:58
  17.8 3.1 %collective-permute-start.1 = (bf16[64,1152]{1,0:T(8,128)(2,1)S(1)}, bf16[64,1152]{1,0:T(8,128)(2,1)S(1)}, u32[]{:S(2)}, u32[]{:S(2)}) collective-permute-start(bf16[64,1152]{1,0:T(8,128)(2,1)S(1)} %get-tuple-element.16), channel_id=1, source_target_pairs={{4,0},{68,64},{0,4},{64,68},{12,8},{76,72},{8,12},{72,76},{20,16},... | collective-permute-start | bytes 442376 | tf_op jit(solution)/shard_map/ppermute | solution.py:54
  20.9 4.5 %collective-permute-start.4 = (bf16[64,1152]{1,0:T(8,128)(2,1)S(1)}, bf16[64,1152]{1,0:T(8,128)(2,1)S(1)}, u32[]{:S(2)}, u32[]{:S(2)}) collective-permute-start(bf16[64,1152]{1,0:T(8,128)(2,1)S(1)} %get-tuple-element.16), channel_id=1, source_target_pairs={{28,0},{92,64},{8,4},{72,68},{4,8},{68,72},{16,12},{80,76},{12,16}... | collective-permute-start | bytes 442376 | tf_op jit(solution)/shard_map/ppermute | solution.py:54
  25.5 4.3 %collective-permute-start.7 = (bf16[64,1152]{1,0:T(8,128)(2,1)S(1)}, bf16[64,1152]{1,0:T(8,128)(2,1)S(1)}, u32[]{:S(2)}, u32[]{:S(2)}) collective-permute-start(bf16[64,1152]{1,0:T(8,128)(2,1)S(1)} %get-tuple-element.16), channel_id=1, source_target_pairs={{64,0},{0,64},{68,4},{4,68},{72,8},{8,72},{76,12},{12,76},{80,16},... | collective-permute-start | bytes 442376 | tf_op jit(solution)/shard_map/ppermute | solution.py:54
  31.1 0.1 maximum_bitcast_fusion.refs_0_.scalars
  31.2 0.0 all-to-all-done.gathered
  31.2 0.1 order.1
  31.3 3.4 %collective-permute-start.2 = (bf16[192,1152]{1,0:T(8,128)(2,1)S(1)}, bf16[192,1152]{1,0:T(8,128)(2,1)S(1)}, u32[]{:S(2)}, u32[]{:S(2)}) collective-permute-start(bf16[192,1152]{1,0:T(8,128)(2,1)S(1)} %get-tuple-element.17), channel_id=1, source_target_pairs={{4,0},{68,64},{0,4},{64,68},{12,8},{76,72},{8,12},{72,76},{20,16},... | collective-permute-start | bytes 1327112 | tf_op jit(solution)/shard_map/ppermute | solution.py:54
  34.7 0.0 collective-permute-done.1
  34.7 1.9 %collective-permute-start.5 = (bf16[192,1152]{1,0:T(8,128)(2,1)S(1)}, bf16[192,1152]{1,0:T(8,128)(2,1)S(1)}, u32[]{:S(2)}, u32[]{:S(2)}) collective-permute-start(bf16[192,1152]{1,0:T(8,128)(2,1)S(1)} %get-tuple-element.17), channel_id=1, source_target_pairs={{28,0},{92,64},{8,4},{72,68},{4,8},{68,72},{16,12},{80,76},{12,16}... | collective-permute-start | bytes 1327112 | tf_op jit(solution)/shard_map/ppermute | solution.py:54
  36.6 0.0 collective-permute-done.4
  36.6 3.1 %collective-permute-start.8 = (bf16[192,1152]{1,0:T(8,128)(2,1)S(1)}, bf16[192,1152]{1,0:T(8,128)(2,1)S(1)}, u32[]{:S(2)}, u32[]{:S(2)}) collective-permute-start(bf16[192,1152]{1,0:T(8,128)(2,1)S(1)} %get-tuple-element.17), channel_id=1, source_target_pairs={{64,0},{0,64},{68,4},{4,68},{72,8},{8,72},{76,12},{12,76},{80,16},... | collective-permute-start | bytes 1327112 | tf_op jit(solution)/shard_map/ppermute | solution.py:54
  39.7 1.9 %collective-permute-start = (bf16[256,1152]{1,0:T(8,128)(2,1)S(1)}, bf16[256,1152]{1,0:T(8,128)(2,1)S(1)}, u32[]{:S(2)}, u32[]{:S(2)}) collective-permute-start(bf16[256,1152]{1,0:T(8,128)(2,1)S(1)} %get-tuple-element.15.refs_1_), channel_id=1, source_target_pairs={{0,32},{32,0},{1,33},{33,1},{2,34},{34,2},{3,35},{35,3},{4,36},{36... | collective-permute-start | bytes 1769480 | tf_op jit(solution)/shard_map/ppermute | solution.py:62
  41.7 0.0 collective-permute-done.2
  41.7 2.4 %collective-permute-start.3 = (bf16[256,1152]{1,0:T(8,128)(2,1)S(1)}, bf16[256,1152]{1,0:T(8,128)(2,1)S(1)}, u32[]{:S(2)}, u32[]{:S(2)}) collective-permute-start(bf16[256,1152]{1,0:T(8,128)(2,1)S(1)} %constant_dynamic-update-slice_fusion.refs_1_), channel_id=1, source_target_pairs={{0,32},{32,0},{1,33},{33,1},{2,34},{34,2},{3,35},{35,3},{4,36},{36... | collective-permute-start | bytes 1769480 | tf_op jit(solution)/shard_map/ppermute | solution.py:62
  44.1 0.8 collective-permute-done.5
  45.0 1.9 %collective-permute-start.6 = (bf16[256,1152]{1,0:T(8,128)(2,1)S(1)}, bf16[256,1152]{1,0:T(8,128)(2,1)S(1)}, u32[]{:S(2)}, u32[]{:S(2)}) collective-permute-start(bf16[256,1152]{1,0:T(8,128)(2,1)S(1)} %constant_dynamic-update-slice_fusion.2.refs_2_), channel_id=1, source_target_pairs={{0,32},{32,0},{1,33},{33,1},{2,34},{34,2},{3,35},{35,3},{4,36},{36... | collective-permute-start | bytes 1769480 | tf_op jit(solution)/shard_map/ppermute | solution.py:62
  46.9 0.0 collective-permute-done.7
  47.0 0.0 collective-permute-done.8
  47.0 2.4 %collective-permute-start.9 = (bf16[256,1152]{1,0:T(8,128)(2,1)S(1)}, bf16[256,1152]{1,0:T(8,128)(2,1)S(1)}, u32[]{:S(2)}, u32[]{:S(2)}) collective-permute-start(bf16[256,1152]{1,0:T(8,128)(2,1)S(1)} %constant_dynamic-update-slice_fusion.4.refs_3_), channel_id=1, source_target_pairs={{0,32},{32,0},{1,33},{33,1},{2,34},{34,2},{3,35},{35,3},{4,36},{36... | collective-permute-start | bytes 1769480 | tf_op jit(solution)/shard_map/ppermute | solution.py:62
  49.4 0.0 collective-permute-done.refs_4_
  49.5 0.0 collective-permute-done.3.refs_5_
  49.5 0.0 collective-permute-done.6.refs_6_
  49.5 2.0 %weigh.1 = (bf16[256,768]{1,0:T(8,128)(2,1)S(1)}, bf16[256,768]{1,0:T(8,128)(2,1)S(1)}, bf16[256,768]{1,0:T(8,128)(2,1)S(1)}) custom-call(f32[1,2]{1,0:T(1,128)S(1)} %maximum_bitcast_fusion.refs_0_.scalars, bf16[256,1152]{1,0:T(8,128)(2,1)S(1)} %constant_dynamic-update-slice_fusion.refs_1_, ...), custom_call_target="tpu_custom_call" | custom-call | flops 1358954496 | bytes 3538948 | tf_op jit(solution)/shard_map/weigh/pallas_call | solution.py:267
  51.5 0.1 constant_dynamic-update-slice_fusion.8
  51.6 0.1 constant_dynamic-update-slice_fusion.7
  51.7 0.0 collective-permute-done.9
  51.7 0.1 constant_dynamic-update-slice_fusion.6.refs_2_.refs_7_
  51.8 2.8 %tile.3 = (bf16[256,1152]{1,0:T(8,128)(2,1)S(1)}, bf16[256,1152]{1,0:T(8,128)(2,1)S(1)}, bf16[256,1152]{1,0:T(8,128)(2,1)S(1)}) custom-call(f32[1,2]{1,0:T(1,128)S(1)} %maximum_bitcast_fusion.refs_0_.scalars, bf16[256,1152]{1,0:T(8,128)(2,1)S(1)} %constant_dynamic-update-slice_fusion.refs_1_, ...), custom_call_target="tpu_custom_call" | custom-call | flops 2264924160 | bytes 5308420 | tf_op jit(solution)/shard_map/tile/pallas_call | solution.py:267
  54.5 2.3 %collective-permute-start.10 = (bf16[256,1152]{1,0:T(8,128)(2,1)S(1)}, bf16[256,1152]{1,0:T(8,128)(2,1)S(1)}, u32[]{:S(2)}, u32[]{:S(2)}) collective-permute-start(bf16[256,1152]{1,0:T(8,128)(2,1)S(1)} %get-tuple-element.21), channel_id=1, source_target_pairs={{4,0},{68,64},{0,4},{64,68},{12,8},{76,72},{8,12},{72,76},{20,16},... | collective-permute-start | bytes 1769480 | tf_op jit(solution)/shard_map/ppermute | solution.py:54
  56.8 6.5 %collective-permute-start.11 = (bf16[256,1152]{1,0:T(8,128)(2,1)S(1)}, bf16[256,1152]{1,0:T(8,128)(2,1)S(1)}, u32[]{:S(2)}, u32[]{:S(2)}) collective-permute-start(bf16[256,1152]{1,0:T(8,128)(2,1)S(1)} %get-tuple-element.22), channel_id=1, source_target_pairs={{28,0},{92,64},{8,4},{72,68},{4,8},{68,72},{16,12},{80,76},{12,16}... | collective-permute-start | bytes 1769480 | tf_op jit(solution)/shard_map/ppermute | solution.py:54
  63.4 3.7 %collective-permute-start.12 = (bf16[192,1152]{1,0:T(8,128)(2,1)S(1)}, bf16[192,1152]{1,0:T(8,128)(2,1)S(1)}, u32[]{:S(2)}, u32[]{:S(2)}) collective-permute-start(bf16[192,1152]{1,0:T(8,128)(2,1)S(1)} %slice.6), channel_id=1, source_target_pairs={{64,0},{0,64},{68,4},{4,68},{72,8},{8,72},{76,12},{12,76},{80,16},... | collective-permute-start | bytes 1327112 | tf_op jit(solution)/shard_map/ppermute | solution.py:54
  67.2 1.6 %tile.2.mine = f32[256,1152]{1,0:T(8,128)S(1)} custom-call(f32[1,2]{1,0:T(1,128)S(1)} %maximum_bitcast_fusion.refs_0_.scalars, bf16[256,1152]{1,0:T(8,128)(2,1)S(1)} %get-tuple-element.15.refs_1_, bf16[1024,1152]{1,0:T(8,128)(2,1)S(1)} %constant_dynamic-update-slice_fusion.6.refs_2_.refs_7_), custom_call_target="tpu_custom_call" | custom-call | flops 1207959552 | bytes 2949124 | tf_op jit(solution)/shard_map/tile/pallas_call | solution.py:267
  68.8 0.0 copy-start
  68.8 0.0 copy-start.1
  68.8 4.9 %collective-permute-done.12.tail = bf16[192,1152]{1,0:T(8,128)(2,1)S(1)} collective-permute-done((bf16[192,1152]{1,0:T(8,128)(2,1)S(1)}, bf16[192,1152]{1,0:T(8,128)(2,1)S(1)}, u32[]{:S(2)}, u32[]{:S(2)}) %collective-permute-start.12) | collective-permute-done | bytes 442400 | tf_op jit(solution)/shard_map/ppermute | solution.py:54
  73.7 0.0 collective-permute-done.10.first
  73.7 0.0 collective-permute-done.11.second
  73.7 1.1 %merge.1 = bf16[4,64,1152]{2,1,0:T(8,128)(2,1)} custom-call(f32[256,1152]{1,0:T(8,128)S(1)} %tile.2.mine, bf16[256,1152]{1,0:T(8,128)(2,1)S(1)} %collective-permute-done.10.first, bf16[256,1152]{1,0:T(8,128)(2,1)S(1)} %collective-permute-done.11.second, bf16[192,1152]{1,0:T(8,128)(2,1)S(1)} %collective-permute-done.12.tail), custom_call_target="tpu_custom_call" | custom-call | tf_op jit(solution)/shard_map/merge/pallas_call | solution.py:243
  74.8 3.7 %all-to-all-start.1 = ((bf16[4,64,1152]{2,1,0:T(8,128)(2,1)}), bf16[4,64,1152]{2,1,0:T(8,128)(2,1)S(1)}, u32[]{:S(2)}, u32[]{:S(2)}) async-start(bf16[4,64,1152]{2,1,0:T(8,128)(2,1)} %merge.1), calls=%async_computation.1 | async-start | bytes 1179648 | tf_op jit(solution)/shard_map/all_to_all | solution.py:58
  78.5 5.7 %collective-permute-start.13 = (bf16[64,1152]{1,0:T(8,128)(2,1)S(1)}, bf16[64,1152]{1,0:T(8,128)(2,1)S(1)}, u32[]{:S(2)}, u32[]{:S(2)}) collective-permute-start(bf16[64,1152]{1,0:T(8,128)(2,1)S(1)} %slice.7), channel_id=1, source_target_pairs={{64,0},{0,64},{68,4},{4,68},{72,8},{8,72},{76,12},{12,76},{80,16},... | collective-permute-start | bytes 442376 | tf_op jit(solution)/shard_map/ppermute | solution.py:54
  84.3 5.3 %collective-permute-done.13.head = bf16[64,1152]{1,0:T(8,128)(2,1)S(1)} collective-permute-done((bf16[64,1152]{1,0:T(8,128)(2,1)S(1)}, bf16[64,1152]{1,0:T(8,128)(2,1)S(1)}, u32[]{:S(2)}, u32[]{:S(2)}) %collective-permute-start.13) | collective-permute-done | bytes 147488 | tf_op jit(solution)/shard_map/ppermute | solution.py:54
  89.6 0.0 all-to-all-done.1.parts
  89.6 0.1 sum.1
  89.7 2.2 %all_gather.7.pair = f32[64,1152]{1,0:T(8,128)S(1)} all-gather(f32[32,1152]{1,0:T(8,128)S(1)} %get-tuple-element.25), channel_id=1, replica_groups=mesh['zl'=2,'xh'=2,'xl'=2,'c'=2,'y'=8,'zh'=4] {'c'}, dimensions={0}, use_global_device_ids=true | all-gather | bytes 442368 | tf_op jit(solution)/shard_map/all_gather | solution.py:66
  91.9 0.0 copy-done
  92.0 0.0 copy-done.1
  92.0 0.9 %finish.1 = (f32[32,1152]{1,0:T(8,128)}, f32[32,1152]{1,0:T(8,128)}) custom-call(f32[1,2]{1,0:T(1,128)S(1)} %maximum_bitcast_fusion.refs_0_.scalars, f32[32,1152]{1,0:T(8,128)S(1)} %get-tuple-element.24.summed, f32[64,1152]{1,0:T(8,128)S(1)} %all_gather.7.pair, bf16[32,1152]{1,0:T(8,128)(2,1)S(1)} %copy-done, bf16[32,1152]{1,0:T(8,128)(2,1)S(1)} %copy-done.1), custom_call_target="tpu_custom_call" | custom-call | tf_op jit(solution)/shard_map/finish/pallas_call | solution.py:307
  (9 shorter events, 0.3 us)
Async XLA Ops:
  11.0 20.2 %all-to-all-start = ((bf16[4,64,1152]{2,1,0:T(8,128)(2,1)}), bf16[4,64,1152]{2,1,0:T(8,128)(2,1)S(1)}, u32[]{:S(2)}, u32[]{:S(2)}) async-start(bf16[4,64,1152]{2,1,0:T(8,128)(2,1)} %get-tuple-element.14), calls=%async_computation | async-start | bytes 1179648 | tf_op jit(solution)/shard_map/all_to_all | solution.py:58
  17.8 16.8 %collective-permute-start.1 = (bf16[64,1152]{1,0:T(8,128)(2,1)S(1)}, bf16[64,1152]{1,0:T(8,128)(2,1)S(1)}, u32[]{:S(2)}, u32[]{:S(2)}) collective-permute-start(bf16[64,1152]{1,0:T(8,128)(2,1)S(1)} %get-tuple-element.16), channel_id=1, source_target_pairs={{4,0},{68,64},{0,4},{64,68},{12,8},{76,72},{8,12},{72,76},{20,16},... | collective-permute-start | bytes 442376 | tf_op jit(solution)/shard_map/ppermute | solution.py:54
  20.9 15.7 %collective-permute-start.4 = (bf16[64,1152]{1,0:T(8,128)(2,1)S(1)}, bf16[64,1152]{1,0:T(8,128)(2,1)S(1)}, u32[]{:S(2)}, u32[]{:S(2)}) collective-permute-start(bf16[64,1152]{1,0:T(8,128)(2,1)S(1)} %get-tuple-element.16), channel_id=1, source_target_pairs={{28,0},{92,64},{8,4},{72,68},{4,8},{68,72},{16,12},{80,76},{12,16}... | collective-permute-start | bytes 442376 | tf_op jit(solution)/shard_map/ppermute | solution.py:54
  25.5 21.4 %collective-permute-start.7 = (bf16[64,1152]{1,0:T(8,128)(2,1)S(1)}, bf16[64,1152]{1,0:T(8,128)(2,1)S(1)}, u32[]{:S(2)}, u32[]{:S(2)}) collective-permute-start(bf16[64,1152]{1,0:T(8,128)(2,1)S(1)} %get-tuple-element.16), channel_id=1, source_target_pairs={{64,0},{0,64},{68,4},{4,68},{72,8},{8,72},{76,12},{12,76},{80,16},... | collective-permute-start | bytes 442376 | tf_op jit(solution)/shard_map/ppermute | solution.py:54
  31.3 10.4 %collective-permute-start.2 = (bf16[192,1152]{1,0:T(8,128)(2,1)S(1)}, bf16[192,1152]{1,0:T(8,128)(2,1)S(1)}, u32[]{:S(2)}, u32[]{:S(2)}) collective-permute-start(bf16[192,1152]{1,0:T(8,128)(2,1)S(1)} %get-tuple-element.17), channel_id=1, source_target_pairs={{4,0},{68,64},{0,4},{64,68},{12,8},{76,72},{8,12},{72,76},{20,16},... | collective-permute-start | bytes 1327112 | tf_op jit(solution)/shard_map/ppermute | solution.py:54
  34.7 10.3 %collective-permute-start.5 = (bf16[192,1152]{1,0:T(8,128)(2,1)S(1)}, bf16[192,1152]{1,0:T(8,128)(2,1)S(1)}, u32[]{:S(2)}, u32[]{:S(2)}) collective-permute-start(bf16[192,1152]{1,0:T(8,128)(2,1)S(1)} %get-tuple-element.17), channel_id=1, source_target_pairs={{28,0},{92,64},{8,4},{72,68},{4,8},{68,72},{16,12},{80,76},{12,16}... | collective-permute-start | bytes 1327112 | tf_op jit(solution)/shard_map/ppermute | solution.py:54
  36.6 10.3 %collective-permute-start.8 = (bf16[192,1152]{1,0:T(8,128)(2,1)S(1)}, bf16[192,1152]{1,0:T(8,128)(2,1)S(1)}, u32[]{:S(2)}, u32[]{:S(2)}) collective-permute-start(bf16[192,1152]{1,0:T(8,128)(2,1)S(1)} %get-tuple-element.17), channel_id=1, source_target_pairs={{64,0},{0,64},{68,4},{4,68},{72,8},{8,72},{76,12},{12,76},{80,16},... | collective-permute-start | bytes 1327112 | tf_op jit(solution)/shard_map/ppermute | solution.py:54
  39.7 9.7 %collective-permute-start = (bf16[256,1152]{1,0:T(8,128)(2,1)S(1)}, bf16[256,1152]{1,0:T(8,128)(2,1)S(1)}, u32[]{:S(2)}, u32[]{:S(2)}) collective-permute-start(bf16[256,1152]{1,0:T(8,128)(2,1)S(1)} %get-tuple-element.15.refs_1_), channel_id=1, source_target_pairs={{0,32},{32,0},{1,33},{33,1},{2,34},{34,2},{3,35},{35,3},{4,36},{36... | collective-permute-start | bytes 1769480 | tf_op jit(solution)/shard_map/ppermute | solution.py:62
  41.7 7.8 %collective-permute-start.3 = (bf16[256,1152]{1,0:T(8,128)(2,1)S(1)}, bf16[256,1152]{1,0:T(8,128)(2,1)S(1)}, u32[]{:S(2)}, u32[]{:S(2)}) collective-permute-start(bf16[256,1152]{1,0:T(8,128)(2,1)S(1)} %constant_dynamic-update-slice_fusion.refs_1_), channel_id=1, source_target_pairs={{0,32},{32,0},{1,33},{33,1},{2,34},{34,2},{3,35},{35,3},{4,36},{36... | collective-permute-start | bytes 1769480 | tf_op jit(solution)/shard_map/ppermute | solution.py:62
  45.0 4.5 %collective-permute-start.6 = (bf16[256,1152]{1,0:T(8,128)(2,1)S(1)}, bf16[256,1152]{1,0:T(8,128)(2,1)S(1)}, u32[]{:S(2)}, u32[]{:S(2)}) collective-permute-start(bf16[256,1152]{1,0:T(8,128)(2,1)S(1)} %constant_dynamic-update-slice_fusion.2.refs_2_), channel_id=1, source_target_pairs={{0,32},{32,0},{1,33},{33,1},{2,34},{34,2},{3,35},{35,3},{4,36},{36... | collective-permute-start | bytes 1769480 | tf_op jit(solution)/shard_map/ppermute | solution.py:62
  47.0 4.7 %collective-permute-start.9 = (bf16[256,1152]{1,0:T(8,128)(2,1)S(1)}, bf16[256,1152]{1,0:T(8,128)(2,1)S(1)}, u32[]{:S(2)}, u32[]{:S(2)}) collective-permute-start(bf16[256,1152]{1,0:T(8,128)(2,1)S(1)} %constant_dynamic-update-slice_fusion.4.refs_3_), channel_id=1, source_target_pairs={{0,32},{32,0},{1,33},{33,1},{2,34},{34,2},{3,35},{35,3},{4,36},{36... | collective-permute-start | bytes 1769480 | tf_op jit(solution)/shard_map/ppermute | solution.py:62
  54.5 19.2 %collective-permute-start.10 = (bf16[256,1152]{1,0:T(8,128)(2,1)S(1)}, bf16[256,1152]{1,0:T(8,128)(2,1)S(1)}, u32[]{:S(2)}, u32[]{:S(2)}) collective-permute-start(bf16[256,1152]{1,0:T(8,128)(2,1)S(1)} %get-tuple-element.21), channel_id=1, source_target_pairs={{4,0},{68,64},{0,4},{64,68},{12,8},{76,72},{8,12},{72,76},{20,16},... | collective-permute-start | bytes 1769480 | tf_op jit(solution)/shard_map/ppermute | solution.py:54
  56.8 16.8 %collective-permute-start.11 = (bf16[256,1152]{1,0:T(8,128)(2,1)S(1)}, bf16[256,1152]{1,0:T(8,128)(2,1)S(1)}, u32[]{:S(2)}, u32[]{:S(2)}) collective-permute-start(bf16[256,1152]{1,0:T(8,128)(2,1)S(1)} %get-tuple-element.22), channel_id=1, source_target_pairs={{28,0},{92,64},{8,4},{72,68},{4,8},{68,72},{16,12},{80,76},{12,16}... | collective-permute-start | bytes 1769480 | tf_op jit(solution)/shard_map/ppermute | solution.py:54
  63.4 10.3 %collective-permute-start.12 = (bf16[192,1152]{1,0:T(8,128)(2,1)S(1)}, bf16[192,1152]{1,0:T(8,128)(2,1)S(1)}, u32[]{:S(2)}, u32[]{:S(2)}) collective-permute-start(bf16[192,1152]{1,0:T(8,128)(2,1)S(1)} %slice.6), channel_id=1, source_target_pairs={{64,0},{0,64},{68,4},{4,68},{72,8},{8,72},{76,12},{12,76},{80,16},... | collective-permute-start | bytes 1327112 | tf_op jit(solution)/shard_map/ppermute | solution.py:54
  68.8 23.2 %copy-start = (bf16[32,1152]{1,0:T(8,128)(2,1)S(1)}, bf16[32,1152]{1,0:T(8,128)(2,1)}, u32[]{:S(2)}) copy-start(bf16[32,1152]{1,0:T(8,128)(2,1)} %image.1) | copy-start | bytes 221188
  68.8 23.2 %copy-start.1 = (bf16[32,1152]{1,0:T(8,128)(2,1)S(1)}, bf16[32,1152]{1,0:T(8,128)(2,1)}, u32[]{:S(2)}) copy-start(bf16[32,1152]{1,0:T(8,128)(2,1)} %text.1) | copy-start | bytes 221188
  74.8 14.9 %all-to-all-start.1 = ((bf16[4,64,1152]{2,1,0:T(8,128)(2,1)}), bf16[4,64,1152]{2,1,0:T(8,128)(2,1)S(1)}, u32[]{:S(2)}, u32[]{:S(2)}) async-start(bf16[4,64,1152]{2,1,0:T(8,128)(2,1)} %merge.1), calls=%async_computation.1 | async-start | bytes 1179648 | tf_op jit(solution)/shard_map/all_to_all | solution.py:58
  78.5 11.1 %collective-permute-start.13 = (bf16[64,1152]{1,0:T(8,128)(2,1)S(1)}, bf16[64,1152]{1,0:T(8,128)(2,1)S(1)}, u32[]{:S(2)}, u32[]{:S(2)}) collective-permute-start(bf16[64,1152]{1,0:T(8,128)(2,1)S(1)} %slice.7), channel_id=1, source_target_pairs={{64,0},{0,64},{68,4},{4,68},{72,8},{8,72},{76,12},{12,76},{80,16},... | collective-permute-start | bytes 442376 | tf_op jit(solution)/shard_map/ppermute | solution.py:54

commit v11 on v10

--- a/solution.py
+++ b/solution.py
@@ -212,14 +212,17 @@
     other[...] = total[rows:, :]
 
 
-def finish_kernel(scalars, summed, pair, image, text, grad_image, grad_text):
+def unit_kernel(image, text, img_unit, txt_unit, img_inv, txt_inv):
+    img_unit[...], img_inv[...] = unit_rows(image[...])
+    txt_unit[...], txt_inv[...] = unit_rows(text[...])
+
+
+def finish_kernel(scalars, summed, pair, img_unit, txt_unit, img_inv, txt_inv, grad_image, grad_text):
     speaks_text = lax.axis_index("c") == 0
     scale = scalars[0:1, 0:1]
     own, other = scale * summed[...], scale * from_other_core(pair)
-    img_unit, img_inv = unit_rows(image[...])
-    txt_unit, txt_inv = unit_rows(text[...])
-    grad_image[...] = project_back(jnp.where(speaks_text, other, own), img_unit, img_inv)
-    grad_text[...] = project_back(jnp.where(speaks_text, own, other), txt_unit, txt_inv)
+    grad_image[...] = project_back(jnp.where(speaks_text, other, own), img_unit[...], img_inv[...])
+    grad_text[...] = project_back(jnp.where(speaks_text, own, other), txt_unit[...], txt_inv[...])
 
 
 VMEM = pl.BlockSpec(memory_space=pltpu.VMEM)
@@ -300,18 +303,16 @@
         for block, neighbour in zip((blocks[0], blocks[1], blocks[2][size:]), NEIGHBOURS)
     ]
     head = swap_with(blocks[2][:size], NEIGHBOURS[2])
+    full = jax.ShapeDtypeStruct((rows, width), jnp.float32)
+    column = jax.ShapeDtypeStruct((rows, 1), jnp.float32)
+    units = small_call(unit_kernel, [full, full, column, column], [image_emb, text_emb], "units")
+    mine[0], units = lax.optimization_barrier((mine[0], units))
     (summed,) = tile((0,), [], jnp.float32)
     (merged,) = small_call(merge_kernel, [spread], [summed, first, second, tail], "merge")
     out = jax.ShapeDtypeStruct((rows, width), jnp.float32)
     own, other = small_call(sum_kernel, [out, out], [exchange(merged), head], "sum")
-    return pl.pallas_call(
-        finish_kernel,
-        out_shape=(out, out),
-        in_specs=[VMEM] * 5,
-        out_specs=(VMEM, VMEM),
-        compiler_params=SMALL,
-        name="finish",
-    )(scalars, own, gather_cores(other), image_emb, text_emb)
+    operands = [scalars, own, gather_cores(other), *units]
+    return tuple(small_call(finish_kernel, [out, out], operands, "finish"))
 
 
 def solution(mesh):

time: 94 us -> 94 us (level)
    pallas_call x4 -> x6, Pallas kernels: 2.23 us -> 3.27 us  [small_call(): pl.pallas_call(kernel, out_shape=out_shape, in_specs=[VMEM] * len(operand...]
    pallas_call x1 -> x0, Pallas kernels: 0.94 us -> none  [per_device(): pl.pallas_call(finish_kernel, out_shape=(out, out), in_specs=[VMEM] * 5,...]
where the time goes in v11:
time: 94 us; the launch traced here: 92.9 us
  starting transfers between devices  57.9 us (62%)
  waiting for transfers between devices  10.9 us (12%)
  blocking collectives  10.7 us (11%)
  Pallas kernels  9.63 us (10%)
  between operations  2.27 us (2%)
  other arithmetic  1.02 us (1%)
    ppermute x10, starting transfers between devices, swap_with(): return lax.ppermute(block, NAMES, pairs)  38.6 us
    ppermute x10, waiting for transfers between devices, swap_with(): return lax.ppermute(block, NAMES, pairs)  10.9 us
    all_gather x2, blocking collectives, gather_cores(): return lax.all_gather(block, 'c', axis=0, tiled=True)  10.7 us
    all_to_all x2, starting transfers between devices, exchange(): lax.all_to_all(blocks, NAMES, 0, 0, axis_index_groups=color_groups(), til...  10.6 us
    ppermute x4, starting transfers between devices, swap_cores(): return lax.ppermute(block, 'c', [(0, 1), (1, 0)])  8.65 us
    pallas_call x3, Pallas kernels, call(): pl.pallas_call(kernel, out_shape=out_shape, in_specs=[VMEM] * len(operand...  6.36 us
    pallas_call x6, Pallas kernels, small_call(): pl.pallas_call(kernel, out_shape=out_shape, in_specs=[VMEM] * len(operand...  3.27 us
  transfers between devices with their start and end apart: 16, of which 3 were waited for; matrix products, arithmetic and copies ran while one was open for 1% of the time, Pallas kernels for 4%

profile of v11, /device:TPU:1, one launch (start us, length us, event | category | flops | bytes accessed | tf_op | source)
XLA Modules:
  0.0 92.9 jit_solution(4861090866602447421)
XLA Ops:
  0.6 0.9 %broadcast_select_fusion = (bf16[32,1152]{1,0:T(8,128)(2,1)S(1)}, bf16[32,1152]{1,0:T(8,128)(2,1)S(1)}) fusion(bf16[32,1152]{1,0:T(8,128)(2,1)} %image.1, bf16[32,1152]{1,0:T(8,128)(2,1)} %text.1, pred[]{:T(512)S(6)} %eq.3), kind=kLoop, calls=%fused_computation | loop fusion | flops 73728 | bytes 294913 | tf_op jit(solution)/shard_map/jit(_where)/select_n | solution.py:241
  1.6 8.4 %all_gather.6.pair = bf16[64,1152]{1,0:T(8,128)(2,1)S(1)} all-gather(bf16[32,1152]{1,0:T(8,128)(2,1)S(1)} %get-tuple-element.44), channel_id=1, replica_groups=mesh['zl'=2,'xh'=2,'xl'=2,'c'=2,'y'=8,'zh'=4] {'c'}, dimensions={0}, use_global_device_ids=true | all-gather | bytes 221184 | tf_op jit(solution)/shard_map/all_gather | solution.py:66
  10.0 1.0 %spread.1 = (bf16[4,64,1152]{2,1,0:T(8,128)(2,1)}, bf16[64,1152]{1,0:T(8,128)(2,1)S(1)}) custom-call(bf16[32,1152]{1,0:T(8,128)(2,1)S(1)} %get-tuple-element.45.own, bf16[64,1152]{1,0:T(8,128)(2,1)S(1)} %all_gather.6.pair), custom_call_target="tpu_custom_call" | custom-call | tf_op jit(solution)/shard_map/spread/pallas_call | solution.py:246
  11.0 6.8 %all-to-all-start = ((bf16[4,64,1152]{2,1,0:T(8,128)(2,1)}), bf16[4,64,1152]{2,1,0:T(8,128)(2,1)S(1)}, u32[]{:S(2)}, u32[]{:S(2)}) async-start(bf16[4,64,1152]{2,1,0:T(8,128)(2,1)} %get-tuple-element.23), calls=%async_computation | async-start | bytes 1179648 | tf_op jit(solution)/shard_map/all_to_all | solution.py:58
  17.9 3.1 %collective-permute-start.1 = (bf16[64,1152]{1,0:T(8,128)(2,1)S(1)}, bf16[64,1152]{1,0:T(8,128)(2,1)S(1)}, u32[]{:S(2)}, u32[]{:S(2)}) collective-permute-start(bf16[64,1152]{1,0:T(8,128)(2,1)S(1)} %get-tuple-element.30), channel_id=1, source_target_pairs={{4,0},{68,64},{0,4},{64,68},{12,8},{76,72},{8,12},{72,76},{20,16},... | collective-permute-start | bytes 442376 | tf_op jit(solution)/shard_map/ppermute | solution.py:54
  21.0 4.5 %collective-permute-start.4 = (bf16[64,1152]{1,0:T(8,128)(2,1)S(1)}, bf16[64,1152]{1,0:T(8,128)(2,1)S(1)}, u32[]{:S(2)}, u32[]{:S(2)}) collective-permute-start(bf16[64,1152]{1,0:T(8,128)(2,1)S(1)} %get-tuple-element.30), channel_id=1, source_target_pairs={{28,0},{92,64},{8,4},{72,68},{4,8},{68,72},{16,12},{80,76},{12,16}... | collective-permute-start | bytes 442376 | tf_op jit(solution)/shard_map/ppermute | solution.py:54
  25.5 4.3 %collective-permute-start.7 = (bf16[64,1152]{1,0:T(8,128)(2,1)S(1)}, bf16[64,1152]{1,0:T(8,128)(2,1)S(1)}, u32[]{:S(2)}, u32[]{:S(2)}) collective-permute-start(bf16[64,1152]{1,0:T(8,128)(2,1)S(1)} %get-tuple-element.30), channel_id=1, source_target_pairs={{64,0},{0,64},{68,4},{4,68},{72,8},{8,72},{76,12},{12,76},{80,16},... | collective-permute-start | bytes 442376 | tf_op jit(solution)/shard_map/ppermute | solution.py:54
  31.1 0.1 maximum_bitcast_fusion.refs_0_.scalars
  31.2 0.0 all-to-all-done.gathered
  31.2 0.1 order.1
  31.3 3.4 %collective-permute-start.2 = (bf16[192,1152]{1,0:T(8,128)(2,1)S(1)}, bf16[192,1152]{1,0:T(8,128)(2,1)S(1)}, u32[]{:S(2)}, u32[]{:S(2)}) collective-permute-start(bf16[192,1152]{1,0:T(8,128)(2,1)S(1)} %get-tuple-element.31), channel_id=1, source_target_pairs={{4,0},{68,64},{0,4},{64,68},{12,8},{76,72},{8,12},{72,76},{20,16},... | collective-permute-start | bytes 1327112 | tf_op jit(solution)/shard_map/ppermute | solution.py:54
  34.7 0.0 collective-permute-done.1
  34.7 1.9 %collective-permute-start.5 = (bf16[192,1152]{1,0:T(8,128)(2,1)S(1)}, bf16[192,1152]{1,0:T(8,128)(2,1)S(1)}, u32[]{:S(2)}, u32[]{:S(2)}) collective-permute-start(bf16[192,1152]{1,0:T(8,128)(2,1)S(1)} %get-tuple-element.31), channel_id=1, source_target_pairs={{28,0},{92,64},{8,4},{72,68},{4,8},{68,72},{16,12},{80,76},{12,16}... | collective-permute-start | bytes 1327112 | tf_op jit(solution)/shard_map/ppermute | solution.py:54
  36.6 0.0 collective-permute-done.4
  36.7 3.1 %collective-permute-start.8 = (bf16[192,1152]{1,0:T(8,128)(2,1)S(1)}, bf16[192,1152]{1,0:T(8,128)(2,1)S(1)}, u32[]{:S(2)}, u32[]{:S(2)}) collective-permute-start(bf16[192,1152]{1,0:T(8,128)(2,1)S(1)} %get-tuple-element.31), channel_id=1, source_target_pairs={{64,0},{0,64},{68,4},{4,68},{72,8},{8,72},{76,12},{12,76},{80,16},... | collective-permute-start | bytes 1327112 | tf_op jit(solution)/shard_map/ppermute | solution.py:54
  39.8 1.9 %collective-permute-start = (bf16[256,1152]{1,0:T(8,128)(2,1)S(1)}, bf16[256,1152]{1,0:T(8,128)(2,1)S(1)}, u32[]{:S(2)}, u32[]{:S(2)}) collective-permute-start(bf16[256,1152]{1,0:T(8,128)(2,1)S(1)} %get-tuple-element.29.refs_1_), channel_id=1, source_target_pairs={{0,32},{32,0},{1,33},{33,1},{2,34},{34,2},{3,35},{35,3},{4,36},{36... | collective-permute-start | bytes 1769480 | tf_op jit(solution)/shard_map/ppermute | solution.py:62
  41.7 0.0 collective-permute-done.2
  41.7 2.4 %collective-permute-start.3 = (bf16[256,1152]{1,0:T(8,128)(2,1)S(1)}, bf16[256,1152]{1,0:T(8,128)(2,1)S(1)}, u32[]{:S(2)}, u32[]{:S(2)}) collective-permute-start(bf16[256,1152]{1,0:T(8,128)(2,1)S(1)} %constant_dynamic-update-slice_fusion.refs_1_), channel_id=1, source_target_pairs={{0,32},{32,0},{1,33},{33,1},{2,34},{34,2},{3,35},{35,3},{4,36},{36... | collective-permute-start | bytes 1769480 | tf_op jit(solution)/shard_map/ppermute | solution.py:62
  44.2 0.8 collective-permute-done.5
  45.0 1.9 %collective-permute-start.6 = (bf16[256,1152]{1,0:T(8,128)(2,1)S(1)}, bf16[256,1152]{1,0:T(8,128)(2,1)S(1)}, u32[]{:S(2)}, u32[]{:S(2)}) collective-permute-start(bf16[256,1152]{1,0:T(8,128)(2,1)S(1)} %constant_dynamic-update-slice_fusion.2.refs_2_), channel_id=1, source_target_pairs={{0,32},{32,0},{1,33},{33,1},{2,34},{34,2},{3,35},{35,3},{4,36},{36... | collective-permute-start | bytes 1769480 | tf_op jit(solution)/shard_map/ppermute | solution.py:62
  46.9 0.0 collective-permute-done.7
  47.0 0.0 collective-permute-done.8
  47.0 2.4 %collective-permute-start.9 = (bf16[256,1152]{1,0:T(8,128)(2,1)S(1)}, bf16[256,1152]{1,0:T(8,128)(2,1)S(1)}, u32[]{:S(2)}, u32[]{:S(2)}) collective-permute-start(bf16[256,1152]{1,0:T(8,128)(2,1)S(1)} %constant_dynamic-update-slice_fusion.4.refs_3_), channel_id=1, source_target_pairs={{0,32},{32,0},{1,33},{33,1},{2,34},{34,2},{3,35},{35,3},{4,36},{36... | collective-permute-start | bytes 1769480 | tf_op jit(solution)/shard_map/ppermute | solution.py:62
  49.4 0.0 collective-permute-done.refs_4_
  49.5 0.0 collective-permute-done.3.refs_5_
  49.5 0.0 collective-permute-done.6.refs_6_
  49.5 2.0 %weigh.1 = (bf16[256,768]{1,0:T(8,128)(2,1)S(1)}, bf16[256,768]{1,0:T(8,128)(2,1)S(1)}, bf16[256,768]{1,0:T(8,128)(2,1)S(1)}) custom-call(f32[1,2]{1,0:T(1,128)S(1)} %maximum_bitcast_fusion.refs_0_.scalars, bf16[256,1152]{1,0:T(8,128)(2,1)S(1)} %constant_dynamic-update-slice_fusion.refs_1_, ...), custom_call_target="tpu_custom_call" | custom-call | flops 1358954496 | bytes 3538948 | tf_op jit(solution)/shard_map/weigh/pallas_call | solution.py:270
  51.5 0.1 constant_dynamic-update-slice_fusion.8
  51.6 0.1 constant_dynamic-update-slice_fusion.7
  51.7 0.0 collective-permute-done.9
  51.7 0.1 constant_dynamic-update-slice_fusion.6.refs_2_.refs_7_
  51.8 0.0 copy-start
  51.8 0.0 copy-start.1
  51.8 2.8 %tile.3 = (bf16[256,1152]{1,0:T(8,128)(2,1)S(1)}, bf16[256,1152]{1,0:T(8,128)(2,1)S(1)}, bf16[256,1152]{1,0:T(8,128)(2,1)S(1)}) custom-call(f32[1,2]{1,0:T(1,128)S(1)} %maximum_bitcast_fusion.refs_0_.scalars, bf16[256,1152]{1,0:T(8,128)(2,1)S(1)} %constant_dynamic-update-slice_fusion.refs_1_, ...), custom_call_target="tpu_custom_call" | custom-call | flops 2264924160 | bytes 5308420 | tf_op jit(solution)/shard_map/tile/pallas_call | solution.py:270
  54.6 2.3 %collective-permute-start.10 = (bf16[256,1152]{1,0:T(8,128)(2,1)S(1)}, bf16[256,1152]{1,0:T(8,128)(2,1)S(1)}, u32[]{:S(2)}, u32[]{:S(2)}) collective-permute-start(bf16[256,1152]{1,0:T(8,128)(2,1)S(1)} %get-tuple-element.35), channel_id=1, source_target_pairs={{4,0},{68,64},{0,4},{64,68},{12,8},{76,72},{8,12},{72,76},{20,16},... | collective-permute-start | bytes 1769480 | tf_op jit(solution)/shard_map/ppermute | solution.py:54
  56.9 6.5 %collective-permute-start.11 = (bf16[256,1152]{1,0:T(8,128)(2,1)S(1)}, bf16[256,1152]{1,0:T(8,128)(2,1)S(1)}, u32[]{:S(2)}, u32[]{:S(2)}) collective-permute-start(bf16[256,1152]{1,0:T(8,128)(2,1)S(1)} %get-tuple-element.36), channel_id=1, source_target_pairs={{28,0},{92,64},{8,4},{72,68},{4,8},{68,72},{16,12},{80,76},{12,16}... | collective-permute-start | bytes 1769480 | tf_op jit(solution)/shard_map/ppermute | solution.py:54
  63.5 3.7 %collective-permute-start.12 = (bf16[192,1152]{1,0:T(8,128)(2,1)S(1)}, bf16[192,1152]{1,0:T(8,128)(2,1)S(1)}, u32[]{:S(2)}, u32[]{:S(2)}) collective-permute-start(bf16[192,1152]{1,0:T(8,128)(2,1)S(1)} %slice.6), channel_id=1, source_target_pairs={{64,0},{0,64},{68,4},{4,68},{72,8},{8,72},{76,12},{12,76},{80,16},... | collective-permute-start | bytes 1327112 | tf_op jit(solution)/shard_map/ppermute | solution.py:54
  67.2 0.0 copy-done
  67.2 0.0 copy-done.1
  67.2 0.1 units.1
  67.3 1.6 %tile.2.mine = f32[256,1152]{1,0:T(8,128)S(1)} custom-call(f32[1,2]{1,0:T(1,128)S(1)} %maximum_bitcast_fusion.refs_0_.scalars, bf16[256,1152]{1,0:T(8,128)(2,1)S(1)} %get-tuple-element.29.refs_1_, bf16[1024,1152]{1,0:T(8,128)(2,1)S(1)} %constant_dynamic-update-slice_fusion.6.refs_2_.refs_7_), custom_call_target="tpu_custom_call" | custom-call | flops 1207959552 | bytes 2949124 | tf_op jit(solution)/shard_map/tile/pallas_call | solution.py:270
  69.0 4.8 %collective-permute-done.12.tail = bf16[192,1152]{1,0:T(8,128)(2,1)S(1)} collective-permute-done((bf16[192,1152]{1,0:T(8,128)(2,1)S(1)}, bf16[192,1152]{1,0:T(8,128)(2,1)S(1)}, u32[]{:S(2)}, u32[]{:S(2)}) %collective-permute-start.12) | collective-permute-done | bytes 442400 | tf_op jit(solution)/shard_map/ppermute | solution.py:54
  73.7 0.0 collective-permute-done.10.first
  73.7 0.0 collective-permute-done.11.second
  73.7 1.1 %merge.1 = bf16[4,64,1152]{2,1,0:T(8,128)(2,1)} custom-call(f32[256,1152]{1,0:T(8,128)S(1)} %tile.2.mine, bf16[256,1152]{1,0:T(8,128)(2,1)S(1)} %collective-permute-done.10.first, bf16[256,1152]{1,0:T(8,128)(2,1)S(1)} %collective-permute-done.11.second, bf16[192,1152]{1,0:T(8,128)(2,1)S(1)} %collective-permute-done.12.tail), custom_call_target="tpu_custom_call" | custom-call | tf_op jit(solution)/shard_map/merge/pallas_call | solution.py:246
  74.8 3.7 %all-to-all-start.1 = ((bf16[4,64,1152]{2,1,0:T(8,128)(2,1)}), bf16[4,64,1152]{2,1,0:T(8,128)(2,1)S(1)}, u32[]{:S(2)}, u32[]{:S(2)}) async-start(bf16[4,64,1152]{2,1,0:T(8,128)(2,1)} %merge.1), calls=%async_computation.1 | async-start | bytes 1179648 | tf_op jit(solution)/shard_map/all_to_all | solution.py:58
  78.6 5.7 %collective-permute-start.13 = (bf16[64,1152]{1,0:T(8,128)(2,1)S(1)}, bf16[64,1152]{1,0:T(8,128)(2,1)S(1)}, u32[]{:S(2)}, u32[]{:S(2)}) collective-permute-start(bf16[64,1152]{1,0:T(8,128)(2,1)S(1)} %slice.7), channel_id=1, source_target_pairs={{64,0},{0,64},{68,4},{4,68},{72,8},{8,72},{76,12},{12,76},{80,16},... | collective-permute-start | bytes 442376 | tf_op jit(solution)/shard_map/ppermute | solution.py:54
  84.3 5.4 %collective-permute-done.13.head = bf16[64,1152]{1,0:T(8,128)(2,1)S(1)} collective-permute-done((bf16[64,1152]{1,0:T(8,128)(2,1)S(1)}, bf16[64,1152]{1,0:T(8,128)(2,1)S(1)}, u32[]{:S(2)}, u32[]{:S(2)}) %collective-permute-start.13) | collective-permute-done | bytes 147488 | tf_op jit(solution)/shard_map/ppermute | solution.py:54
  89.7 0.0 all-to-all-done.1.parts
  89.7 0.1 sum.1
  89.8 2.2 %all_gather.7.pair = f32[64,1152]{1,0:T(8,128)S(1)} all-gather(f32[32,1152]{1,0:T(8,128)S(1)} %get-tuple-element.39), channel_id=1, replica_groups=mesh['zl'=2,'xh'=2,'xl'=2,'c'=2,'y'=8,'zh'=4] {'c'}, dimensions={0}, use_global_device_ids=true | all-gather | bytes 442368 | tf_op jit(solution)/shard_map/all_gather | solution.py:66
  92.0 0.9 finish.1
  (9 shorter events, 0.3 us)
Async XLA Ops:
  11.0 20.2 %all-to-all-start = ((bf16[4,64,1152]{2,1,0:T(8,128)(2,1)}), bf16[4,64,1152]{2,1,0:T(8,128)(2,1)S(1)}, u32[]{:S(2)}, u32[]{:S(2)}) async-start(bf16[4,64,1152]{2,1,0:T(8,128)(2,1)} %get-tuple-element.23), calls=%async_computation | async-start | bytes 1179648 | tf_op jit(solution)/shard_map/all_to_all | solution.py:58
  17.9 16.8 %collective-permute-start.1 = (bf16[64,1152]{1,0:T(8,128)(2,1)S(1)}, bf16[64,1152]{1,0:T(8,128)(2,1)S(1)}, u32[]{:S(2)}, u32[]{:S(2)}) collective-permute-start(bf16[64,1152]{1,0:T(8,128)(2,1)S(1)} %get-tuple-element.30), channel_id=1, source_target_pairs={{4,0},{68,64},{0,4},{64,68},{12,8},{76,72},{8,12},{72,76},{20,16},... | collective-permute-start | bytes 442376 | tf_op jit(solution)/shard_map/ppermute | solution.py:54
  21.0 15.7 %collective-permute-start.4 = (bf16[64,1152]{1,0:T(8,128)(2,1)S(1)}, bf16[64,1152]{1,0:T(8,128)(2,1)S(1)}, u32[]{:S(2)}, u32[]{:S(2)}) collective-permute-start(bf16[64,1152]{1,0:T(8,128)(2,1)S(1)} %get-tuple-element.30), channel_id=1, source_target_pairs={{28,0},{92,64},{8,4},{72,68},{4,8},{68,72},{16,12},{80,76},{12,16}... | collective-permute-start | bytes 442376 | tf_op jit(solution)/shard_map/ppermute | solution.py:54
  25.5 21.4 %collective-permute-start.7 = (bf16[64,1152]{1,0:T(8,128)(2,1)S(1)}, bf16[64,1152]{1,0:T(8,128)(2,1)S(1)}, u32[]{:S(2)}, u32[]{:S(2)}) collective-permute-start(bf16[64,1152]{1,0:T(8,128)(2,1)S(1)} %get-tuple-element.30), channel_id=1, source_target_pairs={{64,0},{0,64},{68,4},{4,68},{72,8},{8,72},{76,12},{12,76},{80,16},... | collective-permute-start | bytes 442376 | tf_op jit(solution)/shard_map/ppermute | solution.py:54
  31.3 10.4 %collective-permute-start.2 = (bf16[192,1152]{1,0:T(8,128)(2,1)S(1)}, bf16[192,1152]{1,0:T(8,128)(2,1)S(1)}, u32[]{:S(2)}, u32[]{:S(2)}) collective-permute-start(bf16[192,1152]{1,0:T(8,128)(2,1)S(1)} %get-tuple-element.31), channel_id=1, source_target_pairs={{4,0},{68,64},{0,4},{64,68},{12,8},{76,72},{8,12},{72,76},{20,16},... | collective-permute-start | bytes 1327112 | tf_op jit(solution)/shard_map/ppermute | solution.py:54
  34.7 10.3 %collective-permute-start.5 = (bf16[192,1152]{1,0:T(8,128)(2,1)S(1)}, bf16[192,1152]{1,0:T(8,128)(2,1)S(1)}, u32[]{:S(2)}, u32[]{:S(2)}) collective-permute-start(bf16[192,1152]{1,0:T(8,128)(2,1)S(1)} %get-tuple-element.31), channel_id=1, source_target_pairs={{28,0},{92,64},{8,4},{72,68},{4,8},{68,72},{16,12},{80,76},{12,16}... | collective-permute-start | bytes 1327112 | tf_op jit(solution)/shard_map/ppermute | solution.py:54
  36.7 10.3 %collective-permute-start.8 = (bf16[192,1152]{1,0:T(8,128)(2,1)S(1)}, bf16[192,1152]{1,0:T(8,128)(2,1)S(1)}, u32[]{:S(2)}, u32[]{:S(2)}) collective-permute-start(bf16[192,1152]{1,0:T(8,128)(2,1)S(1)} %get-tuple-element.31), channel_id=1, source_target_pairs={{64,0},{0,64},{68,4},{4,68},{72,8},{8,72},{76,12},{12,76},{80,16},... | collective-permute-start | bytes 1327112 | tf_op jit(solution)/shard_map/ppermute | solution.py:54
  39.8 9.7 %collective-permute-start = (bf16[256,1152]{1,0:T(8,128)(2,1)S(1)}, bf16[256,1152]{1,0:T(8,128)(2,1)S(1)}, u32[]{:S(2)}, u32[]{:S(2)}) collective-permute-start(bf16[256,1152]{1,0:T(8,128)(2,1)S(1)} %get-tuple-element.29.refs_1_), channel_id=1, source_target_pairs={{0,32},{32,0},{1,33},{33,1},{2,34},{34,2},{3,35},{35,3},{4,36},{36... | collective-permute-start | bytes 1769480 | tf_op jit(solution)/shard_map/ppermute | solution.py:62
  41.7 7.8 %collective-permute-start.3 = (bf16[256,1152]{1,0:T(8,128)(2,1)S(1)}, bf16[256,1152]{1,0:T(8,128)(2,1)S(1)}, u32[]{:S(2)}, u32[]{:S(2)}) collective-permute-start(bf16[256,1152]{1,0:T(8,128)(2,1)S(1)} %constant_dynamic-update-slice_fusion.refs_1_), channel_id=1, source_target_pairs={{0,32},{32,0},{1,33},{33,1},{2,34},{34,2},{3,35},{35,3},{4,36},{36... | collective-permute-start | bytes 1769480 | tf_op jit(solution)/shard_map/ppermute | solution.py:62
  45.0 4.5 %collective-permute-start.6 = (bf16[256,1152]{1,0:T(8,128)(2,1)S(1)}, bf16[256,1152]{1,0:T(8,128)(2,1)S(1)}, u32[]{:S(2)}, u32[]{:S(2)}) collective-permute-start(bf16[256,1152]{1,0:T(8,128)(2,1)S(1)} %constant_dynamic-update-slice_fusion.2.refs_2_), channel_id=1, source_target_pairs={{0,32},{32,0},{1,33},{33,1},{2,34},{34,2},{3,35},{35,3},{4,36},{36... | collective-permute-start | bytes 1769480 | tf_op jit(solution)/shard_map/ppermute | solution.py:62
  47.0 4.7 %collective-permute-start.9 = (bf16[256,1152]{1,0:T(8,128)(2,1)S(1)}, bf16[256,1152]{1,0:T(8,128)(2,1)S(1)}, u32[]{:S(2)}, u32[]{:S(2)}) collective-permute-start(bf16[256,1152]{1,0:T(8,128)(2,1)S(1)} %constant_dynamic-update-slice_fusion.4.refs_3_), channel_id=1, source_target_pairs={{0,32},{32,0},{1,33},{33,1},{2,34},{34,2},{3,35},{35,3},{4,36},{36... | collective-permute-start | bytes 1769480 | tf_op jit(solution)/shard_map/ppermute | solution.py:62
  51.8 15.4 %copy-start = (bf16[32,1152]{1,0:T(8,128)(2,1)S(1)}, bf16[32,1152]{1,0:T(8,128)(2,1)}, u32[]{:S(2)}) copy-start(bf16[32,1152]{1,0:T(8,128)(2,1)} %image.1) | copy-start | bytes 221188
  51.8 15.4 %copy-start.1 = (bf16[32,1152]{1,0:T(8,128)(2,1)S(1)}, bf16[32,1152]{1,0:T(8,128)(2,1)}, u32[]{:S(2)}) copy-start(bf16[32,1152]{1,0:T(8,128)(2,1)} %text.1) | copy-start | bytes 221188
  54.6 19.2 %collective-permute-start.10 = (bf16[256,1152]{1,0:T(8,128)(2,1)S(1)}, bf16[256,1152]{1,0:T(8,128)(2,1)S(1)}, u32[]{:S(2)}, u32[]{:S(2)}) collective-permute-start(bf16[256,1152]{1,0:T(8,128)(2,1)S(1)} %get-tuple-element.35), channel_id=1, source_target_pairs={{4,0},{68,64},{0,4},{64,68},{12,8},{76,72},{8,12},{72,76},{20,16},... | collective-permute-start | bytes 1769480 | tf_op jit(solution)/shard_map/ppermute | solution.py:54
  56.9 16.8 %collective-permute-start.11 = (bf16[256,1152]{1,0:T(8,128)(2,1)S(1)}, bf16[256,1152]{1,0:T(8,128)(2,1)S(1)}, u32[]{:S(2)}, u32[]{:S(2)}) collective-permute-start(bf16[256,1152]{1,0:T(8,128)(2,1)S(1)} %get-tuple-element.36), channel_id=1, source_target_pairs={{28,0},{92,64},{8,4},{72,68},{4,8},{68,72},{16,12},{80,76},{12,16}... | collective-permute-start | bytes 1769480 | tf_op jit(solution)/shard_map/ppermute | solution.py:54
  63.5 10.3 %collective-permute-start.12 = (bf16[192,1152]{1,0:T(8,128)(2,1)S(1)}, bf16[192,1152]{1,0:T(8,128)(2,1)S(1)}, u32[]{:S(2)}, u32[]{:S(2)}) collective-permute-start(bf16[192,1152]{1,0:T(8,128)(2,1)S(1)} %slice.6), channel_id=1, source_target_pairs={{64,0},{0,64},{68,4},{4,68},{72,8},{8,72},{76,12},{12,76},{80,16},... | collective-permute-start | bytes 1327112 | tf_op jit(solution)/shard_map/ppermute | solution.py:54
  74.8 14.9 %all-to-all-start.1 = ((bf16[4,64,1152]{2,1,0:T(8,128)(2,1)}), bf16[4,64,1152]{2,1,0:T(8,128)(2,1)S(1)}, u32[]{:S(2)}, u32[]{:S(2)}) async-start(bf16[4,64,1152]{2,1,0:T(8,128)(2,1)} %merge.1), calls=%async_computation.1 | async-start | bytes 1179648 | tf_op jit(solution)/shard_map/all_to_all | solution.py:58
  78.6 11.1 %collective-permute-start.13 = (bf16[64,1152]{1,0:T(8,128)(2,1)S(1)}, bf16[64,1152]{1,0:T(8,128)(2,1)S(1)}, u32[]{:S(2)}, u32[]{:S(2)}) collective-permute-start(bf16[64,1152]{1,0:T(8,128)(2,1)S(1)} %slice.7), channel_id=1, source_target_pairs={{64,0},{0,64},{68,4},{4,68},{72,8},{8,72},{76,12},{12,76},{80,16},... | collective-permute-start | bytes 442376 | tf_op jit(solution)/shard_map/ppermute | solution.py:54

commit v12 on v11

--- a/solution.py
+++ b/solution.py
@@ -197,17 +197,20 @@
 def merge_kernel(mine, first, second, tail, blocks):
     size = blocks.shape[1]
     member = own_member()
-    for j in range(COLORS):
+    blocks[member] = jnp.zeros(blocks.shape[1:], blocks.dtype)
+    for j in range(1, COLORS):
         place = slice(j * size, (j + 1) * size)
         total = mine[place, :] + first[place, :].astype(jnp.float32) + second[place, :].astype(jnp.float32)
-        if j > 0:
-            total = total + tail[(j - 1) * size : j * size, :].astype(jnp.float32)
+        total = total + tail[(j - 1) * size : j * size, :].astype(jnp.float32)
         blocks[member ^ j] = total.astype(blocks.dtype)
 
 
-def sum_kernel(parts, head, own, other):
+def sum_kernel(parts, mine, first, second, head, own, other):
     rows = own.shape[0]
-    total = head[...].astype(jnp.float32) + jnp.sum(parts[...].astype(jnp.float32), axis=0)
+    size = parts.shape[1]
+    total = mine[:size, :] + jnp.sum(parts[...].astype(jnp.float32), axis=0)
+    for received in (first, second, head):
+        total = total + received[:size, :].astype(jnp.float32)
     own[...] = total[:rows, :]
     other[...] = total[rows:, :]
 
@@ -310,7 +313,7 @@
     (summed,) = tile((0,), [], jnp.float32)
     (merged,) = small_call(merge_kernel, [spread], [summed, first, second, tail], "merge")
     out = jax.ShapeDtypeStruct((rows, width), jnp.float32)
-    own, other = small_call(sum_kernel, [out, out], [exchange(merged), head], "sum")
+    own, other = small_call(sum_kernel, [out, out], [exchange(merged), summed, first, second, head], "sum")
     operands = [scalars, own, gather_cores(other), *units]
     return tuple(small_call(finish_kernel, [out, out], operands, "finish"))
 

time: 94 us -> 93.9 us (level)
  local copies, waits for them, and re-layouts: 0.49 us -> 3.05 us
  waiting for transfers between devices: 10.9 us -> 8.38 us
    ppermute x10, waiting for transfers between devices: 10.9 us -> 8.36 us  [swap_with(): return lax.ppermute(block, NAMES, pairs)]
    unnamed x10 -> x28, local copies, waits for them, and re-layouts: 0.24 us -> 2.8 us
where the time goes in v12:
time: 93.9 us; the launch traced here: 92.8 us
  starting transfers between devices  58 us (62%)
  blocking collectives  10.5 us (11%)
  Pallas kernels  9.56 us (10%)
  waiting for transfers between devices  8.38 us (9%)
  local copies, waits for them, and re-layouts  3.05 us (3%)
  between operations  2.32 us (2%)
  other arithmetic  1.02 us (1%)
    ppermute x10, starting transfers between devices, swap_with(): return lax.ppermute(block, NAMES, pairs)  38.8 us
    all_to_all x2, starting transfers between devices, exchange(): lax.all_to_all(blocks, NAMES, 0, 0, axis_index_groups=color_groups(), til...  10.6 us
    all_gather x2, blocking collectives, gather_cores(): return lax.all_gather(block, 'c', axis=0, tiled=True)  10.5 us
    ppermute x4, starting transfers between devices, swap_cores(): return lax.ppermute(block, 'c', [(0, 1), (1, 0)])  8.65 us
    ppermute x10, waiting for transfers between devices, swap_with(): return lax.ppermute(block, NAMES, pairs)  8.36 us
    pallas_call x3, Pallas kernels, call(): pl.pallas_call(kernel, out_shape=out_shape, in_specs=[VMEM] * len(operand...  6.36 us
    pallas_call x6, Pallas kernels, small_call(): pl.pallas_call(kernel, out_shape=out_shape, in_specs=[VMEM] * len(operand...  3.2 us
    unnamed x28, local copies, waits for them, and re-layouts  2.8 us
  transfers between devices with their start and end apart: 16, of which 3 were waited for; matrix products, arithmetic and copies ran while one was open for 1% of the time, Pallas kernels for 4%

profile of v12, /device:TPU:1, one launch (start us, length us, event | category | flops | bytes accessed | tf_op | source)
XLA Modules:
  0.0 92.8 jit_solution(605795315007841776)
XLA Ops:
  0.6 0.9 %broadcast_select_fusion = (bf16[32,1152]{1,0:T(8,128)(2,1)S(1)}, bf16[32,1152]{1,0:T(8,128)(2,1)S(1)}) fusion(bf16[32,1152]{1,0:T(8,128)(2,1)} %image.1, bf16[32,1152]{1,0:T(8,128)(2,1)} %text.1, pred[]{:T(512)S(6)} %eq.3), kind=kLoop, calls=%fused_computation | loop fusion | flops 73728 | bytes 294913 | tf_op jit(solution)/shard_map/jit(_where)/select_n | solution.py:244
  1.6 8.4 %all_gather.6.pair = bf16[64,1152]{1,0:T(8,128)(2,1)S(1)} all-gather(bf16[32,1152]{1,0:T(8,128)(2,1)S(1)} %get-tuple-element.44), channel_id=1, replica_groups=mesh['zl'=2,'xh'=2,'xl'=2,'c'=2,'y'=8,'zh'=4] {'c'}, dimensions={0}, use_global_device_ids=true | all-gather | bytes 221184 | tf_op jit(solution)/shard_map/all_gather | solution.py:66
  10.0 1.0 %spread.1 = (bf16[4,64,1152]{2,1,0:T(8,128)(2,1)}, bf16[64,1152]{1,0:T(8,128)(2,1)S(1)}) custom-call(bf16[32,1152]{1,0:T(8,128)(2,1)S(1)} %get-tuple-element.45.own, bf16[64,1152]{1,0:T(8,128)(2,1)S(1)} %all_gather.6.pair), custom_call_target="tpu_custom_call" | custom-call | tf_op jit(solution)/shard_map/spread/pallas_call | solution.py:249
  11.0 6.8 %all-to-all-start = ((bf16[4,64,1152]{2,1,0:T(8,128)(2,1)}), bf16[4,64,1152]{2,1,0:T(8,128)(2,1)S(1)}, u32[]{:S(2)}, u32[]{:S(2)}) async-start(bf16[4,64,1152]{2,1,0:T(8,128)(2,1)} %get-tuple-element.23), calls=%async_computation | async-start | bytes 1179648 | tf_op jit(solution)/shard_map/all_to_all | solution.py:58
  17.8 3.1 %collective-permute-start.1 = (bf16[64,1152]{1,0:T(8,128)(2,1)S(1)}, bf16[64,1152]{1,0:T(8,128)(2,1)S(1)}, u32[]{:S(2)}, u32[]{:S(2)}) collective-permute-start(bf16[64,1152]{1,0:T(8,128)(2,1)S(1)} %get-tuple-element.30), channel_id=1, source_target_pairs={{4,0},{68,64},{0,4},{64,68},{12,8},{76,72},{8,12},{72,76},{20,16},... | collective-permute-start | bytes 442376 | tf_op jit(solution)/shard_map/ppermute | solution.py:54
  20.9 4.5 %collective-permute-start.4 = (bf16[64,1152]{1,0:T(8,128)(2,1)S(1)}, bf16[64,1152]{1,0:T(8,128)(2,1)S(1)}, u32[]{:S(2)}, u32[]{:S(2)}) collective-permute-start(bf16[64,1152]{1,0:T(8,128)(2,1)S(1)} %get-tuple-element.30), channel_id=1, source_target_pairs={{28,0},{92,64},{8,4},{72,68},{4,8},{68,72},{16,12},{80,76},{12,16}... | collective-permute-start | bytes 442376 | tf_op jit(solution)/shard_map/ppermute | solution.py:54
  25.5 4.3 %collective-permute-start.7 = (bf16[64,1152]{1,0:T(8,128)(2,1)S(1)}, bf16[64,1152]{1,0:T(8,128)(2,1)S(1)}, u32[]{:S(2)}, u32[]{:S(2)}) collective-permute-start(bf16[64,1152]{1,0:T(8,128)(2,1)S(1)} %get-tuple-element.30), channel_id=1, source_target_pairs={{64,0},{0,64},{68,4},{4,68},{72,8},{8,72},{76,12},{12,76},{80,16},... | collective-permute-start | bytes 442376 | tf_op jit(solution)/shard_map/ppermute | solution.py:54
  31.1 0.1 maximum_bitcast_fusion.refs_0_.scalars
  31.2 0.0 all-to-all-done.gathered
  31.2 0.1 order.1
  31.3 3.4 %collective-permute-start.2 = (bf16[192,1152]{1,0:T(8,128)(2,1)S(1)}, bf16[192,1152]{1,0:T(8,128)(2,1)S(1)}, u32[]{:S(2)}, u32[]{:S(2)}) collective-permute-start(bf16[192,1152]{1,0:T(8,128)(2,1)S(1)} %get-tuple-element.31), channel_id=1, source_target_pairs={{4,0},{68,64},{0,4},{64,68},{12,8},{76,72},{8,12},{72,76},{20,16},... | collective-permute-start | bytes 1327112 | tf_op jit(solution)/shard_map/ppermute | solution.py:54
  34.6 0.0 collective-permute-done.1
  34.7 1.9 %collective-permute-start.5 = (bf16[192,1152]{1,0:T(8,128)(2,1)S(1)}, bf16[192,1152]{1,0:T(8,128)(2,1)S(1)}, u32[]{:S(2)}, u32[]{:S(2)}) collective-permute-start(bf16[192,1152]{1,0:T(8,128)(2,1)S(1)} %get-tuple-element.31), channel_id=1, source_target_pairs={{28,0},{92,64},{8,4},{72,68},{4,8},{68,72},{16,12},{80,76},{12,16}... | collective-permute-start | bytes 1327112 | tf_op jit(solution)/shard_map/ppermute | solution.py:54
  36.6 0.0 collective-permute-done.4
  36.6 3.1 %collective-permute-start.8 = (bf16[192,1152]{1,0:T(8,128)(2,1)S(1)}, bf16[192,1152]{1,0:T(8,128)(2,1)S(1)}, u32[]{:S(2)}, u32[]{:S(2)}) collective-permute-start(bf16[192,1152]{1,0:T(8,128)(2,1)S(1)} %get-tuple-element.31), channel_id=1, source_target_pairs={{64,0},{0,64},{68,4},{4,68},{72,8},{8,72},{76,12},{12,76},{80,16},... | collective-permute-start | bytes 1327112 | tf_op jit(solution)/shard_map/ppermute | solution.py:54
  39.7 1.9 %collective-permute-start = (bf16[256,1152]{1,0:T(8,128)(2,1)S(1)}, bf16[256,1152]{1,0:T(8,128)(2,1)S(1)}, u32[]{:S(2)}, u32[]{:S(2)}) collective-permute-start(bf16[256,1152]{1,0:T(8,128)(2,1)S(1)} %get-tuple-element.29.refs_1_), channel_id=1, source_target_pairs={{0,32},{32,0},{1,33},{33,1},{2,34},{34,2},{3,35},{35,3},{4,36},{36... | collective-permute-start | bytes 1769480 | tf_op jit(solution)/shard_map/ppermute | solution.py:62
  41.6 0.0 collective-permute-done.2
  41.7 2.4 %collective-permute-start.3 = (bf16[256,1152]{1,0:T(8,128)(2,1)S(1)}, bf16[256,1152]{1,0:T(8,128)(2,1)S(1)}, u32[]{:S(2)}, u32[]{:S(2)}) collective-permute-start(bf16[256,1152]{1,0:T(8,128)(2,1)S(1)} %constant_dynamic-update-slice_fusion.refs_1_), channel_id=1, source_target_pairs={{0,32},{32,0},{1,33},{33,1},{2,34},{34,2},{3,35},{35,3},{4,36},{36... | collective-permute-start | bytes 1769480 | tf_op jit(solution)/shard_map/ppermute | solution.py:62
  44.1 0.8 collective-permute-done.5
  45.0 1.9 %collective-permute-start.6 = (bf16[256,1152]{1,0:T(8,128)(2,1)S(1)}, bf16[256,1152]{1,0:T(8,128)(2,1)S(1)}, u32[]{:S(2)}, u32[]{:S(2)}) collective-permute-start(bf16[256,1152]{1,0:T(8,128)(2,1)S(1)} %constant_dynamic-update-slice_fusion.2.refs_2_), channel_id=1, source_target_pairs={{0,32},{32,0},{1,33},{33,1},{2,34},{34,2},{3,35},{35,3},{4,36},{36... | collective-permute-start | bytes 1769480 | tf_op jit(solution)/shard_map/ppermute | solution.py:62
  46.9 0.0 collective-permute-done.7
  46.9 0.0 collective-permute-done.8
  47.0 2.4 %collective-permute-start.9 = (bf16[256,1152]{1,0:T(8,128)(2,1)S(1)}, bf16[256,1152]{1,0:T(8,128)(2,1)S(1)}, u32[]{:S(2)}, u32[]{:S(2)}) collective-permute-start(bf16[256,1152]{1,0:T(8,128)(2,1)S(1)} %constant_dynamic-update-slice_fusion.4.refs_3_), channel_id=1, source_target_pairs={{0,32},{32,0},{1,33},{33,1},{2,34},{34,2},{3,35},{35,3},{4,36},{36... | collective-permute-start | bytes 1769480 | tf_op jit(solution)/shard_map/ppermute | solution.py:62
  49.4 0.0 collective-permute-done.refs_4_
  49.5 0.0 collective-permute-done.3.refs_5_
  49.5 0.0 collective-permute-done.6.refs_6_
  49.5 2.0 %weigh.1 = (bf16[256,768]{1,0:T(8,128)(2,1)S(1)}, bf16[256,768]{1,0:T(8,128)(2,1)S(1)}, bf16[256,768]{1,0:T(8,128)(2,1)S(1)}) custom-call(f32[1,2]{1,0:T(1,128)S(1)} %maximum_bitcast_fusion.refs_0_.scalars, bf16[256,1152]{1,0:T(8,128)(2,1)S(1)} %constant_dynamic-update-slice_fusion.refs_1_, ...), custom_call_target="tpu_custom_call" | custom-call | flops 1358954496 | bytes 3538948 | tf_op jit(solution)/shard_map/weigh/pallas_call | solution.py:273
  51.5 0.1 constant_dynamic-update-slice_fusion.8
  51.6 0.1 constant_dynamic-update-slice_fusion.7
  51.6 0.0 collective-permute-done.9
  51.7 0.1 constant_dynamic-update-slice_fusion.6.refs_2_.refs_7_
  51.7 0.0 copy-done.8
  51.7 0.0 copy-start
  51.8 0.0 copy-start.1
  51.8 2.8 %tile.3 = (bf16[256,1152]{1,0:T(8,128)(2,1)S(1)}, bf16[256,1152]{1,0:T(8,128)(2,1)S(1)}, bf16[256,1152]{1,0:T(8,128)(2,1)S(1)}) custom-call(f32[1,2]{1,0:T(1,128)S(1)} %maximum_bitcast_fusion.refs_0_.scalars, bf16[256,1152]{1,0:T(8,128)(2,1)S(1)} %constant_dynamic-update-slice_fusion.refs_1_, ...), custom_call_target="tpu_custom_call" | custom-call | flops 2264924160 | bytes 5308420 | tf_op jit(solution)/shard_map/tile/pallas_call | solution.py:273
  54.5 2.3 %collective-permute-start.10 = (bf16[256,1152]{1,0:T(8,128)(2,1)S(1)}, bf16[256,1152]{1,0:T(8,128)(2,1)S(1)}, u32[]{:S(2)}, u32[]{:S(2)}) collective-permute-start(bf16[256,1152]{1,0:T(8,128)(2,1)S(1)} %get-tuple-element.35), channel_id=1, source_target_pairs={{4,0},{68,64},{0,4},{64,68},{12,8},{76,72},{8,12},{72,76},{20,16},... | collective-permute-start | bytes 1769480 | tf_op jit(solution)/shard_map/ppermute | solution.py:54
  56.9 6.5 %collective-permute-start.11 = (bf16[256,1152]{1,0:T(8,128)(2,1)S(1)}, bf16[256,1152]{1,0:T(8,128)(2,1)S(1)}, u32[]{:S(2)}, u32[]{:S(2)}) collective-permute-start(bf16[256,1152]{1,0:T(8,128)(2,1)S(1)} %get-tuple-element.36), channel_id=1, source_target_pairs={{28,0},{92,64},{8,4},{72,68},{4,8},{68,72},{16,12},{80,76},{12,16}... | collective-permute-start | bytes 1769480 | tf_op jit(solution)/shard_map/ppermute | solution.py:54
  63.4 3.7 %collective-permute-start.12 = (bf16[192,1152]{1,0:T(8,128)(2,1)S(1)}, bf16[192,1152]{1,0:T(8,128)(2,1)S(1)}, u32[]{:S(2)}, u32[]{:S(2)}) collective-permute-start(bf16[192,1152]{1,0:T(8,128)(2,1)S(1)} %slice.6), channel_id=1, source_target_pairs={{64,0},{0,64},{68,4},{4,68},{72,8},{8,72},{76,12},{12,76},{80,16},... | collective-permute-start | bytes 1327112 | tf_op jit(solution)/shard_map/ppermute | solution.py:54
  67.2 0.0 copy-done
  67.2 0.0 copy-done.1
  67.2 0.1 units.1
  67.3 0.0 copy-start.2
  67.3 0.7 copy-done.2
  68.0 0.7 copy-done.4
  68.7 0.6 copy-done.6
  69.3 0.6 copy-done.9
  69.9 1.6 %tile.2.mine = f32[256,1152]{1,0:T(8,128)S(1)} custom-call(f32[1,2]{1,0:T(1,128)S(1)} %copy-done.9, bf16[256,1152]{1,0:T(8,128)(2,1)S(1)} %get-tuple-element.29.refs_1_, bf16[1024,1152]{1,0:T(8,128)(2,1)S(1)} %constant_dynamic-update-slice_fusion.6.refs_2_.refs_7_), custom_call_target="tpu_custom_call" | custom-call | flops 1207959552 | bytes 2949124 | tf_op jit(solution)/shard_map/tile/pallas_call | solution.py:273
  71.5 2.2 %collective-permute-done.12.tail = bf16[192,1152]{1,0:T(8,128)(2,1)S(1)} collective-permute-done((bf16[192,1152]{1,0:T(8,128)(2,1)S(1)}, bf16[192,1152]{1,0:T(8,128)(2,1)S(1)}, u32[]{:S(2)}, u32[]{:S(2)}) %collective-permute-start.12) | collective-permute-done | bytes 442400 | tf_op jit(solution)/shard_map/ppermute | solution.py:54
  73.7 0.0 collective-permute-done.10.first
  73.7 0.0 collective-permute-done.11.second
  73.7 1.0 %merge.1 = bf16[4,64,1152]{2,1,0:T(8,128)(2,1)} custom-call(f32[256,1152]{1,0:T(8,128)S(1)} %tile.2.mine, bf16[256,1152]{1,0:T(8,128)(2,1)S(1)} %collective-permute-done.10.first, bf16[256,1152]{1,0:T(8,128)(2,1)S(1)} %collective-permute-done.11.second, bf16[192,1152]{1,0:T(8,128)(2,1)S(1)} %collective-permute-done.12.tail), custom_call_target="tpu_custom_call" | custom-call | tf_op jit(solution)/shard_map/merge/pallas_call | solution.py:249
  74.7 3.7 %all-to-all-start.1 = ((bf16[4,64,1152]{2,1,0:T(8,128)(2,1)}), bf16[4,64,1152]{2,1,0:T(8,128)(2,1)S(1)}, u32[]{:S(2)}, u32[]{:S(2)}) async-start(bf16[4,64,1152]{2,1,0:T(8,128)(2,1)} %merge.1), calls=%async_computation.1 | async-start | bytes 1179648 | tf_op jit(solution)/shard_map/all_to_all | solution.py:58
  78.5 0.0 copy-start.3
  78.5 0.0 copy-start.5
  78.5 0.0 copy-start.7
  78.5 0.0 copy-start.10
  78.5 5.9 %collective-permute-start.13 = (bf16[64,1152]{1,0:T(8,128)(2,1)S(1)}, bf16[64,1152]{1,0:T(8,128)(2,1)S(1)}, u32[]{:S(2)}, u32[]{:S(2)}) collective-permute-start(bf16[64,1152]{1,0:T(8,128)(2,1)S(1)} %slice.7), channel_id=1, source_target_pairs={{64,0},{0,64},{68,4},{4,68},{72,8},{8,72},{76,12},{12,76},{80,16},... | collective-permute-start | bytes 442376 | tf_op jit(solution)/shard_map/ppermute | solution.py:54
  84.4 5.3 %collective-permute-done.13.head = bf16[64,1152]{1,0:T(8,128)(2,1)S(1)} collective-permute-done((bf16[64,1152]{1,0:T(8,128)(2,1)S(1)}, bf16[64,1152]{1,0:T(8,128)(2,1)S(1)}, u32[]{:S(2)}, u32[]{:S(2)}) %collective-permute-start.13) | collective-permute-done | bytes 147488 | tf_op jit(solution)/shard_map/ppermute | solution.py:54
  89.7 0.0 all-to-all-done.1.parts
  89.7 0.1 sum.1
  89.9 2.0 %all_gather.7.pair = f32[64,1152]{1,0:T(8,128)S(1)} all-gather(f32[32,1152]{1,0:T(8,128)S(1)} %get-tuple-element.39), channel_id=1, replica_groups=mesh['zl'=2,'xh'=2,'xl'=2,'c'=2,'y'=8,'zh'=4] {'c'}, dimensions={0}, use_global_device_ids=true | all-gather | bytes 442368 | tf_op jit(solution)/shard_map/all_gather | solution.py:66
  91.9 0.0 copy-done.3
  91.9 0.0 copy-done.10
  91.9 0.9 finish.1
  (15 shorter events, 0.3 us)
Async XLA Ops:
  11.0 20.2 %all-to-all-start = ((bf16[4,64,1152]{2,1,0:T(8,128)(2,1)}), bf16[4,64,1152]{2,1,0:T(8,128)(2,1)S(1)}, u32[]{:S(2)}, u32[]{:S(2)}) async-start(bf16[4,64,1152]{2,1,0:T(8,128)(2,1)} %get-tuple-element.23), calls=%async_computation | async-start | bytes 1179648 | tf_op jit(solution)/shard_map/all_to_all | solution.py:58
  17.8 16.8 %collective-permute-start.1 = (bf16[64,1152]{1,0:T(8,128)(2,1)S(1)}, bf16[64,1152]{1,0:T(8,128)(2,1)S(1)}, u32[]{:S(2)}, u32[]{:S(2)}) collective-permute-start(bf16[64,1152]{1,0:T(8,128)(2,1)S(1)} %get-tuple-element.30), channel_id=1, source_target_pairs={{4,0},{68,64},{0,4},{64,68},{12,8},{76,72},{8,12},{72,76},{20,16},... | collective-permute-start | bytes 442376 | tf_op jit(solution)/shard_map/ppermute | solution.py:54
  20.9 15.7 %collective-permute-start.4 = (bf16[64,1152]{1,0:T(8,128)(2,1)S(1)}, bf16[64,1152]{1,0:T(8,128)(2,1)S(1)}, u32[]{:S(2)}, u32[]{:S(2)}) collective-permute-start(bf16[64,1152]{1,0:T(8,128)(2,1)S(1)} %get-tuple-element.30), channel_id=1, source_target_pairs={{28,0},{92,64},{8,4},{72,68},{4,8},{68,72},{16,12},{80,76},{12,16}... | collective-permute-start | bytes 442376 | tf_op jit(solution)/shard_map/ppermute | solution.py:54
  25.5 21.4 %collective-permute-start.7 = (bf16[64,1152]{1,0:T(8,128)(2,1)S(1)}, bf16[64,1152]{1,0:T(8,128)(2,1)S(1)}, u32[]{:S(2)}, u32[]{:S(2)}) collective-permute-start(bf16[64,1152]{1,0:T(8,128)(2,1)S(1)} %get-tuple-element.30), channel_id=1, source_target_pairs={{64,0},{0,64},{68,4},{4,68},{72,8},{8,72},{76,12},{12,76},{80,16},... | collective-permute-start | bytes 442376 | tf_op jit(solution)/shard_map/ppermute | solution.py:54
  31.2 20.6 %copy-start.8 = (f32[1,2]{1,0:T(1,128)}, f32[1,2]{1,0:T(1,128)S(1)}, u32[]{:S(2)}) copy-start(f32[1,2]{1,0:T(1,128)S(1)} %maximum_bitcast_fusion.refs_0_.scalars) | copy-start | bytes 28
  31.3 10.4 %collective-permute-start.2 = (bf16[192,1152]{1,0:T(8,128)(2,1)S(1)}, bf16[192,1152]{1,0:T(8,128)(2,1)S(1)}, u32[]{:S(2)}, u32[]{:S(2)}) collective-permute-start(bf16[192,1152]{1,0:T(8,128)(2,1)S(1)} %get-tuple-element.31), channel_id=1, source_target_pairs={{4,0},{68,64},{0,4},{64,68},{12,8},{76,72},{8,12},{72,76},{20,16},... | collective-permute-start | bytes 1327112 | tf_op jit(solution)/shard_map/ppermute | solution.py:54
  34.7 10.3 %collective-permute-start.5 = (bf16[192,1152]{1,0:T(8,128)(2,1)S(1)}, bf16[192,1152]{1,0:T(8,128)(2,1)S(1)}, u32[]{:S(2)}, u32[]{:S(2)}) collective-permute-start(bf16[192,1152]{1,0:T(8,128)(2,1)S(1)} %get-tuple-element.31), channel_id=1, source_target_pairs={{28,0},{92,64},{8,4},{72,68},{4,8},{68,72},{16,12},{80,76},{12,16}... | collective-permute-start | bytes 1327112 | tf_op jit(solution)/shard_map/ppermute | solution.py:54
  36.6 10.3 %collective-permute-start.8 = (bf16[192,1152]{1,0:T(8,128)(2,1)S(1)}, bf16[192,1152]{1,0:T(8,128)(2,1)S(1)}, u32[]{:S(2)}, u32[]{:S(2)}) collective-permute-start(bf16[192,1152]{1,0:T(8,128)(2,1)S(1)} %get-tuple-element.31), channel_id=1, source_target_pairs={{64,0},{0,64},{68,4},{4,68},{72,8},{8,72},{76,12},{12,76},{80,16},... | collective-permute-start | bytes 1327112 | tf_op jit(solution)/shard_map/ppermute | solution.py:54
  39.7 9.7 %collective-permute-start = (bf16[256,1152]{1,0:T(8,128)(2,1)S(1)}, bf16[256,1152]{1,0:T(8,128)(2,1)S(1)}, u32[]{:S(2)}, u32[]{:S(2)}) collective-permute-start(bf16[256,1152]{1,0:T(8,128)(2,1)S(1)} %get-tuple-element.29.refs_1_), channel_id=1, source_target_pairs={{0,32},{32,0},{1,33},{33,1},{2,34},{34,2},{3,35},{35,3},{4,36},{36... | collective-permute-start | bytes 1769480 | tf_op jit(solution)/shard_map/ppermute | solution.py:62
  41.7 7.8 %collective-permute-start.3 = (bf16[256,1152]{1,0:T(8,128)(2,1)S(1)}, bf16[256,1152]{1,0:T(8,128)(2,1)S(1)}, u32[]{:S(2)}, u32[]{:S(2)}) collective-permute-start(bf16[256,1152]{1,0:T(8,128)(2,1)S(1)} %constant_dynamic-update-slice_fusion.refs_1_), channel_id=1, source_target_pairs={{0,32},{32,0},{1,33},{33,1},{2,34},{34,2},{3,35},{35,3},{4,36},{36... | collective-permute-start | bytes 1769480 | tf_op jit(solution)/shard_map/ppermute | solution.py:62
  45.0 4.5 %collective-permute-start.6 = (bf16[256,1152]{1,0:T(8,128)(2,1)S(1)}, bf16[256,1152]{1,0:T(8,128)(2,1)S(1)}, u32[]{:S(2)}, u32[]{:S(2)}) collective-permute-start(bf16[256,1152]{1,0:T(8,128)(2,1)S(1)} %constant_dynamic-update-slice_fusion.2.refs_2_), channel_id=1, source_target_pairs={{0,32},{32,0},{1,33},{33,1},{2,34},{34,2},{3,35},{35,3},{4,36},{36... | collective-permute-start | bytes 1769480 | tf_op jit(solution)/shard_map/ppermute | solution.py:62
  47.0 4.7 %collective-permute-start.9 = (bf16[256,1152]{1,0:T(8,128)(2,1)S(1)}, bf16[256,1152]{1,0:T(8,128)(2,1)S(1)}, u32[]{:S(2)}, u32[]{:S(2)}) collective-permute-start(bf16[256,1152]{1,0:T(8,128)(2,1)S(1)} %constant_dynamic-update-slice_fusion.4.refs_3_), channel_id=1, source_target_pairs={{0,32},{32,0},{1,33},{33,1},{2,34},{34,2},{3,35},{35,3},{4,36},{36... | collective-permute-start | bytes 1769480 | tf_op jit(solution)/shard_map/ppermute | solution.py:62
  51.7 15.5 %copy-start = (bf16[32,1152]{1,0:T(8,128)(2,1)S(1)}, bf16[32,1152]{1,0:T(8,128)(2,1)}, u32[]{:S(2)}) copy-start(bf16[32,1152]{1,0:T(8,128)(2,1)} %image.1) | copy-start | bytes 221188
  51.8 15.4 %copy-start.1 = (bf16[32,1152]{1,0:T(8,128)(2,1)S(1)}, bf16[32,1152]{1,0:T(8,128)(2,1)}, u32[]{:S(2)}) copy-start(bf16[32,1152]{1,0:T(8,128)(2,1)} %text.1) | copy-start | bytes 221188
  54.5 19.2 %collective-permute-start.10 = (bf16[256,1152]{1,0:T(8,128)(2,1)S(1)}, bf16[256,1152]{1,0:T(8,128)(2,1)S(1)}, u32[]{:S(2)}, u32[]{:S(2)}) collective-permute-start(bf16[256,1152]{1,0:T(8,128)(2,1)S(1)} %get-tuple-element.35), channel_id=1, source_target_pairs={{4,0},{68,64},{0,4},{64,68},{12,8},{76,72},{8,12},{72,76},{20,16},... | collective-permute-start | bytes 1769480 | tf_op jit(solution)/shard_map/ppermute | solution.py:54
  56.9 16.8 %collective-permute-start.11 = (bf16[256,1152]{1,0:T(8,128)(2,1)S(1)}, bf16[256,1152]{1,0:T(8,128)(2,1)S(1)}, u32[]{:S(2)}, u32[]{:S(2)}) collective-permute-start(bf16[256,1152]{1,0:T(8,128)(2,1)S(1)} %get-tuple-element.36), channel_id=1, source_target_pairs={{28,0},{92,64},{8,4},{72,68},{4,8},{68,72},{16,12},{80,76},{12,16}... | collective-permute-start | bytes 1769480 | tf_op jit(solution)/shard_map/ppermute | solution.py:54
  63.4 10.3 %collective-permute-start.12 = (bf16[192,1152]{1,0:T(8,128)(2,1)S(1)}, bf16[192,1152]{1,0:T(8,128)(2,1)S(1)}, u32[]{:S(2)}, u32[]{:S(2)}) collective-permute-start(bf16[192,1152]{1,0:T(8,128)(2,1)S(1)} %slice.6), channel_id=1, source_target_pairs={{64,0},{0,64},{68,4},{4,68},{72,8},{8,72},{76,12},{12,76},{80,16},... | collective-permute-start | bytes 1327112 | tf_op jit(solution)/shard_map/ppermute | solution.py:54
  67.3 0.7 copy-start.2
  68.0 0.7 copy-start.4
  68.7 0.6 copy-start.6
  69.3 0.6 copy-start.9
  74.7 15.0 %all-to-all-start.1 = ((bf16[4,64,1152]{2,1,0:T(8,128)(2,1)}), bf16[4,64,1152]{2,1,0:T(8,128)(2,1)S(1)}, u32[]{:S(2)}, u32[]{:S(2)}) async-start(bf16[4,64,1152]{2,1,0:T(8,128)(2,1)} %merge.1), calls=%async_computation.1 | async-start | bytes 1179648 | tf_op jit(solution)/shard_map/all_to_all | solution.py:58
  78.5 13.5 %copy-start.3 = (f32[32,1152]{1,0:T(8,128)S(1)}, f32[32,1152]{1,0:T(8,128)}, u32[]{:S(2)}) copy-start(f32[32,1152]{1,0:T(8,128)} %copy-done.2) | copy-start | bytes 442372
  78.5 13.5 %copy-start.5 = (f32[32,1152]{1,0:T(8,128)S(1)}, f32[32,1152]{1,0:T(8,128)}, u32[]{:S(2)}) copy-start(f32[32,1152]{1,0:T(8,128)} %copy-done.4) | copy-start | bytes 442372
  78.5 13.5 %copy-start.7 = (f32[32,1]{1,0:T(8,128)S(1)}, f32[32,1]{1,0:T(8,128)}, u32[]{:S(2)}) copy-start(f32[32,1]{1,0:T(8,128)} %copy-done.6) | copy-start | bytes 388
  78.5 13.5 %copy-start.10 = (f32[1,2]{1,0:T(1,128)S(1)}, f32[1,2]{1,0:T(1,128)}, u32[]{:S(2)}) copy-start(f32[1,2]{1,0:T(1,128)} %copy-done.8) | copy-start | bytes 28
  78.5 11.2 %collective-permute-start.13 = (bf16[64,1152]{1,0:T(8,128)(2,1)S(1)}, bf16[64,1152]{1,0:T(8,128)(2,1)S(1)}, u32[]{:S(2)}, u32[]{:S(2)}) collective-permute-start(bf16[64,1152]{1,0:T(8,128)(2,1)S(1)} %slice.7), channel_id=1, source_target_pairs={{64,0},{0,64},{68,4},{4,68},{72,8},{8,72},{76,12},{12,76},{80,16},... | collective-permute-start | bytes 442376 | tf_op jit(solution)/shard_map/ppermute | solution.py:54
